TPU v7x, 512 devices: a whole 4x4x16 slice. The times are simulated.
512 devices in a mesh: gx: 32 (over z, core), gy: 16 (over x, y).
Axes of the slice: x: 4, y: 4, z: 16, core: 2. Of those that a mesh axis runs over, the one named last changes fastest.
Arguments:
- offsets: float32 [6144, 3, 128], P(('gx', 'gy')), may hold values from 0 to 1
- widths: float32 [6144, 128], P(('gx', 'gy')), may hold values from 0.6 to 2.5
- solvation: float32 [6144, 128], P(('gx', 'gy')), may hold values from -6 to 6
- heading: int32 [6144, 1], P(('gx', 'gy')), may hold values from 0 to 8; in each aligned block of 12 rows (0 to 11, 12 to 23, ...) at most 3 rows name the same one
- old_map: float32 [256, 384, 1024], P('gx', 'gy'), may hold values from -6 to 6
Outputs:
- new_map: float32 [256, 384, 1024], P('gx', 'gy')
Inputs may be any that keep to these rules, and one draw needn't show every extreme that they name: `heading`: entry d moves a block d // 3 - 1 tiles along x and d % 3 - 1 tiles along y from the tile of the device that stores it; among the 12 blocks of one device at most 3 share an entry.
All inputs are finite; a program needn't handle non-finite values.
Results may differ from a plain program's by a relative error of at most 0.0003.
Values sent between devices are 32-bit elements; how exact they have to be, the bound alone decides.
No kernel may reach another device: no remote copies, remote signals or barrier semaphores. Data moves between devices by JAX's collectives and lax.ppermute only.
A program may use at most 64 MiB of HBM per device.

v0:
```python
import jax
import jax.numpy as jnp
from jax import lax
from jax.sharding import PartitionSpec as P

SLOTS = 3
W = 5


def passed_along(value, axis, steps):
    count = lax.axis_size(axis)
    first, last = (max(0, -steps), min(count, count - steps))
    return lax.ppermute(value, axis, [(source, source + steps) for source in range(first, last)])


def block_field(rel, width_row, weight_row, span_x, span_y, span_z):
    alpha = 0.5 / (width_row * width_row)
    delta_x = span_x[None, :] - rel[0][:, None]
    delta_y = span_y[None, :] - rel[1][:, None]
    delta_z = span_z[None, :] - rel[2][:, None]
    along_x = jnp.exp(-alpha[:, None] * delta_x * delta_x)
    along_y = jnp.exp(-alpha[:, None] * delta_y * delta_y)
    along_z = jnp.exp(-alpha[:, None] * delta_z * delta_z)
    plane = weight_row[:, None, None] * along_x[:, :, None] * along_y[:, None, :]
    plane = plane.reshape(plane.shape[0], -1)
    return lax.dot_general(
        plane, along_z, (((0,), (0,)), ((), ())), precision=lax.Precision.HIGHEST
    )


def fold_rows(partial_value):
    core = partial_value[W : partial_value.shape[0] - W]
    for stride in (1, -1):
        edge = partial_value[partial_value.shape[0] - W :] if stride == 1 else partial_value[:W]
        landed = passed_along(edge, "gx", stride)
        if stride == 1:
            core = core.at[:W].add(landed)
        else:
            core = core.at[core.shape[0] - W :].add(landed)
    return core


def fold_cols(partial_value):
    core = partial_value[:, W : partial_value.shape[1] - W]
    for stride in (1, -1):
        edge = (
            partial_value[:, partial_value.shape[1] - W :] if stride == 1 else partial_value[:, :W]
        )
        landed = passed_along(edge, "gy", stride)
        if stride == 1:
            core = core.at[:, :W].add(landed)
        else:
            core = core.at[:, core.shape[1] - W :].add(landed)
    return core


def body(offsets, widths, solvation, heading, old_map):
    tile_x, tile_y, depth = old_map.shape
    stored = offsets.shape[0]
    lanes = offsets.shape[2]
    target = heading[:, 0]
    numbers = jnp.arange(stored)
    shared = target[:, None] == target[None, :]
    before = numbers[:, None] > numbers[None, :]
    order_rank = jnp.sum((shared & before).astype(jnp.int32), axis=1)
    slot_index = target * SLOTS + order_rank
    placing = (slot_index[:, None] == jnp.arange(9 * SLOTS)[None, :]).astype(jnp.float32)
    features = jnp.concatenate([offsets, widths[:, None, :], solvation[:, None, :]], axis=1)
    packed = jnp.einsum("bs,bkw->skw", placing, features, precision=lax.Precision.HIGHEST)
    packed = packed.reshape(3, 3, SLOTS, 5, lanes)
    filled = jnp.sum(placing, axis=0).reshape(3, 3, SLOTS)
    row_feats = [packed[0], packed[1], packed[2]]
    row_live = [filled[0], filled[1], filled[2]]
    for stride in (1, -1):
        moved = passed_along((packed[stride + 1], filled[stride + 1]), "gx", stride)
        row_feats[stride + 1] = moved[0]
        row_live[stride + 1] = moved[1]
    row_feats = jnp.stack(row_feats, axis=0)
    row_live = jnp.stack(row_live, axis=0)
    col_feats = [row_feats[:, 0], row_feats[:, 1], row_feats[:, 2]]
    col_live = [row_live[:, 0], row_live[:, 1], row_live[:, 2]]
    for stride in (1, -1):
        moved = passed_along((row_feats[:, stride + 1], row_live[:, stride + 1]), "gy", stride)
        col_feats[stride + 1] = moved[0]
        col_live[stride + 1] = moved[1]
    blocks = jnp.stack(col_feats, axis=0).reshape(9 * SLOTS, 5, lanes)
    present = jnp.stack(col_live, axis=0).reshape(9 * SLOTS)
    ext_x = tile_x + 2 * W
    ext_y = tile_y + 2 * W
    span_x = jnp.arange(ext_x).astype(jnp.float32) - W
    span_y = jnp.arange(ext_y).astype(jnp.float32) - W
    span_z = jnp.arange(depth).astype(jnp.float32)

    def accumulate(number, total):
        block = blocks[number]
        flag = present[number]
        rel = (block[0] * tile_x, block[1] * tile_y, block[2] * depth)
        width_row = block[3] + (1.0 - flag)
        return total + block_field(rel, width_row, block[4], span_x, span_y, span_z)

    empty = jnp.zeros((ext_x * ext_y, depth), jnp.float32)
    keys = ((1.0 - present) * 64.0).astype(jnp.int32) + jnp.arange(9 * SLOTS)
    arrange = jnp.argsort(keys, stable=True)
    blocks = blocks[arrange]
    present = present[arrange]
    count = jnp.sum(present).astype(jnp.int32)
    partial_value = lax.fori_loop(0, count, accumulate, empty)
    partial_value = partial_value.reshape(ext_x, ext_y, depth)
    core = fold_rows(fold_cols(partial_value))
    return old_map + core


def solution(mesh):
    placed = (
        P(("gx", "gy"), None, None),
        P(("gx", "gy"), None),
        P(("gx", "gy"), None),
        P(("gx", "gy"), None),
        P("gx", "gy", None),
    )
    return jax.shard_map(
        body, mesh=mesh, in_specs=placed, out_specs=P("gx", "gy", None), check_vma=False
    )
```

profile of v0, /device:TPU:251, one launch (start us, length us, event | category | flops | bytes accessed | tf_op | source)
XLA Modules:
  0.0 136.3 jit_solution(17494970713766242491)
XLA Ops:
  1.8 5.3 %collective-permute-start.1 = (f32[3,3]{1,0:T(4,128)S(1)}, f32[3,3]{1,0:T(4,128)S(1)}, u32[]{:S(2)}, u32[]{:S(2)}) collective-permute-start(f32[3,3]{1,0:T(4,128)S(1)} %squeeze.33), channel_id=1, source_target_pairs={{0,16},{16,32},{32,48},{48,64},{64,80},{80,96},{96,112},{112,128},... | collective-permute-start | bytes 116 | tf_op jit(solution)/shard_map/ppermute | solution.py:13
  7.2 1.9 %collective-permute-start = (f32[3,3]{1,0:T(4,128)S(1)}, f32[3,3]{1,0:T(4,128)S(1)}, u32[]{:S(2)}, u32[]{:S(2)}) collective-permute-start(f32[3,3]{1,0:T(4,128)S(1)} %squeeze.32), channel_id=1, source_target_pairs={{16,0},{32,16},{48,32},{64,48},{80,64},{96,80},{112,96},{128,112},... | collective-permute-start | bytes 116 | tf_op jit(solution)/shard_map/ppermute | solution.py:13
  10.9 4.9 %collective-permute-start.5 = (f32[3,3,5,128]{3,2,1,0:T(8,128)S(1)}, f32[3,3,5,128]{3,2,1,0:T(8,128)S(1)}, u32[]{:S(2)}, u32[]{:S(2)}) collective-permute-start(f32[3,3,5,128]{3,2,1,0:T(8,128)S(1)} %bitcast.68), channel_id=1, source_target_pairs={{0,16},{16,32},{32,48},{48,64},{64,80},{80,96},{96,112},{112,128},... | collective-permute-start | bytes 69128 | tf_op jit(solution)/shard_map/ppermute | solution.py:13
  15.8 1.9 %collective-permute-start.4 = (f32[3,3,5,128]{3,2,1,0:T(8,128)S(1)}, f32[3,3,5,128]{3,2,1,0:T(8,128)S(1)}, u32[]{:S(2)}, u32[]{:S(2)}) collective-permute-start(f32[3,3,5,128]{3,2,1,0:T(8,128)S(1)} %bitcast.69), channel_id=1, source_target_pairs={{16,0},{32,16},{48,32},{64,48},{80,64},{96,80},{112,96},{128,112},... | collective-permute-start | bytes 69128 | tf_op jit(solution)/shard_map/ppermute | solution.py:13
  17.9 2.8 %collective-permute-start.3 = (f32[3,3]{1,0:T(4,128)S(1)}, f32[3,3]{1,0:T(4,128)S(1)}, u32[]{:S(2)}, u32[]{:S(2)}) collective-permute-start(f32[3,3]{1,0:T(4,128)S(1)} %bitcast.73), channel_id=1, source_target_pairs={{0,1},{1,2},{2,3},{3,4},{4,5},{5,6},{6,7},{7,8},{8,9},{9,10},{10,1... | collective-permute-start | bytes 116 | tf_op jit(solution)/shard_map/ppermute | solution.py:13
  20.7 2.5 %collective-permute-start.2 = (f32[3,3]{1,0:T(4,128)S(1)}, f32[3,3]{1,0:T(4,128)S(1)}, u32[]{:S(2)}, u32[]{:S(2)}) collective-permute-start(f32[3,3]{1,0:T(4,128)S(1)} %bitcast.72), channel_id=1, source_target_pairs={{1,0},{2,1},{3,2},{4,3},{5,4},{6,5},{7,6},{8,7},{9,8},{10,9},{11,1... | collective-permute-start | bytes 116 | tf_op jit(solution)/shard_map/ppermute | solution.py:13
  23.2 3.9 %collective-permute-done.2 = f32[3,3]{1,0:T(4,128)S(1)} collective-permute-done((f32[3,3]{1,0:T(4,128)S(1)}, f32[3,3]{1,0:T(4,128)S(1)}, u32[]{:S(2)}, u32[]{:S(2)}) %collective-permute-start.2) | collective-permute-done | bytes 68 | tf_op jit(solution)/shard_map/ppermute | solution.py:13
  28.9 1.9 %collective-permute-start.6 = (f32[3,3,5,128]{3,2,1,0:T(8,128)S(1)}, f32[3,3,5,128]{3,2,1,0:T(8,128)S(1)}, u32[]{:S(2)}, u32[]{:S(2)}) collective-permute-start(f32[3,3,5,128]{3,2,1,0:T(8,128)S(1)} %get-tuple-element.138), channel_id=1, source_target_pairs={{1,0},{2,1},{3,2},{4,3},{5,4},{6,5},{7,6},{8,7},{9,8},{10,9},{11,1... | collective-permute-start | bytes 69128 | tf_op jit(solution)/shard_map/ppermute | solution.py:13
  30.8 5.5 %collective-permute-start.7 = (f32[3,3,5,128]{3,2,1,0:T(8,128)S(1)}, f32[3,3,5,128]{3,2,1,0:T(8,128)S(1)}, u32[]{:S(2)}, u32[]{:S(2)}) collective-permute-start(f32[3,3,5,128]{3,2,1,0:T(8,128)S(1)} %get-tuple-element.139), channel_id=1, source_target_pairs={{0,1},{1,2},{2,3},{3,4},{4,5},{5,6},{6,7},{7,8},{8,9},{9,10},{10,1... | collective-permute-start | bytes 69128 | tf_op jit(solution)/shard_map/ppermute | solution.py:13
  39.4 53.2 %while.15 = (s32[]{:T(128)}, f32[612,1024]{1,0:T(8,128)S(1)}, s32[]{:T(128)}, f32[27,5,128]{2,1,0:T(8,128)S(1)}, f32[27]{0:T(128)S(1)}, /*index=5*/s32[]{:T(128)}, s32[]{:T(128)}, s32[]{:T(128)}, f32[1]{0:T(128)}) while((s32[]{:T(128)}, f32[612,1024]{1,0:T(8,128)S(1)}, s32[]{:T(128)}, f32[27,5,128]{2,1,0:T(8,128)S(1)}, ...), condition=%wide.region_5.6_spmd.clone, body=%wide.region_4.5_spmd.clone.sunk | while | flops 963715328 | bytes 6342727 | solution.py:107
  41.1 2.7 %convolution_add_fusion.2 = f32[612,1024]{1,0:T(8,128)S(1)} fusion(f32[612,1024]{1,0:T(8,128)S(1)} %get-tuple-element.202, f32[128,612]{0,1:T(8,128)S(1)} %mul.223, f32[128]{0:T(128)S(1)} %get-tuple-element.191, f32[1024]{0:T(1024)S(1)} %iota_convert_fusion.2, f32[128]{0:T(128)S(1)} %get-tuple-element.188), kind=kOutput, calls=%fused_computation.5.clone.1 | convolution fusion | flops 963612672 | bytes 5331968 | tf_op jit(solution)/shard_map/while/body/dot_general | solution.py:26
  45.5 2.7 %convolution_add_fusion.2 = f32[612,1024]{1,0:T(8,128)S(1)} fusion(f32[612,1024]{1,0:T(8,128)S(1)} %get-tuple-element.202, f32[128,612]{0,1:T(8,128)S(1)} %mul.223, f32[128]{0:T(128)S(1)} %get-tuple-element.191, f32[1024]{0:T(1024)S(1)} %iota_convert_fusion.2, f32[128]{0:T(128)S(1)} %get-tuple-element.188), kind=kOutput, calls=%fused_computation.5.clone.1 | convolution fusion | flops 963612672 | bytes 5331968 | tf_op jit(solution)/shard_map/while/body/dot_general | solution.py:26
  49.9 2.7 %convolution_add_fusion.2 = f32[612,1024]{1,0:T(8,128)S(1)} fusion(f32[612,1024]{1,0:T(8,128)S(1)} %get-tuple-element.202, f32[128,612]{0,1:T(8,128)S(1)} %mul.223, f32[128]{0:T(128)S(1)} %get-tuple-element.191, f32[1024]{0:T(1024)S(1)} %iota_convert_fusion.2, f32[128]{0:T(128)S(1)} %get-tuple-element.188), kind=kOutput, calls=%fused_computation.5.clone.1 | convolution fusion | flops 963612672 | bytes 5331968 | tf_op jit(solution)/shard_map/while/body/dot_general | solution.py:26
  54.4 2.7 %convolution_add_fusion.2 = f32[612,1024]{1,0:T(8,128)S(1)} fusion(f32[612,1024]{1,0:T(8,128)S(1)} %get-tuple-element.202, f32[128,612]{0,1:T(8,128)S(1)} %mul.223, f32[128]{0:T(128)S(1)} %get-tuple-element.191, f32[1024]{0:T(1024)S(1)} %iota_convert_fusion.2, f32[128]{0:T(128)S(1)} %get-tuple-element.188), kind=kOutput, calls=%fused_computation.5.clone.1 | convolution fusion | flops 963612672 | bytes 5331968 | tf_op jit(solution)/shard_map/while/body/dot_general | solution.py:26
  58.8 2.7 %convolution_add_fusion.2 = f32[612,1024]{1,0:T(8,128)S(1)} fusion(f32[612,1024]{1,0:T(8,128)S(1)} %get-tuple-element.202, f32[128,612]{0,1:T(8,128)S(1)} %mul.223, f32[128]{0:T(128)S(1)} %get-tuple-element.191, f32[1024]{0:T(1024)S(1)} %iota_convert_fusion.2, f32[128]{0:T(128)S(1)} %get-tuple-element.188), kind=kOutput, calls=%fused_computation.5.clone.1 | convolution fusion | flops 963612672 | bytes 5331968 | tf_op jit(solution)/shard_map/while/body/dot_general | solution.py:26
  63.2 2.7 %convolution_add_fusion.2 = f32[612,1024]{1,0:T(8,128)S(1)} fusion(f32[612,1024]{1,0:T(8,128)S(1)} %get-tuple-element.202, f32[128,612]{0,1:T(8,128)S(1)} %mul.223, f32[128]{0:T(128)S(1)} %get-tuple-element.191, f32[1024]{0:T(1024)S(1)} %iota_convert_fusion.2, f32[128]{0:T(128)S(1)} %get-tuple-element.188), kind=kOutput, calls=%fused_computation.5.clone.1 | convolution fusion | flops 963612672 | bytes 5331968 | tf_op jit(solution)/shard_map/while/body/dot_general | solution.py:26
  67.6 2.7 %convolution_add_fusion.2 = f32[612,1024]{1,0:T(8,128)S(1)} fusion(f32[612,1024]{1,0:T(8,128)S(1)} %get-tuple-element.202, f32[128,612]{0,1:T(8,128)S(1)} %mul.223, f32[128]{0:T(128)S(1)} %get-tuple-element.191, f32[1024]{0:T(1024)S(1)} %iota_convert_fusion.2, f32[128]{0:T(128)S(1)} %get-tuple-element.188), kind=kOutput, calls=%fused_computation.5.clone.1 | convolution fusion | flops 963612672 | bytes 5331968 | tf_op jit(solution)/shard_map/while/body/dot_general | solution.py:26
  72.1 2.7 %convolution_add_fusion.2 = f32[612,1024]{1,0:T(8,128)S(1)} fusion(f32[612,1024]{1,0:T(8,128)S(1)} %get-tuple-element.202, f32[128,612]{0,1:T(8,128)S(1)} %mul.223, f32[128]{0:T(128)S(1)} %get-tuple-element.191, f32[1024]{0:T(1024)S(1)} %iota_convert_fusion.2, f32[128]{0:T(128)S(1)} %get-tuple-element.188), kind=kOutput, calls=%fused_computation.5.clone.1 | convolution fusion | flops 963612672 | bytes 5331968 | tf_op jit(solution)/shard_map/while/body/dot_general | solution.py:26
  76.5 2.7 %convolution_add_fusion.2 = f32[612,1024]{1,0:T(8,128)S(1)} fusion(f32[612,1024]{1,0:T(8,128)S(1)} %get-tuple-element.202, f32[128,612]{0,1:T(8,128)S(1)} %mul.223, f32[128]{0:T(128)S(1)} %get-tuple-element.191, f32[1024]{0:T(1024)S(1)} %iota_convert_fusion.2, f32[128]{0:T(128)S(1)} %get-tuple-element.188), kind=kOutput, calls=%fused_computation.5.clone.1 | convolution fusion | flops 963612672 | bytes 5331968 | tf_op jit(solution)/shard_map/while/body/dot_general | solution.py:26
  80.9 2.7 %convolution_add_fusion.2 = f32[612,1024]{1,0:T(8,128)S(1)} fusion(f32[612,1024]{1,0:T(8,128)S(1)} %get-tuple-element.202, f32[128,612]{0,1:T(8,128)S(1)} %mul.223, f32[128]{0:T(128)S(1)} %get-tuple-element.191, f32[1024]{0:T(1024)S(1)} %iota_convert_fusion.2, f32[128]{0:T(128)S(1)} %get-tuple-element.188), kind=kOutput, calls=%fused_computation.5.clone.1 | convolution fusion | flops 963612672 | bytes 5331968 | tf_op jit(solution)/shard_map/while/body/dot_general | solution.py:26
  85.4 2.7 %convolution_add_fusion.2 = f32[612,1024]{1,0:T(8,128)S(1)} fusion(f32[612,1024]{1,0:T(8,128)S(1)} %get-tuple-element.202, f32[128,612]{0,1:T(8,128)S(1)} %mul.223, f32[128]{0:T(128)S(1)} %get-tuple-element.191, f32[1024]{0:T(1024)S(1)} %iota_convert_fusion.2, f32[128]{0:T(128)S(1)} %get-tuple-element.188), kind=kOutput, calls=%fused_computation.5.clone.1 | convolution fusion | flops 963612672 | bytes 5331968 | tf_op jit(solution)/shard_map/while/body/dot_general | solution.py:26
  89.8 2.7 %convolution_add_fusion.2 = f32[612,1024]{1,0:T(8,128)S(1)} fusion(f32[612,1024]{1,0:T(8,128)S(1)} %get-tuple-element.202, f32[128,612]{0,1:T(8,128)S(1)} %mul.223, f32[128]{0:T(128)S(1)} %get-tuple-element.191, f32[1024]{0:T(1024)S(1)} %iota_convert_fusion.2, f32[128]{0:T(128)S(1)} %get-tuple-element.188), kind=kOutput, calls=%fused_computation.5.clone.1 | convolution fusion | flops 963612672 | bytes 5331968 | tf_op jit(solution)/shard_map/while/body/dot_general | solution.py:26
  92.6 1.9 %reshape.321 = f32[18,34,1024]{2,1,0:T(8,128)} reshape(f32[612,1024]{1,0:T(8,128)S(1)} %get-tuple-element.98) | data formatting | bytes 5013504 | tf_op jit(solution)/shard_map/reshape | solution.py:108
  94.5 1.7 %fusion.29 = (f32[18,5,1024]{2,1,0:T(8,128)S(1)}, f32[18,5,1024]{2,1,0:T(8,128)S(1)}) fusion(f32[18,34,1024]{2,1,0:T(8,128)} %reshape.321), kind=kLoop, calls=%fused_computation.64 | loop fusion | bytes 1474560 | tf_op jit(solution)/shard_map/slice | solution.py:47
  96.4 5.3 %collective-permute-start.8 = (f32[18,5,1024]{2,0,1:T(8,128)S(1)}, f32[18,5,1024]{2,0,1:T(8,128)S(1)}, u32[]{:S(2)}, u32[]{:S(2)}) collective-permute-start(f32[18,5,1024]{2,0,1:T(8,128)S(1)} %copy.61), channel_id=1, source_target_pairs={{0,1},{1,2},{2,3},{3,4},{4,5},{5,6},{6,7},{7,8},{8,9},{9,10},{10,1... | collective-permute-start | bytes 1105928 | tf_op jit(solution)/shard_map/ppermute | solution.py:13
  101.9 1.9 %collective-permute-start.9 = (f32[18,5,1024]{2,0,1:T(8,128)S(1)}, f32[18,5,1024]{2,0,1:T(8,128)S(1)}, u32[]{:S(2)}, u32[]{:S(2)}) collective-permute-start(f32[18,5,1024]{2,0,1:T(8,128)S(1)} %copy.63), channel_id=1, source_target_pairs={{1,0},{2,1},{3,2},{4,3},{5,4},{6,5},{7,6},{8,7},{9,8},{10,9},{11,1... | collective-permute-start | bytes 1105928 | tf_op jit(solution)/shard_map/ppermute | solution.py:13
  104.2 7.7 %collective-permute-done.8 = f32[18,5,1024]{2,0,1:T(8,128)S(1)} collective-permute-done((f32[18,5,1024]{2,0,1:T(8,128)S(1)}, f32[18,5,1024]{2,0,1:T(8,128)S(1)}, u32[]{:S(2)}, u32[]{:S(2)}) %collective-permute-start.8) | collective-permute-done | bytes 368672 | tf_op jit(solution)/shard_map/ppermute | solution.py:13
  113.5 4.6 %collective-permute-done.9 = f32[18,5,1024]{2,0,1:T(8,128)S(1)} collective-permute-done((f32[18,5,1024]{2,0,1:T(8,128)S(1)}, f32[18,5,1024]{2,0,1:T(8,128)S(1)}, u32[]{:S(2)}, u32[]{:S(2)}) %collective-permute-start.9) | collective-permute-done | bytes 368672 | tf_op jit(solution)/shard_map/ppermute | solution.py:13
  119.5 4.3 %collective-permute-start.10 = (f32[5,24,1024]{2,1,0:T(8,128)S(1)}, f32[5,24,1024]{2,1,0:T(8,128)S(1)}, u32[]{:S(2)}, u32[]{:S(2)}) collective-permute-start(f32[5,24,1024]{2,1,0:T(8,128)S(1)} %get-tuple-element.137), channel_id=1, source_target_pairs={{0,16},{16,32},{32,48},{48,64},{64,80},{80,96},{96,112},{112,128},... | collective-permute-start | bytes 1474568 | tf_op jit(solution)/shard_map/ppermute | solution.py:13
  123.8 1.9 %collective-permute-start.11 = (f32[5,24,1024]{2,1,0:T(8,128)S(1)}, f32[5,24,1024]{2,1,0:T(8,128)S(1)}, u32[]{:S(2)}, u32[]{:S(2)}) collective-permute-start(f32[5,24,1024]{2,1,0:T(8,128)S(1)} %get-tuple-element.136), channel_id=1, source_target_pairs={{16,0},{32,16},{48,32},{64,48},{80,64},{96,80},{112,96},{128,112},... | collective-permute-start | bytes 1474568 | tf_op jit(solution)/shard_map/ppermute | solution.py:13
  125.8 3.8 %collective-permute-done.10 = f32[5,24,1024]{2,1,0:T(8,128)S(1)} collective-permute-done((f32[5,24,1024]{2,1,0:T(8,128)S(1)}, f32[5,24,1024]{2,1,0:T(8,128)S(1)}, u32[]{:S(2)}, u32[]{:S(2)}) %collective-permute-start.10) | collective-permute-done | bytes 491552 | tf_op jit(solution)/shard_map/ppermute | solution.py:13
  129.6 5.5 %collective-permute-done.11 = f32[5,24,1024]{2,1,0:T(8,128)S(1)} collective-permute-done((f32[5,24,1024]{2,1,0:T(8,128)S(1)}, f32[5,24,1024]{2,1,0:T(8,128)S(1)}, u32[]{:S(2)}, u32[]{:S(2)}) %collective-permute-start.11) | collective-permute-done | bytes 491552 | tf_op jit(solution)/shard_map/ppermute | solution.py:13
  (174 shorter events, 23.9 us)
Async XLA Ops:
  1.8 16.0 %collective-permute-start.1 = (f32[3,3]{1,0:T(4,128)S(1)}, f32[3,3]{1,0:T(4,128)S(1)}, u32[]{:S(2)}, u32[]{:S(2)}) collective-permute-start(f32[3,3]{1,0:T(4,128)S(1)} %squeeze.33), channel_id=1, source_target_pairs={{0,16},{16,32},{32,48},{48,64},{64,80},{80,96},{96,112},{112,128},... | collective-permute-start | bytes 116 | tf_op jit(solution)/shard_map/ppermute | solution.py:13
  7.2 10.6 %collective-permute-start = (f32[3,3]{1,0:T(4,128)S(1)}, f32[3,3]{1,0:T(4,128)S(1)}, u32[]{:S(2)}, u32[]{:S(2)}) collective-permute-start(f32[3,3]{1,0:T(4,128)S(1)} %squeeze.32), channel_id=1, source_target_pairs={{16,0},{32,16},{48,32},{64,48},{80,64},{96,80},{112,96},{128,112},... | collective-permute-start | bytes 116 | tf_op jit(solution)/shard_map/ppermute | solution.py:13
  10.9 17.9 %collective-permute-start.5 = (f32[3,3,5,128]{3,2,1,0:T(8,128)S(1)}, f32[3,3,5,128]{3,2,1,0:T(8,128)S(1)}, u32[]{:S(2)}, u32[]{:S(2)}) collective-permute-start(f32[3,3,5,128]{3,2,1,0:T(8,128)S(1)} %bitcast.68), channel_id=1, source_target_pairs={{0,16},{16,32},{32,48},{48,64},{64,80},{80,96},{96,112},{112,128},... | collective-permute-start | bytes 69128 | tf_op jit(solution)/shard_map/ppermute | solution.py:13
  15.8 13.1 %collective-permute-start.4 = (f32[3,3,5,128]{3,2,1,0:T(8,128)S(1)}, f32[3,3,5,128]{3,2,1,0:T(8,128)S(1)}, u32[]{:S(2)}, u32[]{:S(2)}) collective-permute-start(f32[3,3,5,128]{3,2,1,0:T(8,128)S(1)} %bitcast.69), channel_id=1, source_target_pairs={{16,0},{32,16},{48,32},{64,48},{80,64},{96,80},{112,96},{128,112},... | collective-permute-start | bytes 69128 | tf_op jit(solution)/shard_map/ppermute | solution.py:13
  17.9 5.3 %collective-permute-start.3 = (f32[3,3]{1,0:T(4,128)S(1)}, f32[3,3]{1,0:T(4,128)S(1)}, u32[]{:S(2)}, u32[]{:S(2)}) collective-permute-start(f32[3,3]{1,0:T(4,128)S(1)} %bitcast.73), channel_id=1, source_target_pairs={{0,1},{1,2},{2,3},{3,4},{4,5},{5,6},{6,7},{7,8},{8,9},{9,10},{10,1... | collective-permute-start | bytes 116 | tf_op jit(solution)/shard_map/ppermute | solution.py:13
  20.7 6.4 %collective-permute-start.2 = (f32[3,3]{1,0:T(4,128)S(1)}, f32[3,3]{1,0:T(4,128)S(1)}, u32[]{:S(2)}, u32[]{:S(2)}) collective-permute-start(f32[3,3]{1,0:T(4,128)S(1)} %bitcast.72), channel_id=1, source_target_pairs={{1,0},{2,1},{3,2},{4,3},{5,4},{6,5},{7,6},{8,7},{9,8},{10,9},{11,1... | collective-permute-start | bytes 116 | tf_op jit(solution)/shard_map/ppermute | solution.py:13
  28.9 9.5 %collective-permute-start.6 = (f32[3,3,5,128]{3,2,1,0:T(8,128)S(1)}, f32[3,3,5,128]{3,2,1,0:T(8,128)S(1)}, u32[]{:S(2)}, u32[]{:S(2)}) collective-permute-start(f32[3,3,5,128]{3,2,1,0:T(8,128)S(1)} %get-tuple-element.138), channel_id=1, source_target_pairs={{1,0},{2,1},{3,2},{4,3},{5,4},{6,5},{7,6},{8,7},{9,8},{10,9},{11,1... | collective-permute-start | bytes 69128 | tf_op jit(solution)/shard_map/ppermute | solution.py:13
  30.8 7.6 %collective-permute-start.7 = (f32[3,3,5,128]{3,2,1,0:T(8,128)S(1)}, f32[3,3,5,128]{3,2,1,0:T(8,128)S(1)}, u32[]{:S(2)}, u32[]{:S(2)}) collective-permute-start(f32[3,3,5,128]{3,2,1,0:T(8,128)S(1)} %get-tuple-element.139), channel_id=1, source_target_pairs={{0,1},{1,2},{2,3},{3,4},{4,5},{5,6},{6,7},{7,8},{8,9},{9,10},{10,1... | collective-permute-start | bytes 69128 | tf_op jit(solution)/shard_map/ppermute | solution.py:13
  94.5 9.4 %copy-start = (f32[18,34,1024]{2,1,0:T(8,128)S(1)}, f32[18,34,1024]{2,1,0:T(8,128)}, u32[]{:S(2)}) copy-start(f32[18,34,1024]{2,1,0:T(8,128)} %reshape.321) | copy-start | bytes 7520260
  96.4 15.5 %collective-permute-start.8 = (f32[18,5,1024]{2,0,1:T(8,128)S(1)}, f32[18,5,1024]{2,0,1:T(8,128)S(1)}, u32[]{:S(2)}, u32[]{:S(2)}) collective-permute-start(f32[18,5,1024]{2,0,1:T(8,128)S(1)} %copy.61), channel_id=1, source_target_pairs={{0,1},{1,2},{2,3},{3,4},{4,5},{5,6},{6,7},{7,8},{8,9},{9,10},{10,1... | collective-permute-start | bytes 1105928 | tf_op jit(solution)/shard_map/ppermute | solution.py:13
  101.9 16.1 %collective-permute-start.9 = (f32[18,5,1024]{2,0,1:T(8,128)S(1)}, f32[18,5,1024]{2,0,1:T(8,128)S(1)}, u32[]{:S(2)}, u32[]{:S(2)}) collective-permute-start(f32[18,5,1024]{2,0,1:T(8,128)S(1)} %copy.63), channel_id=1, source_target_pairs={{1,0},{2,1},{3,2},{4,3},{5,4},{6,5},{7,6},{8,7},{9,8},{10,9},{11,1... | collective-permute-start | bytes 1105928 | tf_op jit(solution)/shard_map/ppermute | solution.py:13
  119.5 15.8 %copy-start.1 = (f32[8,24,1024]{2,1,0:T(8,128)S(1)}, f32[8,24,1024]{2,1,0:T(8,128)}, u32[]{:S(2)}) copy-start(f32[8,24,1024]{2,1,0:T(8,128)} %param.19) | copy-start | bytes 2359300
  119.5 10.0 %collective-permute-start.10 = (f32[5,24,1024]{2,1,0:T(8,128)S(1)}, f32[5,24,1024]{2,1,0:T(8,128)S(1)}, u32[]{:S(2)}, u32[]{:S(2)}) collective-permute-start(f32[5,24,1024]{2,1,0:T(8,128)S(1)} %get-tuple-element.137), channel_id=1, source_target_pairs={{0,16},{16,32},{32,48},{48,64},{64,80},{80,96},{96,112},{112,128},... | collective-permute-start | bytes 1474568 | tf_op jit(solution)/shard_map/ppermute | solution.py:13
  123.8 11.4 %collective-permute-start.11 = (f32[5,24,1024]{2,1,0:T(8,128)S(1)}, f32[5,24,1024]{2,1,0:T(8,128)S(1)}, u32[]{:S(2)}, u32[]{:S(2)}) collective-permute-start(f32[5,24,1024]{2,1,0:T(8,128)S(1)} %get-tuple-element.136), channel_id=1, source_target_pairs={{16,0},{32,16},{48,32},{64,48},{80,64},{96,80},{112,96},{128,112},... | collective-permute-start | bytes 1474568 | tf_op jit(solution)/shard_map/ppermute | solution.py:13
where the time goes:
time: 137 us; the launch traced here: 136 us
  starting transfers between devices  40 us (29%)
  matrix products  33.8 us (25%)
  waiting for transfers between devices  25.5 us (19%)
  local copies, waits for them, and re-layouts  18.1 us (13%)
  loops' own time  9.39 us (7%)
  other arithmetic  8.39 us (6%)
    ppermute x12, starting transfers between devices, passed_along(): lax.ppermute(value, axis, [(source, source + steps) for source in range(f...  40 us
    dot_general x12, matrix products, block_field(): lax.dot_general(plane, along_z, (((0,), (0,)), ((), ())), precision=lax.P...  32.8 us
    ppermute x12, waiting for transfers between devices, passed_along(): lax.ppermute(value, axis, [(source, source + steps) for source in range(f...  25.5 us
    another operation x1, loops' own time, body(): partial_value = lax.fori_loop(0, count, accumulate, empty)  9.39 us
    dynamic_slice x12, local copies, waits for them, and re-layouts, accumulate(): flag = present[number]  8 us
  transfers between devices with their start and end apart: 12, of which 5 were waited for; matrix products, arithmetic and copies ran while one was open for 5% of the time, Pallas kernels for 0%

commit v1 on v0

v1 whole, which is shorter than its diff:
```python
import functools
import jax
import jax.numpy as jnp
from jax import lax
from jax.experimental import pallas as pl
from jax.experimental.pallas import tpu as pltpu
from jax.sharding import PartitionSpec as P

LOG2E = 1.4426950408889634
NT = (((1,), (1,)), ((), ()))
FAR = 1.0e6
f32 = jnp.float32
ROWS = (192, 272, 192)
START = (0, 192, 464)

def quotient(n, d):
    shift = 16
    return lax.shift_right_logical(n * (((1 << shift) + d - 1) // d), shift)

def fill_tables(ti, tj):
    for g in range(3):
        n = ROWS[g]
        m = lax.broadcasted_iota(jnp.int32, (n, 128), 0)
        if g == 1:
            core, e = m < 192, m - 192
            right = e >= 40
            e = jnp.where(right, e - 40, e)
            ci = quotient(m, 24)
            dead = None
        else:
            core, e = m < 120, m - 120
            right = e >= 32
            e = jnp.where(right, e - 32, e)
            dead = e >= 32
            ci = quotient(m, 24)
            if g == 2:
                e = e + 8
        cj = m - ci * 24
        if g == 2:
            ci = ci + 3
        e = jnp.maximum(e, 0)
        ei = quotient(e, 5)
        ej = e - ei * 5 + jnp.where(right, 24, -5)
        i = jnp.where(core, ci, ei)
        j = jnp.where(core, cj, ej)
        i = (i + (8, 0, -8)[g]).astype(f32)
        if dead is not None:
            out = (ei >= 5) if g == 0 else (ei < 3)
            i = jnp.where((~core) & (out | dead), FAR, i)
        ti[START[g]:START[g] + n, :] = i
        tj[START[g]:START[g] + n, :] = j.astype(f32)

def split(v):
    h = v.astype(jnp.bfloat16)
    return h, (v - h.astype(f32)).astype(jnp.bfloat16)

def field_kernel(own_ref, p1_ref, p2_ref, m1_ref, m2_ref, old_ref, core_ref, left_ref, right_ref,
                 lists, acc, ti, tj):
    depth = old_ref.shape[2]
    fill_tables(ti, tj)
    acc[...] = jnp.zeros_like(acc)
    sources = (
        ((own_ref, 0), (p1_ref, 0), (p2_ref, 0)),
        ((own_ref, 1), (p1_ref, 1), (m1_ref, 0)),
        ((own_ref, 2), (m1_ref, 1), (m2_ref, 0)),
    )
    row = lax.broadcasted_iota(jnp.int32, (8, 128), 0)
    dead = jnp.where(row == 3, 1.0, 0.0).astype(f32)
    counts = []
    for g in range(3):
        cnt = jnp.int32(0)
        for ref, part in sources[g]:
            seg = ref[part]
            bits = jnp.zeros((1, 128), f32)
            for s in range(9):
                bits = bits + seg[s, 5:6, :] * float(1 << s)
            mask = jnp.max(bits).astype(jnp.int32)
            for s in range(9):
                lists[g, cnt] = seg[s]
                cnt = cnt + (lax.shift_right_logical(mask, s) & 1)
        lists[g, cnt] = dead
        counts.append(cnt)
    kio = lax.broadcasted_iota(jnp.int32, (256, 1), 0).astype(f32)

    def pair(g, p):
        n = ROWS[g]
        rec = jnp.concatenate([lists[g, 2 * p], lists[g, 2 * p + 1]], axis=1)
        x, y, z = rec[0:1] * 8.0, rec[1:2] * 24.0, rec[2:3] * 1024.0
        c = (-0.5 * LOG2E) / (rec[3:4] * rec[3:4])
        weight = rec[4:5]
        tic = ti[START[g]:START[g] + n, :]
        tjc = tj[START[g]:START[g] + n, :]
        dx = jnp.concatenate([tic, tic], axis=1) - x
        dy = jnp.concatenate([tjc, tjc], axis=1) - y
        ph, plo = split(jnp.exp2((dx * dx + dy * dy) * c) * weight)
        for b in range(depth // 256):
            ks = slice(b * 256, b * 256 + 256)
            d = kio + (b * 256.0 - z)
            zh, zl = split(jnp.exp2(d * (d * c)))
            dot = functools.partial(lax.dot_general, dimension_numbers=NT, preferred_element_type=f32)
            t = dot(jnp.concatenate([ph, plo], 0), zh)
            r = t[:n] + t[n:] + dot(ph, zl)
            if g == 1:
                acc[:, ks] += r
            elif g == 0:
                acc[0:120, ks] += r[0:120]
                acc[192:224, ks] += r[120:152]
                acc[232:264, ks] += r[152:184]
            else:
                acc[72:192, ks] += r[0:120]
                acc[200:232, ks] += r[120:152]
                acc[240:272, ks] += r[152:184]

    for g in range(3):
        def step(p, carry, g=g):
            pair(g, p)
            return carry
        lax.fori_loop(0, lax.shift_right_logical(counts[g] + 1, 1), step, 0)
    core_ref[...] = old_ref[...] + acc[0:192, :].reshape(core_ref.shape)
    left_ref[...] = acc[192:232, :]
    right_ref[...] = acc[232:272, :]


def pack_kernel(heading, offsets, widths, solvation, minus, same, plus, slots, taken):
    slots[...] = jnp.zeros_like(slots)
    for h in range(9):
        taken[h] = 0
    tile_row, tile_rows = lax.axis_index("gx"), lax.axis_size("gx")
    for b in range(offsets.shape[0]):
        h = heading[b, 0]
        n = taken[h]
        taken[h] = n + 1
        row, col = lax.div(h, 3), lax.rem(h, 3)
        place = col * 9 + row * 3 + n
        slots[place, 0:3, :] = offsets[b]
        slots[place, 3:4, :] = widths[b:b + 1, :]
        slots[place, 4:5, :] = solvation[b:b + 1, :]
        home = tile_row + row - 1
        inside = (home >= 0) & (home < tile_rows)
        slots[place, 5:6, :] = jnp.full((1, 128), jnp.where(inside, 1.0, 0.0), f32)
    for k, out in enumerate((minus, same, plus)):
        out[...] = slots[9 * k:9 * k + 9].reshape(out.shape)


def edge_kernel(core, from_left, from_right, out):
    side = pl.program_id(0)
    out[...] = core[...]

    @pl.when(side == 0)
    def _():
        for i in range(8):
            out[i, 0:5, :] += from_left[i * 5:i * 5 + 5, :]

    @pl.when(side == 1)
    def _():
        for i in range(8):
            out[i, 3:8, :] += from_right[i * 5:i * 5 + 5, :]


def passed_along(value, axis, steps):
    count = lax.axis_size(axis)
    first, last = (max(0, -steps), min(count, count - steps))
    return lax.ppermute(value, axis, [(source, source + steps) for source in range(first, last)])


def body(offsets, widths, solvation, heading, old_map):
    depth = old_map.shape[2]
    vm = pl.BlockSpec(memory_space=pltpu.VMEM)
    third = jax.ShapeDtypeStruct((3, 3, 8, 128), f32)
    minus, same, plus = pl.pallas_call(
        pack_kernel,
        out_shape=[third] * 3,
        in_specs=[pl.BlockSpec(memory_space=pltpu.SMEM), vm, vm, vm],
        out_specs=[vm] * 3,
        scratch_shapes=[pltpu.VMEM((27, 8, 128), f32), pltpu.SMEM((9,), jnp.int32)],
        name="pack",
    )(heading, offsets, widths, solvation)
    own = jnp.concatenate(
        [same, passed_along(plus, "gy", 1), passed_along(minus, "gy", -1)], axis=1
    )
    above1 = passed_along(own[1:3], "gx", 1)
    above2 = passed_along(own[2:3], "gx", 2)
    below1 = passed_along(own[0:2], "gx", -1)
    below2 = passed_along(own[0:1], "gx", -2)
    edge = jax.ShapeDtypeStruct((40, depth), f32)
    core, left, right = pl.pallas_call(
        field_kernel,
        out_shape=[jax.ShapeDtypeStruct(old_map.shape, f32), edge, edge],
        in_specs=[vm] * 6,
        out_specs=[vm] * 3,
        scratch_shapes=[
            pltpu.VMEM((3, 28, 8, 128), f32),
            pltpu.VMEM((272, depth), f32),
            pltpu.VMEM((656, 128), f32),
            pltpu.VMEM((656, 128), f32),
        ],
        compiler_params=pltpu.CompilerParams(vmem_limit_bytes=40 * 1024 * 1024),
        name="field",
    )(own, above1, above2, below1, below2, old_map)
    from_left = passed_along(right, "gy", 1)
    from_right = passed_along(left, "gy", -1)
    block = pl.BlockSpec((8, 8, depth), lambda s: (0, 2 * s, 0))
    whole = pl.BlockSpec((40, depth), lambda s: (0, 0))
    return pl.pallas_call(
        edge_kernel,
        grid=(2,),
        out_shape=jax.ShapeDtypeStruct(old_map.shape, f32),
        in_specs=[block, whole, whole],
        out_specs=block,
        input_output_aliases={0: 0},
        name="edges",
    )(core, from_left, from_right)


def solution(mesh):
    placed = (
        P(("gx", "gy"), None, None),
        P(("gx", "gy"), None),
        P(("gx", "gy"), None),
        P(("gx", "gy"), None),
        P("gx", "gy", None),
    )
    return jax.shard_map(
        body, mesh=mesh, in_specs=placed, out_specs=P("gx", "gy", None), check_vma=False
    )
```

time: 137 us -> 59.1 us (0.43)
  the two profiles are of different devices: /device:TPU:251 before, /device:TPU:410 now
where the time goes in v1:
time: 59.1 us; the launch traced here: 58.6 us
  starting transfers between devices  22 us (37%)
  Pallas kernels  16.8 us (28%)
  waiting for transfers between devices  15.7 us (27%)
  local copies, waits for them, and re-layouts  3.93 us (7%)
    ppermute x8, starting transfers between devices, passed_along(): lax.ppermute(value, axis, [(source, source + steps) for source in range(f...  22 us
    ppermute x8, waiting for transfers between devices, passed_along(): lax.ppermute(value, axis, [(source, source + steps) for source in range(f...  15.7 us
    pallas_call x1, Pallas kernels, body(): pl.pallas_call(field_kernel, out_shape=[jax.ShapeDtypeStruct(old_map.shap...  13.2 us
    unnamed x9, local copies, waits for them, and re-layouts  3.9 us
    pallas_call x1, Pallas kernels, body(): pl.pallas_call(edge_kernel, grid=(2,), out_shape=jax.ShapeDtypeStruct(old...  1.96 us
    pallas_call x1, Pallas kernels, body(): pl.pallas_call(pack_kernel, out_shape=[third] * 3, in_specs=[pl.BlockSpec...  1.67 us
  transfers between devices with their start and end apart: 8, of which 4 were waited for; matrix products, arithmetic and copies ran while one was open for 1% of the time, Pallas kernels for 0%

profile of v1, /device:TPU:410, one launch (start us, length us, event | category | flops | bytes accessed | tf_op | source)
XLA Modules:
  0.0 58.6 jit_solution(8131105965558550982)
XLA Ops:
  0.0 1.3 %copy.7.heading = s32[12,1]{1,0:T(8,128)} copy(s32[12,1]{0,1:T(1,128)} %param.8) | data formatting | bytes 96 | tf_op args[3]
  1.3 1.7 %pack.1 = (f32[3,3,8,128]{3,2,1,0:T(8,128)}, f32[3,3,8,128]{3,2,1,0:T(8,128)}, f32[3,3,8,128]{3,2,1,0:T(8,128)}) custom-call(s32[12,1]{1,0:T(8,128)} %copy.7.heading, f32[12,3,128]{2,1,0:T(4,128)} %offsets.1, f32[12,128]{1,0:T(8,128)} %widths.1, f32[12,128]{1,0:T(8,128)} %solvation.1), custom_call_target="tpu_custom_call" | custom-call | tf_op jit(solution)/shard_map/pack/pallas_call | solution.py:170
  3.0 3.0 %collective-permute-start = (f32[3,3,8,128]{3,2,1,0:T(8,128)}, f32[3,3,8,128]{3,2,1,0:T(8,128)S(1)}, u32[]{:S(2)}, u32[]{:S(2)}) collective-permute-start(f32[3,3,8,128]{3,2,1,0:T(8,128)} %get-tuple-element.12), channel_id=1, source_target_pairs={{0,1},{1,2},{2,3},{3,4},{4,5},{5,6},{6,7},{7,8},{8,9},{9,10},{10,1... | collective-permute-start | bytes 110600 | tf_op jit(solution)/shard_map/ppermute | solution.py:163
  6.1 2.8 %collective-permute-start.1 = (f32[3,3,8,128]{3,2,1,0:T(8,128)}, f32[3,3,8,128]{3,2,1,0:T(8,128)S(1)}, u32[]{:S(2)}, u32[]{:S(2)}) collective-permute-start(f32[3,3,8,128]{3,2,1,0:T(8,128)} %get-tuple-element.13), channel_id=1, source_target_pairs={{1,0},{2,1},{3,2},{4,3},{5,4},{6,5},{7,6},{8,7},{9,8},{10,9},{11,1... | collective-permute-start | bytes 110600 | tf_op jit(solution)/shard_map/ppermute | solution.py:163
  8.8 0.8 %constant_dynamic-update-slice_fusion.2 = f32[3,9,8,128]{3,2,1,0:T(8,128)S(1)} fusion(f32[3,3,8,128]{3,2,1,0:T(8,128)} %get-tuple-element.11), kind=kLoop, calls=%fused_computation.2 | loop fusion | bytes 73728
  9.6 0.0 collective-permute-done
  9.6 4.6 %collective-permute-done.1 = f32[3,3,8,128]{3,2,1,0:T(8,128)S(1)} collective-permute-done((f32[3,3,8,128]{3,2,1,0:T(8,128)}, f32[3,3,8,128]{3,2,1,0:T(8,128)S(1)}, u32[]{:S(2)}, u32[]{:S(2)}) %collective-permute-start.1) | collective-permute-done | bytes 36896 | tf_op jit(solution)/shard_map/ppermute | solution.py:163
  14.2 2.1 %collective-permute-start.4 = (f32[2,9,8,128]{3,2,1,0:T(8,128)S(1)}, f32[2,9,8,128]{3,2,1,0:T(8,128)S(1)}, u32[]{:S(2)}, u32[]{:S(2)}) collective-permute-start(f32[2,9,8,128]{3,2,1,0:T(8,128)S(1)} %get-tuple-element.19), channel_id=1, source_target_pairs={{16,0},{32,16},{48,32},{64,48},{80,64},{96,80},{112,96},{128,112},... | collective-permute-start | bytes 221192 | tf_op jit(solution)/shard_map/ppermute | solution.py:163
  16.4 2.2 %collective-permute-start.2 = (f32[2,9,8,128]{3,2,1,0:T(8,128)S(1)}, f32[2,9,8,128]{3,2,1,0:T(8,128)S(1)}, u32[]{:S(2)}, u32[]{:S(2)}) collective-permute-start(f32[2,9,8,128]{3,2,1,0:T(8,128)S(1)} %get-tuple-element.20), channel_id=1, source_target_pairs={{0,16},{16,32},{32,48},{48,64},{64,80},{80,96},{96,112},{112,128},... | collective-permute-start | bytes 221192 | tf_op jit(solution)/shard_map/ppermute | solution.py:163
  18.6 4.1 %collective-permute-start.5 = (f32[1,9,8,128]{3,2,1,0:T(8,128)S(1)}, f32[1,9,8,128]{3,2,1,0:T(8,128)S(1)}, u32[]{:S(2)}, u32[]{:S(2)}) collective-permute-start(f32[1,9,8,128]{3,2,1,0:T(8,128)S(1)} %get-tuple-element.17), channel_id=1, source_target_pairs={{32,0},{48,16},{64,32},{80,48},{96,64},{112,80},{128,96},{144,112}... | collective-permute-start | bytes 110600 | tf_op jit(solution)/shard_map/ppermute | solution.py:163
  22.7 1.9 %collective-permute-start.3 = (f32[1,9,8,128]{3,2,1,0:T(8,128)S(1)}, f32[1,9,8,128]{3,2,1,0:T(8,128)S(1)}, u32[]{:S(2)}, u32[]{:S(2)}) collective-permute-start(f32[1,9,8,128]{3,2,1,0:T(8,128)S(1)} %get-tuple-element.18), channel_id=1, source_target_pairs={{0,32},{16,48},{32,64},{48,80},{64,96},{80,112},{96,128},{112,144}... | collective-permute-start | bytes 110600 | tf_op jit(solution)/shard_map/ppermute | solution.py:163
  24.7 0.0 collective-permute-done.5.m2_ref
  24.7 5.1 %collective-permute-done.3.p2_ref = f32[1,9,8,128]{3,2,1,0:T(8,128)S(1)} collective-permute-done((f32[1,9,8,128]{3,2,1,0:T(8,128)S(1)}, f32[1,9,8,128]{3,2,1,0:T(8,128)S(1)}, u32[]{:S(2)}, u32[]{:S(2)}) %collective-permute-start.3) | collective-permute-done | bytes 36896 | tf_op jit(solution)/shard_map/ppermute | solution.py:163
  29.8 0.0 collective-permute-done.4.m1_ref
  29.8 0.0 collective-permute-done.2.p1_ref
  29.8 0.0 copy-start
  29.8 1.1 %copy-done = f32[8,24,1024]{2,1,0:T(8,128)S(1)} copy-done((f32[8,24,1024]{2,1,0:T(8,128)S(1)}, f32[8,24,1024]{2,1,0:T(8,128)}, u32[]{:S(2)}) %copy-start) | copy-done | bytes 786456
  30.9 13.2 %field.1 = (f32[8,24,1024]{2,1,0:T(8,128)}, f32[40,1024]{1,0:T(8,128)S(1)}, f32[40,1024]{1,0:T(8,128)S(1)}) custom-call(f32[3,9,8,128]{3,2,1,0:T(8,128)S(1)} %constant_dynamic-update-slice_fusion.own_ref, f32[2,9,8,128]{3,2,1,0:T(8,128)S(1)} %collective-permute-done.2.p1_ref, f32[1,9,8,128]{3,2,1,0:T(8,128)S(1)} %collective-permute-done.3.p2_ref, ...), custom_call_target="tpu_custom_call" | custom-call | tf_op jit(solution)/shard_map/field/pallas_call | solution.py:186
  44.1 2.0 %collective-permute-start.6 = (f32[40,1024]{1,0:T(8,128)S(1)}, f32[40,1024]{1,0:T(8,128)S(1)}, u32[]{:S(2)}, u32[]{:S(2)}) collective-permute-start(f32[40,1024]{1,0:T(8,128)S(1)} %get-tuple-element.15), channel_id=1, source_target_pairs={{0,1},{1,2},{2,3},{3,4},{4,5},{5,6},{6,7},{7,8},{8,9},{9,10},{10,1... | collective-permute-start | bytes 491528 | tf_op jit(solution)/shard_map/ppermute | solution.py:163
  46.1 3.8 %collective-permute-start.7 = (f32[40,1024]{1,0:T(8,128)S(1)}, f32[40,1024]{1,0:T(8,128)S(1)}, u32[]{:S(2)}, u32[]{:S(2)}) collective-permute-start(f32[40,1024]{1,0:T(8,128)S(1)} %get-tuple-element.16), channel_id=1, source_target_pairs={{1,0},{2,1},{3,2},{4,3},{5,4},{6,5},{7,6},{8,7},{9,8},{10,9},{11,1... | collective-permute-start | bytes 491528 | tf_op jit(solution)/shard_map/ppermute | solution.py:163
  50.0 1.6 %collective-permute-done.6.from_left = f32[40,1024]{1,0:T(8,128)S(1)} collective-permute-done((f32[40,1024]{1,0:T(8,128)S(1)}, f32[40,1024]{1,0:T(8,128)S(1)}, u32[]{:S(2)}, u32[]{:S(2)}) %collective-permute-start.6) | collective-permute-done | bytes 163872 | tf_op jit(solution)/shard_map/ppermute | solution.py:163
  51.6 0.0 copy-start.1
  51.6 4.4 %collective-permute-done.7.from_right = f32[40,1024]{1,0:T(8,128)S(1)} collective-permute-done((f32[40,1024]{1,0:T(8,128)S(1)}, f32[40,1024]{1,0:T(8,128)S(1)}, u32[]{:S(2)}, u32[]{:S(2)}) %collective-permute-start.7) | collective-permute-done | bytes 163872 | tf_op jit(solution)/shard_map/ppermute | solution.py:163
  56.0 0.0 copy-start.2
  56.0 0.0 copy-done.1
  56.0 0.7 %copy-done.2 = f32[40,1024]{1,0:T(8,128)} copy-done((f32[40,1024]{1,0:T(8,128)}, f32[40,1024]{1,0:T(8,128)S(1)}, u32[]{:S(2)}) %copy-start.2) | copy-done | bytes 163864
  56.7 2.0 %edges.1 = f32[8,24,1024]{2,1,0:T(8,128)} custom-call(f32[8,24,1024]{2,1,0:T(8,128)} %get-tuple-element.14.core, f32[40,1024]{1,0:T(8,128)} %copy-done.1, f32[40,1024]{1,0:T(8,128)} %copy-done.2), custom_call_target="tpu_custom_call", output_to_operand_aliasing={{}: (0, {})} | custom-call | tf_op jit(solution)/shard_map/edges/pallas_call | solution.py:204
  (4 shorter events, 0.0 us)
Async XLA Ops:
  3.0 6.6 %collective-permute-start = (f32[3,3,8,128]{3,2,1,0:T(8,128)}, f32[3,3,8,128]{3,2,1,0:T(8,128)S(1)}, u32[]{:S(2)}, u32[]{:S(2)}) collective-permute-start(f32[3,3,8,128]{3,2,1,0:T(8,128)} %get-tuple-element.12), channel_id=1, source_target_pairs={{0,1},{1,2},{2,3},{3,4},{4,5},{5,6},{6,7},{7,8},{8,9},{9,10},{10,1... | collective-permute-start | bytes 110600 | tf_op jit(solution)/shard_map/ppermute | solution.py:163
  6.1 8.2 %collective-permute-start.1 = (f32[3,3,8,128]{3,2,1,0:T(8,128)}, f32[3,3,8,128]{3,2,1,0:T(8,128)S(1)}, u32[]{:S(2)}, u32[]{:S(2)}) collective-permute-start(f32[3,3,8,128]{3,2,1,0:T(8,128)} %get-tuple-element.13), channel_id=1, source_target_pairs={{1,0},{2,1},{3,2},{4,3},{5,4},{6,5},{7,6},{8,7},{9,8},{10,9},{11,1... | collective-permute-start | bytes 110600 | tf_op jit(solution)/shard_map/ppermute | solution.py:163
  14.2 15.6 %collective-permute-start.4 = (f32[2,9,8,128]{3,2,1,0:T(8,128)S(1)}, f32[2,9,8,128]{3,2,1,0:T(8,128)S(1)}, u32[]{:S(2)}, u32[]{:S(2)}) collective-permute-start(f32[2,9,8,128]{3,2,1,0:T(8,128)S(1)} %get-tuple-element.19), channel_id=1, source_target_pairs={{16,0},{32,16},{48,32},{64,48},{80,64},{96,80},{112,96},{128,112},... | collective-permute-start | bytes 221192 | tf_op jit(solution)/shard_map/ppermute | solution.py:163
  16.4 13.4 %collective-permute-start.2 = (f32[2,9,8,128]{3,2,1,0:T(8,128)S(1)}, f32[2,9,8,128]{3,2,1,0:T(8,128)S(1)}, u32[]{:S(2)}, u32[]{:S(2)}) collective-permute-start(f32[2,9,8,128]{3,2,1,0:T(8,128)S(1)} %get-tuple-element.20), channel_id=1, source_target_pairs={{0,16},{16,32},{32,48},{48,64},{64,80},{80,96},{96,112},{112,128},... | collective-permute-start | bytes 221192 | tf_op jit(solution)/shard_map/ppermute | solution.py:163
  18.6 6.1 %collective-permute-start.5 = (f32[1,9,8,128]{3,2,1,0:T(8,128)S(1)}, f32[1,9,8,128]{3,2,1,0:T(8,128)S(1)}, u32[]{:S(2)}, u32[]{:S(2)}) collective-permute-start(f32[1,9,8,128]{3,2,1,0:T(8,128)S(1)} %get-tuple-element.17), channel_id=1, source_target_pairs={{32,0},{48,16},{64,32},{80,48},{96,64},{112,80},{128,96},{144,112}... | collective-permute-start | bytes 110600 | tf_op jit(solution)/shard_map/ppermute | solution.py:163
  22.7 7.1 %collective-permute-start.3 = (f32[1,9,8,128]{3,2,1,0:T(8,128)S(1)}, f32[1,9,8,128]{3,2,1,0:T(8,128)S(1)}, u32[]{:S(2)}, u32[]{:S(2)}) collective-permute-start(f32[1,9,8,128]{3,2,1,0:T(8,128)S(1)} %get-tuple-element.18), channel_id=1, source_target_pairs={{0,32},{16,48},{32,64},{48,80},{64,96},{80,112},{96,128},{112,144}... | collective-permute-start | bytes 110600 | tf_op jit(solution)/shard_map/ppermute | solution.py:163
  29.8 1.1 %copy-start = (f32[8,24,1024]{2,1,0:T(8,128)S(1)}, f32[8,24,1024]{2,1,0:T(8,128)}, u32[]{:S(2)}) copy-start(f32[8,24,1024]{2,1,0:T(8,128)} %old_ref.1) | copy-start | bytes 2359300
  44.1 7.4 %collective-permute-start.6 = (f32[40,1024]{1,0:T(8,128)S(1)}, f32[40,1024]{1,0:T(8,128)S(1)}, u32[]{:S(2)}, u32[]{:S(2)}) collective-permute-start(f32[40,1024]{1,0:T(8,128)S(1)} %get-tuple-element.15), channel_id=1, source_target_pairs={{0,1},{1,2},{2,3},{3,4},{4,5},{5,6},{6,7},{7,8},{8,9},{9,10},{10,1... | collective-permute-start | bytes 491528 | tf_op jit(solution)/shard_map/ppermute | solution.py:163
  46.1 9.8 %collective-permute-start.7 = (f32[40,1024]{1,0:T(8,128)S(1)}, f32[40,1024]{1,0:T(8,128)S(1)}, u32[]{:S(2)}, u32[]{:S(2)}) collective-permute-start(f32[40,1024]{1,0:T(8,128)S(1)} %get-tuple-element.16), channel_id=1, source_target_pairs={{1,0},{2,1},{3,2},{4,3},{5,4},{6,5},{7,6},{8,7},{9,8},{10,9},{11,1... | collective-permute-start | bytes 491528 | tf_op jit(solution)/shard_map/ppermute | solution.py:163
  51.6 4.4 %copy-start.1 = (f32[40,1024]{1,0:T(8,128)}, f32[40,1024]{1,0:T(8,128)S(1)}, u32[]{:S(2)}) copy-start(f32[40,1024]{1,0:T(8,128)S(1)} %collective-permute-done.6.from_left) | copy-start | bytes 491524
  56.0 0.7 %copy-start.2 = (f32[40,1024]{1,0:T(8,128)}, f32[40,1024]{1,0:T(8,128)S(1)}, u32[]{:S(2)}) copy-start(f32[40,1024]{1,0:T(8,128)S(1)} %collective-permute-done.7.from_right) | copy-start | bytes 491524

commit v2 on v0

v2 whole, which is shorter than its diff:
```python
import functools
import jax
import jax.numpy as jnp
from jax import lax
from jax.experimental import pallas as pl
from jax.experimental.pallas import tpu as pltpu
from jax.sharding import PartitionSpec as P

LOG2E = 1.4426950408889634
FAR = 1.0e6
W = 5
f32, bf16 = jnp.float32, jnp.bfloat16
ABOVE, OWN, BELOW = 0, 1, 2
CORE_ROWS = (128, 192, 128)
EDGE_ROWS = (64, 80, 64)


def quotient(n, d):
    return lax.shift_right_logical(n * ((65536 + d - 1) // d), 16)


def put_rows(ti, tj, start, group, core):
    n = (CORE_ROWS if core else EDGE_ROWS)[group]
    m = lax.broadcasted_iota(jnp.int32, (n, 128), 0)
    if core:
        row = m + (64 if group == BELOW else 0)
        i = quotient(row, 24)
        j = row - i * 24
    else:
        side = m >= n // 2
        e = jnp.where(side, m - n // 2, m) + (8 if group == BELOW else 0)
        i = quotient(e, 5)
        j = e - i * 5 + jnp.where(side, 24, -W)
    place = (i + (8, 0, -8)[group]).astype(f32)
    if group == ABOVE:
        place = jnp.where(i >= W, FAR, place)
    if group == BELOW:
        place = jnp.where(i < 8 - W, FAR, place)
    ti[start:start + n, :] = place
    tj[start:start + n, :] = j.astype(f32)


def split(v):
    h = v.astype(bf16)
    return h, (v - h.astype(f32)).astype(bf16)


def compact(lists, group, sources, blocks):
    row = lax.broadcasted_iota(jnp.int32, (8, 128), 0)
    dead = jnp.where(row == 3, 1.0, 0.0).astype(f32)
    count = jnp.int32(0)
    for ref, part in sources:
        bits = jnp.zeros((1, 128), f32)
        for s in range(9):
            bits = bits + ref[part, s, 5:6, :] * float(1 << s)
        mask = jnp.max(bits).astype(jnp.int32)
        for s in range(9):
            lists[group, count] = ref[part, s]
            count = count + (lax.shift_right_logical(mask, s) & 1)
    for s in range(blocks - 1):
        lists[group, count + s] = dead
    return lax.div(count + (blocks - 1), jnp.int32(blocks))


def add_field(lists, steps, ti, tj, rows, starts, adds, depth, blocks, wide):
    k_io = lax.broadcasted_iota(jnp.int32, (1, wide), 1).astype(f32)
    dot = functools.partial(jnp.dot, preferred_element_type=f32)

    def stage(g, t):
        n = rows[g]
        recs = [lists[g, t * blocks + q] for q in range(blocks)]
        rec = jnp.concatenate(recs, axis=1)
        x, y, weight = rec[0:1] * 8.0, rec[1:2] * 24.0, rec[4:5]
        c = (-0.5 * LOG2E) / (rec[3:4] * rec[3:4])
        ri, rj = ti[starts[g]:starts[g] + n, :], tj[starts[g]:starts[g] + n, :]
        dx = jnp.concatenate([ri] * blocks, axis=1) - x
        dy = jnp.concatenate([rj] * blocks, axis=1) - y
        ph, plo = split(jnp.exp2((dx * dx + dy * dy) * c) * weight)
        cols = jnp.concatenate([jnp.transpose(r) for r in recs], axis=0)
        z = cols[:, 2:3] * 1024.0
        cz = (-0.5 * LOG2E) / (cols[:, 3:4] * cols[:, 3:4])

        def along(b):
            d = k_io - (z - float(b * wide))
            return split(jnp.exp2(d * (d * cz)))

        nxt = along(0)
        for b in range(depth // wide):
            zh, zl = nxt
            if b + 1 < depth // wide:
                nxt = along(b + 1)
            r = dot(jnp.concatenate([ph, plo, ph], 1), jnp.concatenate([zh, zh, zl], 0))
            for ref, to, count, source in adds[g]:
                ref[to:to + count, b * wide:(b + 1) * wide] += r[source:source + count]

    for g in range(3):
        def step(t, carry, g=g):
            stage(g, t)
            return carry
        lax.fori_loop(0, steps[g], step, 0)


def core_adds(ref):
    return [[(ref, 0, 128, 0)], [(ref, 0, 192, 0)], [(ref, 64, 128, 0)]]


def edge_adds(left, right):
    return [
        [(left, 0, 32, 0), (right, 0, 32, 32)],
        [(left, 0, 40, 0), (right, 0, 40, 40)],
        [(left, 8, 32, 0), (right, 8, 32, 32)],
    ]


def both_adds(core, left, right):
    return [
        a + [(ref, to, n, source + CORE_ROWS[g]) for ref, to, n, source in b]
        for g, (a, b) in enumerate(zip(core_adds(core), edge_adds(left, right)))
    ]


def prepare(ti, tj, kinds):
    rows, starts, at = [], [], 0
    for g in range(3):
        starts.append(at)
        for core in kinds:
            put_rows(ti, tj, at, g, core)
            at += (CORE_ROWS if core else EDGE_ROWS)[g]
        rows.append(at - starts[-1])
    return rows, starts


BLOCKS, WIDE = 4, 256


def first_kernel(own, old, core, left, right, lists, ti, tj):
    depth = core.shape[1]
    rows, starts = prepare(ti, tj, (True, False))
    core[...] = old[...].reshape(core.shape)
    for ref in (left, right):
        ref[...] = jnp.zeros_like(ref)
    steps = [compact(lists, g, ((own, g),), BLOCKS) for g in range(3)]
    add_field(lists, steps, ti, tj, rows, starts, both_adds(core, left, right), depth, BLOCKS, WIDE)


def others(above, below, beside):
    return (
        ((above, 1), (beside, 0)),
        ((beside, 1), (beside, 2)),
        ((below, 0), (beside, 3)),
    )


def rest_kernel(above, below, beside, core0, left0, right0, core, left, right, lists, ti, tj):
    depth = core.shape[1]
    rows, starts = prepare(ti, tj, (True, False))
    core[...] = core0[...]
    left[...] = left0[...]
    right[...] = right0[...]
    steps = [compact(lists, g, s, BLOCKS) for g, s in enumerate(others(above, below, beside))]
    add_field(lists, steps, ti, tj, rows, starts, both_adds(core, left, right), depth, BLOCKS, WIDE)


VM = pl.BlockSpec(memory_space=pltpu.VMEM)


def call(kernel, name, outs, rows, capacity, cost, *operands):
    return pl.pallas_call(
        kernel,
        out_shape=[jax.ShapeDtypeStruct(s, f32) for s in outs],
        in_specs=[VM] * len(operands),
        out_specs=[VM] * len(outs),
        scratch_shapes=[
            pltpu.VMEM((3, capacity, 8, 128), f32),
            pltpu.VMEM((rows, 128), f32),
            pltpu.VMEM((rows, 128), f32),
        ],
        compiler_params=pltpu.CompilerParams(vmem_limit_bytes=32 * 1024 * 1024),
        cost_estimate=pl.CostEstimate(
            flops=int(cost * 2e8), bytes_accessed=4_000_000, transcendentals=int(cost * 300_000)
        ),
        name=name,
    )(*operands)


def pack_kernel(heading, offsets, widths, solvation, minus, same, plus, slots, taken):
    slots[...] = jnp.zeros_like(slots)
    for h in range(9):
        taken[h] = 0
    tile_row, tile_rows = lax.axis_index("gx"), lax.axis_size("gx")
    for b in range(offsets.shape[0]):
        h = heading[b]
        n = taken[h]
        taken[h] = n + 1
        row, col = lax.div(h, 3), lax.rem(h, 3)
        place = col * 9 + row * 3 + n
        slots[place, 0:3, :] = offsets[b]
        slots[place, 3:4, :] = widths[b:b + 1, :]
        slots[place, 4:5, :] = solvation[b:b + 1, :]
        home = tile_row + row - 1
        inside = (home >= 0) & (home < tile_rows)
        slots[place, 5:6, :] = jnp.full((1, 128), jnp.where(inside, 1.0, 0.0), f32)
    for k, out in enumerate((minus, same, plus)):
        out[...] = slots[9 * k:9 * k + 9].reshape(out.shape)


def edge_kernel(core, from_left, from_right, out):
    out[:, 8:16, :] = core[:, 8:16, :]
    for i in range(core.shape[0]):
        out[i, 0:8, :] = core[i, 0:8, :]
        out[i, 0:5, :] += from_left[i * 5:i * 5 + 5, :]
        out[i, 16:24, :] = core[i, 16:24, :]
        out[i, 19:24, :] += from_right[i * 5:i * 5 + 5, :]


def passed_along(value, axis, steps):
    count = lax.axis_size(axis)
    first, last = (max(0, -steps), min(count, count - steps))
    return lax.ppermute(value, axis, [(source, source + steps) for source in range(first, last)])


def body(offsets, widths, solvation, heading, old_map):
    depth = old_map.shape[2]
    third = jax.ShapeDtypeStruct((3, 3, 8, 128), f32)
    small = pltpu.CompilerParams(vmem_limit_bytes=8 * 1024 * 1024)
    minus, same, plus = pl.pallas_call(
        pack_kernel,
        out_shape=[third] * 3,
        in_specs=[pl.BlockSpec(memory_space=pltpu.SMEM), VM, VM, VM],
        out_specs=[VM] * 3,
        scratch_shapes=[pltpu.VMEM((27, 8, 128), f32), pltpu.SMEM((9,), jnp.int32)],
        compiler_params=small,
        name="pack",
    )(heading[:, 0], offsets, widths, solvation)
    own = jnp.concatenate(
        [same, passed_along(plus, "gy", 1), passed_along(minus, "gy", -1)], axis=1
    )
    above = passed_along(own[1:3], "gx", 2)
    below = passed_along(own[0:2], "gx", -2)
    plane, edge = (old_map.shape[0] * old_map.shape[1], depth), (40, depth)
    outs = [plane, edge, edge]
    part = call(first_kernel, "first", outs, 656, 36, 12, own, old_map)
    above, below, *part = lax.optimization_barrier((above, below, *part))
    first = lax.rem(lax.axis_index("gx"), 2) == 0
    handed = jnp.stack(
        [
            jnp.where(first, own[1], above[0]),
            jnp.where(first, own[2], own[0]),
            jnp.where(first, below[0], above[1]),
            jnp.where(first, below[1], own[1]),
        ]
    )
    pairs = [(r, r + 1 - 2 * (r % 2)) for r in range(lax.axis_size("gx"))]
    beside = lax.ppermute(handed, "gx", pairs)
    core, left, right = call(rest_kernel, "rest", outs, 656, 36, 24, above, below, beside, *part)
    from_left = passed_along(right, "gy", 1)
    from_right = passed_along(left, "gy", -1)
    return pl.pallas_call(
        edge_kernel,
        out_shape=jax.ShapeDtypeStruct(old_map.shape, f32),
        in_specs=[VM] * 3,
        out_specs=VM,
        compiler_params=small,
        name="edges",
    )(core.reshape(old_map.shape), from_left, from_right)


def solution(mesh):
    placed = (
        P(("gx", "gy"), None, None),
        P(("gx", "gy"), None),
        P(("gx", "gy"), None),
        P(("gx", "gy"), None),
        P("gx", "gy", None),
    )
    return jax.shard_map(
        body, mesh=mesh, in_specs=placed, out_specs=P("gx", "gy", None), check_vma=False
    )
```

time: 137 us -> 55.5 us (0.41)
  the two profiles are of different devices: /device:TPU:251 before, /device:TPU:376 now
where the time goes in v2:
time: 55.5 us; the launch traced here: 55.1 us
  starting transfers between devices  20.7 us (37%)
  Pallas kernels  17.5 us (32%)
  waiting for transfers between devices  12.8 us (23%)
  local copies, waits for them, and re-layouts  3.94 us (7%)
    ppermute x6, starting transfers between devices, passed_along(): lax.ppermute(value, axis, [(source, source + steps) for source in range(f...  18.7 us
    pallas_call x2, Pallas kernels, call(): pl.pallas_call(kernel, out_shape=[jax.ShapeDtypeStruct(s, f32) for s in o...  15.8 us
    ppermute x6, waiting for transfers between devices, passed_along(): lax.ppermute(value, axis, [(source, source + steps) for source in range(f...  11.5 us
    unnamed x12, local copies, waits for them, and re-layouts  3.92 us
    ppermute x1, starting transfers between devices, body(): beside = lax.ppermute(handed, 'gx', pairs)  1.92 us
    ppermute x1, waiting for transfers between devices, body(): beside = lax.ppermute(handed, 'gx', pairs)  1.34 us
  transfers between devices with their start and end apart: 7, of which 4 were waited for; matrix products, arithmetic and copies ran while one was open for 0% of the time, Pallas kernels for 10%

profile of v2, /device:TPU:376, one launch (start us, length us, event | category | flops | bytes accessed | tf_op | source)
XLA Modules:
  0.0 55.1 jit_solution(3259562010940883341)
XLA Ops:
  0.0 0.0 copy-start.3
  0.0 0.7 %copy-done.3 = s32[12,1]{0,1:T(1,128)S(1)} copy-done((s32[12,1]{0,1:T(1,128)S(1)}, s32[12,1]{0,1:T(1,128)}, u32[]{:S(2)}) %copy-start.3) | copy-done | bytes 72
  0.7 0.0 copy-start
  0.7 0.7 %copy-done = f32[12,3,128]{2,1,0:T(4,128)S(1)} copy-done((f32[12,3,128]{2,1,0:T(4,128)S(1)}, f32[12,3,128]{2,1,0:T(4,128)}, u32[]{:S(2)}) %copy-start) | copy-done | bytes 18456
  1.4 0.0 copy-start.1
  1.4 0.7 %copy-done.1 = f32[12,128]{1,0:T(8,128)S(1)} copy-done((f32[12,128]{1,0:T(8,128)S(1)}, f32[12,128]{1,0:T(8,128)}, u32[]{:S(2)}) %copy-start.1) | copy-done | bytes 6168
  2.1 0.0 copy-start.2
  2.1 0.7 %copy-done.2 = f32[12,128]{1,0:T(8,128)S(1)} copy-done((f32[12,128]{1,0:T(8,128)S(1)}, f32[12,128]{1,0:T(8,128)}, u32[]{:S(2)}) %copy-start.2) | copy-done | bytes 6168
  2.8 0.7 %pack.1 = (f32[3,3,8,128]{3,2,1,0:T(8,128)S(1)}, f32[3,3,8,128]{3,2,1,0:T(8,128)S(1)}, f32[3,3,8,128]{3,2,1,0:T(8,128)S(1)}) custom-call(s32[12]{0:T(128)S(1)} %bitcast.3, f32[12,3,128]{2,1,0:T(4,128)S(1)} %copy-done, f32[12,128]{1,0:T(8,128)S(1)} %copy-done.1, f32[12,128]{1,0:T(8,128)S(1)} %copy-done.2), custom_call_target="tpu_custom_call" | custom-call | tf_op jit(solution)/shard_map/pack/pallas_call | solution.py:226
  3.4 3.1 %collective-permute-start = (f32[3,3,8,128]{3,2,1,0:T(8,128)S(1)}, f32[3,3,8,128]{3,2,1,0:T(8,128)S(1)}, u32[]{:S(2)}, u32[]{:S(2)}) collective-permute-start(f32[3,3,8,128]{3,2,1,0:T(8,128)S(1)} %get-tuple-element.20), channel_id=1, source_target_pairs={{0,1},{1,2},{2,3},{3,4},{4,5},{5,6},{6,7},{7,8},{8,9},{9,10},{10,1... | collective-permute-start | bytes 110600 | tf_op jit(solution)/shard_map/ppermute | solution.py:219
  6.5 2.8 %collective-permute-start.1 = (f32[3,3,8,128]{3,2,1,0:T(8,128)S(1)}, f32[3,3,8,128]{3,2,1,0:T(8,128)S(1)}, u32[]{:S(2)}, u32[]{:S(2)}) collective-permute-start(f32[3,3,8,128]{3,2,1,0:T(8,128)S(1)} %get-tuple-element.21), channel_id=1, source_target_pairs={{1,0},{2,1},{3,2},{4,3},{5,4},{6,5},{7,6},{8,7},{9,8},{10,9},{11,1... | collective-permute-start | bytes 110600 | tf_op jit(solution)/shard_map/ppermute | solution.py:219
  9.3 0.0 collective-permute-done
  9.3 5.1 %collective-permute-done.1 = f32[3,3,8,128]{3,2,1,0:T(8,128)S(1)} collective-permute-done((f32[3,3,8,128]{3,2,1,0:T(8,128)S(1)}, f32[3,3,8,128]{3,2,1,0:T(8,128)S(1)}, u32[]{:S(2)}, u32[]{:S(2)}) %collective-permute-start.1) | collective-permute-done | bytes 36896 | tf_op jit(solution)/shard_map/ppermute | solution.py:219
  14.5 2.9 %collective-permute-start.3 = (f32[2,9,8,128]{3,2,1,0:T(8,128)S(1)}, f32[2,9,8,128]{3,2,1,0:T(8,128)S(1)}, u32[]{:S(2)}, u32[]{:S(2)}) collective-permute-start(f32[2,9,8,128]{3,2,1,0:T(8,128)S(1)} %get-tuple-element.37), channel_id=1, source_target_pairs={{32,0},{48,16},{64,32},{80,48},{96,64},{112,80},{128,96},{144,112}... | collective-permute-start | bytes 221192 | tf_op jit(solution)/shard_map/ppermute | solution.py:219
  17.4 4.1 %collective-permute-start.2 = (f32[2,9,8,128]{3,2,1,0:T(8,128)S(1)}, f32[2,9,8,128]{3,2,1,0:T(8,128)S(1)}, u32[]{:S(2)}, u32[]{:S(2)}) collective-permute-start(f32[2,9,8,128]{3,2,1,0:T(8,128)S(1)} %get-tuple-element.38), channel_id=1, source_target_pairs={{0,32},{16,48},{32,64},{48,80},{64,96},{80,112},{96,128},{112,144}... | collective-permute-start | bytes 221192 | tf_op jit(solution)/shard_map/ppermute | solution.py:219
  21.6 0.0 copy-start.4
  21.6 1.1 %copy-done.4 = f32[8,24,1024]{2,1,0:T(8,128)S(1)} copy-done((f32[8,24,1024]{2,1,0:T(8,128)S(1)}, f32[8,24,1024]{2,1,0:T(8,128)}, u32[]{:S(2)}) %copy-start.4) | copy-done | bytes 786456
  22.7 5.7 %first.1 = (f32[192,1024]{1,0:T(8,128)S(1)}, f32[40,1024]{1,0:T(8,128)S(1)}, f32[40,1024]{1,0:T(8,128)S(1)}) custom-call(f32[3,9,8,128]{3,2,1,0:T(8,128)S(1)} %constant_dynamic-update-slice_fusion.own, f32[8,24,1024]{2,1,0:T(8,128)S(1)} %copy-done.4), custom_call_target="tpu_custom_call" | custom-call | flops 2400000000 | bytes 4000000 | tf_op jit(solution)/shard_map/first/pallas_call | solution.py:168
  28.4 0.0 collective-permute-done.3.below
  28.4 0.0 collective-permute-done.2.above
  28.5 1.9 %collective-permute-start.4 = (f32[4,9,8,128]{3,2,1,0:T(8,128)S(1)}, f32[4,9,8,128]{3,2,1,0:T(8,128)S(1)}, u32[]{:S(2)}, u32[]{:S(2)}) collective-permute-start(f32[4,9,8,128]{3,2,1,0:T(8,128)S(1)} %pad_maximum_fusion), channel_id=1, source_target_pairs={{0,16},{16,0},{32,48},{48,32},{64,80},{80,64},{96,112},{112,96},{1... | collective-permute-start | bytes 442376 | tf_op jit(solution)/shard_map/ppermute | solution.py:254
  30.4 1.3 %collective-permute-done.4.beside = f32[4,9,8,128]{3,2,1,0:T(8,128)S(1)} collective-permute-done((f32[4,9,8,128]{3,2,1,0:T(8,128)S(1)}, f32[4,9,8,128]{3,2,1,0:T(8,128)S(1)}, u32[]{:S(2)}, u32[]{:S(2)}) %collective-permute-start.4) | collective-permute-done | bytes 147488 | tf_op jit(solution)/shard_map/ppermute | solution.py:254
  31.7 10.1 %rest.1 = (f32[192,1024]{1,0:T(8,128)S(1)}, f32[40,1024]{1,0:T(8,128)S(1)}, f32[40,1024]{1,0:T(8,128)S(1)}) custom-call(f32[2,9,8,128]{3,2,1,0:T(8,128)S(1)} %collective-permute-done.2.above, f32[2,9,8,128]{3,2,1,0:T(8,128)S(1)} %collective-permute-done.3.below, f32[4,9,8,128]{3,2,1,0:T(8,128)S(1)} %collective-permute-done.4.beside, ...), custom_call_target="tpu_custom_call" | custom-call | flops 4800000000 | bytes 4000000 | tf_op jit(solution)/shard_map/rest/pallas_call | solution.py:168
  41.9 1.9 %collective-permute-start.5 = (f32[40,1024]{1,0:T(8,128)S(1)}, f32[40,1024]{1,0:T(8,128)S(1)}, u32[]{:S(2)}, u32[]{:S(2)}) collective-permute-start(f32[40,1024]{1,0:T(8,128)S(1)} %get-tuple-element.31), channel_id=1, source_target_pairs={{0,1},{1,2},{2,3},{3,4},{4,5},{5,6},{6,7},{7,8},{8,9},{9,10},{10,1... | collective-permute-start | bytes 491528 | tf_op jit(solution)/shard_map/ppermute | solution.py:219
  43.8 3.9 %collective-permute-start.6 = (f32[40,1024]{1,0:T(8,128)S(1)}, f32[40,1024]{1,0:T(8,128)S(1)}, u32[]{:S(2)}, u32[]{:S(2)}) collective-permute-start(f32[40,1024]{1,0:T(8,128)S(1)} %get-tuple-element.32), channel_id=1, source_target_pairs={{1,0},{2,1},{3,2},{4,3},{5,4},{6,5},{7,6},{8,7},{9,8},{10,9},{11,1... | collective-permute-start | bytes 491528 | tf_op jit(solution)/shard_map/ppermute | solution.py:219
  47.7 2.3 %collective-permute-done.5.from_left = f32[40,1024]{1,0:T(8,128)S(1)} collective-permute-done((f32[40,1024]{1,0:T(8,128)S(1)}, f32[40,1024]{1,0:T(8,128)S(1)}, u32[]{:S(2)}, u32[]{:S(2)}) %collective-permute-start.5) | collective-permute-done | bytes 163872 | tf_op jit(solution)/shard_map/ppermute | solution.py:219
  50.0 4.0 %collective-permute-done.6.from_right = f32[40,1024]{1,0:T(8,128)S(1)} collective-permute-done((f32[40,1024]{1,0:T(8,128)S(1)}, f32[40,1024]{1,0:T(8,128)S(1)}, u32[]{:S(2)}, u32[]{:S(2)}) %collective-permute-start.6) | collective-permute-done | bytes 163872 | tf_op jit(solution)/shard_map/ppermute | solution.py:219
  54.0 1.0 %edges.1 = f32[8,24,1024]{2,1,0:T(8,128)} custom-call(f32[8,24,1024]{2,1,0:T(8,128)S(1)} %bitcast.2, f32[40,1024]{1,0:T(8,128)S(1)} %collective-permute-done.5.from_left, f32[40,1024]{1,0:T(8,128)S(1)} %collective-permute-done.6.from_right), custom_call_target="tpu_custom_call" | custom-call | tf_op jit(solution)/shard_map/edges/pallas_call | solution.py:258
  (6 shorter events, 0.1 us)
Async XLA Ops:
  0.0 0.7 %copy-start.3 = (s32[12,1]{0,1:T(1,128)S(1)}, s32[12,1]{0,1:T(1,128)}, u32[]{:S(2)}) copy-start(s32[12,1]{0,1:T(1,128)} %param.8) | copy-start | bytes 148
  0.7 0.7 %copy-start = (f32[12,3,128]{2,1,0:T(4,128)S(1)}, f32[12,3,128]{2,1,0:T(4,128)}, u32[]{:S(2)}) copy-start(f32[12,3,128]{2,1,0:T(4,128)} %offsets.1) | copy-start | bytes 55300
  1.4 0.7 %copy-start.1 = (f32[12,128]{1,0:T(8,128)S(1)}, f32[12,128]{1,0:T(8,128)}, u32[]{:S(2)}) copy-start(f32[12,128]{1,0:T(8,128)} %widths.1) | copy-start | bytes 18436
  2.1 0.7 %copy-start.2 = (f32[12,128]{1,0:T(8,128)S(1)}, f32[12,128]{1,0:T(8,128)}, u32[]{:S(2)}) copy-start(f32[12,128]{1,0:T(8,128)} %solvation.1) | copy-start | bytes 18436
  3.4 5.9 %collective-permute-start = (f32[3,3,8,128]{3,2,1,0:T(8,128)S(1)}, f32[3,3,8,128]{3,2,1,0:T(8,128)S(1)}, u32[]{:S(2)}, u32[]{:S(2)}) collective-permute-start(f32[3,3,8,128]{3,2,1,0:T(8,128)S(1)} %get-tuple-element.20), channel_id=1, source_target_pairs={{0,1},{1,2},{2,3},{3,4},{4,5},{5,6},{6,7},{7,8},{8,9},{9,10},{10,1... | collective-permute-start | bytes 110600 | tf_op jit(solution)/shard_map/ppermute | solution.py:219
  6.5 8.0 %collective-permute-start.1 = (f32[3,3,8,128]{3,2,1,0:T(8,128)S(1)}, f32[3,3,8,128]{3,2,1,0:T(8,128)S(1)}, u32[]{:S(2)}, u32[]{:S(2)}) collective-permute-start(f32[3,3,8,128]{3,2,1,0:T(8,128)S(1)} %get-tuple-element.21), channel_id=1, source_target_pairs={{1,0},{2,1},{3,2},{4,3},{5,4},{6,5},{7,6},{8,7},{9,8},{10,9},{11,1... | collective-permute-start | bytes 110600 | tf_op jit(solution)/shard_map/ppermute | solution.py:219
  14.5 13.9 %collective-permute-start.3 = (f32[2,9,8,128]{3,2,1,0:T(8,128)S(1)}, f32[2,9,8,128]{3,2,1,0:T(8,128)S(1)}, u32[]{:S(2)}, u32[]{:S(2)}) collective-permute-start(f32[2,9,8,128]{3,2,1,0:T(8,128)S(1)} %get-tuple-element.37), channel_id=1, source_target_pairs={{32,0},{48,16},{64,32},{80,48},{96,64},{112,80},{128,96},{144,112}... | collective-permute-start | bytes 221192 | tf_op jit(solution)/shard_map/ppermute | solution.py:219
  17.4 11.0 %collective-permute-start.2 = (f32[2,9,8,128]{3,2,1,0:T(8,128)S(1)}, f32[2,9,8,128]{3,2,1,0:T(8,128)S(1)}, u32[]{:S(2)}, u32[]{:S(2)}) collective-permute-start(f32[2,9,8,128]{3,2,1,0:T(8,128)S(1)} %get-tuple-element.38), channel_id=1, source_target_pairs={{0,32},{16,48},{32,64},{48,80},{64,96},{80,112},{96,128},{112,144}... | collective-permute-start | bytes 221192 | tf_op jit(solution)/shard_map/ppermute | solution.py:219
  21.6 1.1 %copy-start.4 = (f32[8,24,1024]{2,1,0:T(8,128)S(1)}, f32[8,24,1024]{2,1,0:T(8,128)}, u32[]{:S(2)}) copy-start(f32[8,24,1024]{2,1,0:T(8,128)} %old.1) | copy-start | bytes 2359300
  28.5 3.3 %collective-permute-start.4 = (f32[4,9,8,128]{3,2,1,0:T(8,128)S(1)}, f32[4,9,8,128]{3,2,1,0:T(8,128)S(1)}, u32[]{:S(2)}, u32[]{:S(2)}) collective-permute-start(f32[4,9,8,128]{3,2,1,0:T(8,128)S(1)} %pad_maximum_fusion), channel_id=1, source_target_pairs={{0,16},{16,0},{32,48},{48,32},{64,80},{80,64},{96,112},{112,96},{1... | collective-permute-start | bytes 442376 | tf_op jit(solution)/shard_map/ppermute | solution.py:254
  41.9 8.1 %collective-permute-start.5 = (f32[40,1024]{1,0:T(8,128)S(1)}, f32[40,1024]{1,0:T(8,128)S(1)}, u32[]{:S(2)}, u32[]{:S(2)}) collective-permute-start(f32[40,1024]{1,0:T(8,128)S(1)} %get-tuple-element.31), channel_id=1, source_target_pairs={{0,1},{1,2},{2,3},{3,4},{4,5},{5,6},{6,7},{7,8},{8,9},{9,10},{10,1... | collective-permute-start | bytes 491528 | tf_op jit(solution)/shard_map/ppermute | solution.py:219
  43.8 10.3 %collective-permute-start.6 = (f32[40,1024]{1,0:T(8,128)S(1)}, f32[40,1024]{1,0:T(8,128)S(1)}, u32[]{:S(2)}, u32[]{:S(2)}) collective-permute-start(f32[40,1024]{1,0:T(8,128)S(1)} %get-tuple-element.32), channel_id=1, source_target_pairs={{1,0},{2,1},{3,2},{4,3},{5,4},{6,5},{7,6},{8,7},{9,8},{10,9},{11,1... | collective-permute-start | bytes 491528 | tf_op jit(solution)/shard_map/ppermute | solution.py:219

commit v3 on v2

--- a/solution.py
+++ b/solution.py
@@ -59,16 +59,16 @@
             count = count + (lax.shift_right_logical(mask, s) & 1)
     for s in range(blocks - 1):
         lists[group, count + s] = dead
-    return lax.div(count + (blocks - 1), jnp.int32(blocks))
-
-
-def add_field(lists, steps, ti, tj, rows, starts, adds, depth, blocks, wide):
+    return count
+
+
+def add_field(lists, counts, ti, tj, rows, starts, adds, depth, blocks, wide):
     k_io = lax.broadcasted_iota(jnp.int32, (1, wide), 1).astype(f32)
     dot = functools.partial(jnp.dot, preferred_element_type=f32)
 
-    def stage(g, t):
+    def stage(g, at, blocks):
         n = rows[g]
-        recs = [lists[g, t * blocks + q] for q in range(blocks)]
+        recs = [lists[g, at + q] for q in range(blocks)]
         rec = jnp.concatenate(recs, axis=1)
         x, y, weight = rec[0:1] * 8.0, rec[1:2] * 24.0, rec[4:5]
         c = (-0.5 * LOG2E) / (rec[3:4] * rec[3:4])
@@ -95,9 +95,14 @@
 
     for g in range(3):
         def step(t, carry, g=g):
-            stage(g, t)
+            stage(g, t * blocks, blocks)
             return carry
-        lax.fori_loop(0, steps[g], step, 0)
+        whole = lax.div(counts[g] + (blocks // 2 - 1), jnp.int32(blocks))
+        lax.fori_loop(0, whole, step, 0)
+
+        @pl.when(whole * blocks < counts[g])
+        def _(g=g, whole=whole):
+            stage(g, whole * blocks, blocks // 2)
 
 
 def core_adds(ref):
@@ -133,14 +138,13 @@
 BLOCKS, WIDE = 4, 256
 
 
-def first_kernel(own, old, core, left, right, lists, ti, tj):
+def first_kernel(own, core, left, right, lists, ti, tj):
     depth = core.shape[1]
     rows, starts = prepare(ti, tj, (True, False))
-    core[...] = old[...].reshape(core.shape)
-    for ref in (left, right):
+    for ref in (core, left, right):
         ref[...] = jnp.zeros_like(ref)
-    steps = [compact(lists, g, ((own, g),), BLOCKS) for g in range(3)]
-    add_field(lists, steps, ti, tj, rows, starts, both_adds(core, left, right), depth, BLOCKS, WIDE)
+    counts = [compact(lists, g, ((own, g),), BLOCKS) for g in range(3)]
+    add_field(lists, counts, ti, tj, rows, starts, both_adds(core, left, right), depth, BLOCKS, WIDE)
 
 
 def others(above, below, beside):
@@ -157,11 +161,12 @@
     core[...] = core0[...]
     left[...] = left0[...]
     right[...] = right0[...]
-    steps = [compact(lists, g, s, BLOCKS) for g, s in enumerate(others(above, below, beside))]
-    add_field(lists, steps, ti, tj, rows, starts, both_adds(core, left, right), depth, BLOCKS, WIDE)
+    counts = [compact(lists, g, s, BLOCKS) for g, s in enumerate(others(above, below, beside))]
+    add_field(lists, counts, ti, tj, rows, starts, both_adds(core, left, right), depth, BLOCKS, WIDE)
 
 
 VM = pl.BlockSpec(memory_space=pltpu.VMEM)
+HBM = pl.BlockSpec(memory_space=pltpu.HBM)
 
 
 def call(kernel, name, outs, rows, capacity, cost, *operands):
@@ -183,10 +188,17 @@
     )(*operands)
 
 
-def pack_kernel(heading, offsets, widths, solvation, minus, same, plus, slots, taken):
+def pack_kernel(*refs):
+    hbm, (minus, same, plus), local, (slots, taken, sems) = refs[:4], refs[4:7], refs[7:11], refs[11:]
+    fetches = [pltpu.make_async_copy(a, b, sems.at[n]) for n, (a, b) in enumerate(zip(hbm, local))]
+    for fetch in fetches:
+        fetch.start()
+    heading, offsets, widths, solvation = local
     slots[...] = jnp.zeros_like(slots)
     for h in range(9):
         taken[h] = 0
+    for fetch in fetches:
+        fetch.wait()
     tile_row, tile_rows = lax.axis_index("gx"), lax.axis_size("gx")
     for b in range(offsets.shape[0]):
         h = heading[b]
@@ -204,12 +216,10 @@
         out[...] = slots[9 * k:9 * k + 9].reshape(out.shape)
 
 
-def edge_kernel(core, from_left, from_right, out):
-    out[:, 8:16, :] = core[:, 8:16, :]
+def edge_kernel(core, old, from_left, from_right, out):
+    out[...] = core[...] + old[...]
     for i in range(core.shape[0]):
-        out[i, 0:8, :] = core[i, 0:8, :]
         out[i, 0:5, :] += from_left[i * 5:i * 5 + 5, :]
-        out[i, 16:24, :] = core[i, 16:24, :]
         out[i, 19:24, :] += from_right[i * 5:i * 5 + 5, :]
 
 
@@ -226,9 +236,17 @@
     minus, same, plus = pl.pallas_call(
         pack_kernel,
         out_shape=[third] * 3,
-        in_specs=[pl.BlockSpec(memory_space=pltpu.SMEM), VM, VM, VM],
+        in_specs=[HBM] * 4,
         out_specs=[VM] * 3,
-        scratch_shapes=[pltpu.VMEM((27, 8, 128), f32), pltpu.SMEM((9,), jnp.int32)],
+        scratch_shapes=[
+            pltpu.SMEM((offsets.shape[0],), jnp.int32),
+            pltpu.VMEM(offsets.shape, f32),
+            pltpu.VMEM(widths.shape, f32),
+            pltpu.VMEM(solvation.shape, f32),
+            pltpu.VMEM((27, 8, 128), f32),
+            pltpu.SMEM((9,), jnp.int32),
+            pltpu.SemaphoreType.DMA((4,)),
+        ],
         compiler_params=small,
         name="pack",
     )(heading[:, 0], offsets, widths, solvation)
@@ -239,7 +257,7 @@
     below = passed_along(own[0:2], "gx", -2)
     plane, edge = (old_map.shape[0] * old_map.shape[1], depth), (40, depth)
     outs = [plane, edge, edge]
-    part = call(first_kernel, "first", outs, 656, 36, 12, own, old_map)
+    part = call(first_kernel, "first", outs, 656, 36, 12, own)
     above, below, *part = lax.optimization_barrier((above, below, *part))
     first = lax.rem(lax.axis_index("gx"), 2) == 0
     handed = jnp.stack(
@@ -258,11 +276,11 @@
     return pl.pallas_call(
         edge_kernel,
         out_shape=jax.ShapeDtypeStruct(old_map.shape, f32),
-        in_specs=[VM] * 3,
+        in_specs=[VM] * 4,
         out_specs=VM,
         compiler_params=small,
         name="edges",
-    )(core.reshape(old_map.shape), from_left, from_right)
+    )(core.reshape(old_map.shape), old_map, from_left, from_right)
 
 
 def solution(mesh):

time: 55.5 us -> 53.9 us (0.971)
  the two profiles are of different devices: /device:TPU:376 before, /device:TPU:248 now
where the time goes in v3:
time: 53.9 us; the launch traced here: 53.5 us
  starting transfers between devices  20.8 us (39%)
  Pallas kernels  16.9 us (31%)
  waiting for transfers between devices  12.8 us (24%)
  local copies, waits for them, and re-layouts  2.81 us (5%)
    ppermute x6, starting transfers between devices, passed_along(): lax.ppermute(value, axis, [(source, source + steps) for source in range(f...  18.7 us
    pallas_call x2, Pallas kernels, call(): pl.pallas_call(kernel, out_shape=[jax.ShapeDtypeStruct(s, f32) for s in o...  15.1 us
    ppermute x6, waiting for transfers between devices, passed_along(): lax.ppermute(value, axis, [(source, source + steps) for source in range(f...  11.5 us
    unnamed x12, local copies, waits for them, and re-layouts  2.8 us
    ppermute x1, starting transfers between devices, body(): beside = lax.ppermute(handed, 'gx', pairs)  2.05 us
    ppermute x1, waiting for transfers between devices, body(): beside = lax.ppermute(handed, 'gx', pairs)  1.34 us
  transfers between devices with their start and end apart: 7, of which 4 were waited for; matrix products, arithmetic and copies ran while one was open for 0% of the time, Pallas kernels for 10%

profile of v3, /device:TPU:248, one launch (start us, length us, event | category | flops | bytes accessed | tf_op | source)
XLA Modules:
  0.0 53.5 jit_solution(13949146933303984156)
XLA Ops:
  0.0 0.0 copy-start.4
  0.0 0.7 %copy-done.4 = s32[12,1]{0,1:T(1,128)S(1)} copy-done((s32[12,1]{0,1:T(1,128)S(1)}, s32[12,1]{0,1:T(1,128)}, u32[]{:S(2)}) %copy-start.4) | copy-done | bytes 72
  0.7 0.0 copy-start.1
  0.7 0.7 %copy-done.1 = f32[12,3,128]{2,1,0:T(4,128)S(1)} copy-done((f32[12,3,128]{2,1,0:T(4,128)S(1)}, f32[12,3,128]{2,1,0:T(4,128)}, u32[]{:S(2)}) %copy-start.1) | copy-done | bytes 18456
  1.4 0.0 copy-start.2
  1.4 0.7 %copy-done.2 = f32[12,128]{1,0:T(8,128)S(1)} copy-done((f32[12,128]{1,0:T(8,128)S(1)}, f32[12,128]{1,0:T(8,128)}, u32[]{:S(2)}) %copy-start.2) | copy-done | bytes 6168
  2.1 0.0 copy-start.3
  2.1 0.7 %copy-done.3 = f32[12,128]{1,0:T(8,128)S(1)} copy-done((f32[12,128]{1,0:T(8,128)S(1)}, f32[12,128]{1,0:T(8,128)}, u32[]{:S(2)}) %copy-start.3) | copy-done | bytes 6168
  2.8 0.7 %pack.1 = (f32[3,3,8,128]{3,2,1,0:T(8,128)S(1)}, f32[3,3,8,128]{3,2,1,0:T(8,128)S(1)}, f32[3,3,8,128]{3,2,1,0:T(8,128)S(1)}) custom-call(s32[12]{0:T(128)S(1)} %bitcast.3, f32[12,3,128]{2,1,0:T(4,128)S(1)} %copy-done.1, f32[12,128]{1,0:T(8,128)S(1)} %copy-done.2, f32[12,128]{1,0:T(8,128)S(1)} %copy-done.3), custom_call_target="tpu_custom_call" | custom-call | tf_op jit(solution)/shard_map/pack/pallas_call | solution.py:236
  3.5 3.1 %collective-permute-start = (f32[3,3,8,128]{3,2,1,0:T(8,128)S(1)}, f32[3,3,8,128]{3,2,1,0:T(8,128)S(1)}, u32[]{:S(2)}, u32[]{:S(2)}) collective-permute-start(f32[3,3,8,128]{3,2,1,0:T(8,128)S(1)} %get-tuple-element.20), channel_id=1, source_target_pairs={{0,1},{1,2},{2,3},{3,4},{4,5},{5,6},{6,7},{7,8},{8,9},{9,10},{10,1... | collective-permute-start | bytes 110600 | tf_op jit(solution)/shard_map/ppermute | solution.py:229
  6.6 2.8 %collective-permute-start.1 = (f32[3,3,8,128]{3,2,1,0:T(8,128)S(1)}, f32[3,3,8,128]{3,2,1,0:T(8,128)S(1)}, u32[]{:S(2)}, u32[]{:S(2)}) collective-permute-start(f32[3,3,8,128]{3,2,1,0:T(8,128)S(1)} %get-tuple-element.21), channel_id=1, source_target_pairs={{1,0},{2,1},{3,2},{4,3},{5,4},{6,5},{7,6},{8,7},{9,8},{10,9},{11,1... | collective-permute-start | bytes 110600 | tf_op jit(solution)/shard_map/ppermute | solution.py:229
  9.4 0.0 collective-permute-done
  9.4 5.1 %collective-permute-done.1 = f32[3,3,8,128]{3,2,1,0:T(8,128)S(1)} collective-permute-done((f32[3,3,8,128]{3,2,1,0:T(8,128)S(1)}, f32[3,3,8,128]{3,2,1,0:T(8,128)S(1)}, u32[]{:S(2)}, u32[]{:S(2)}) %collective-permute-start.1) | collective-permute-done | bytes 36896 | tf_op jit(solution)/shard_map/ppermute | solution.py:229
  14.5 2.0 %collective-permute-start.3 = (f32[2,9,8,128]{3,2,1,0:T(8,128)S(1)}, f32[2,9,8,128]{3,2,1,0:T(8,128)S(1)}, u32[]{:S(2)}, u32[]{:S(2)}) collective-permute-start(f32[2,9,8,128]{3,2,1,0:T(8,128)S(1)} %get-tuple-element.37), channel_id=1, source_target_pairs={{32,0},{48,16},{64,32},{80,48},{96,64},{112,80},{128,96},{144,112}... | collective-permute-start | bytes 221192 | tf_op jit(solution)/shard_map/ppermute | solution.py:229
  16.6 5.0 %collective-permute-start.2 = (f32[2,9,8,128]{3,2,1,0:T(8,128)S(1)}, f32[2,9,8,128]{3,2,1,0:T(8,128)S(1)}, u32[]{:S(2)}, u32[]{:S(2)}) collective-permute-start(f32[2,9,8,128]{3,2,1,0:T(8,128)S(1)} %get-tuple-element.38), channel_id=1, source_target_pairs={{0,32},{16,48},{32,64},{48,80},{64,96},{80,112},{96,128},{112,144}... | collective-permute-start | bytes 221192 | tf_op jit(solution)/shard_map/ppermute | solution.py:229
  21.6 5.4 %first.1 = (f32[192,1024]{1,0:T(8,128)S(1)}, f32[40,1024]{1,0:T(8,128)S(1)}, f32[40,1024]{1,0:T(8,128)S(1)}) custom-call(f32[3,9,8,128]{3,2,1,0:T(8,128)S(1)} %constant_dynamic-update-slice_fusion.own), custom_call_target="tpu_custom_call" | custom-call | flops 2400000000 | bytes 4000000 | tf_op jit(solution)/shard_map/first/pallas_call | solution.py:173
  27.0 0.0 collective-permute-done.3.below
  27.0 0.0 collective-permute-done.2.above
  27.1 0.0 copy-start
  27.1 2.1 %collective-permute-start.4 = (f32[4,9,8,128]{3,2,1,0:T(8,128)S(1)}, f32[4,9,8,128]{3,2,1,0:T(8,128)S(1)}, u32[]{:S(2)}, u32[]{:S(2)}) collective-permute-start(f32[4,9,8,128]{3,2,1,0:T(8,128)S(1)} %pad_maximum_fusion), channel_id=1, source_target_pairs={{0,16},{16,0},{32,48},{48,32},{64,80},{80,64},{96,112},{112,96},{1... | collective-permute-start | bytes 442376 | tf_op jit(solution)/shard_map/ppermute | solution.py:272
  29.1 1.3 %collective-permute-done.4.beside = f32[4,9,8,128]{3,2,1,0:T(8,128)S(1)} collective-permute-done((f32[4,9,8,128]{3,2,1,0:T(8,128)S(1)}, f32[4,9,8,128]{3,2,1,0:T(8,128)S(1)}, u32[]{:S(2)}, u32[]{:S(2)}) %collective-permute-start.4) | collective-permute-done | bytes 147488 | tf_op jit(solution)/shard_map/ppermute | solution.py:272
  30.5 9.7 %rest.1 = (f32[192,1024]{1,0:T(8,128)S(1)}, f32[40,1024]{1,0:T(8,128)S(1)}, f32[40,1024]{1,0:T(8,128)S(1)}) custom-call(f32[2,9,8,128]{3,2,1,0:T(8,128)S(1)} %collective-permute-done.2.above, f32[2,9,8,128]{3,2,1,0:T(8,128)S(1)} %collective-permute-done.3.below, f32[4,9,8,128]{3,2,1,0:T(8,128)S(1)} %collective-permute-done.4.beside, ...), custom_call_target="tpu_custom_call" | custom-call | flops 4800000000 | bytes 4000000 | tf_op jit(solution)/shard_map/rest/pallas_call | solution.py:173
  40.2 1.9 %collective-permute-start.5 = (f32[40,1024]{1,0:T(8,128)S(1)}, f32[40,1024]{1,0:T(8,128)S(1)}, u32[]{:S(2)}, u32[]{:S(2)}) collective-permute-start(f32[40,1024]{1,0:T(8,128)S(1)} %get-tuple-element.31), channel_id=1, source_target_pairs={{0,1},{1,2},{2,3},{3,4},{4,5},{5,6},{6,7},{7,8},{8,9},{9,10},{10,1... | collective-permute-start | bytes 491528 | tf_op jit(solution)/shard_map/ppermute | solution.py:229
  42.1 3.9 %collective-permute-start.6 = (f32[40,1024]{1,0:T(8,128)S(1)}, f32[40,1024]{1,0:T(8,128)S(1)}, u32[]{:S(2)}, u32[]{:S(2)}) collective-permute-start(f32[40,1024]{1,0:T(8,128)S(1)} %get-tuple-element.32), channel_id=1, source_target_pairs={{1,0},{2,1},{3,2},{4,3},{5,4},{6,5},{7,6},{8,7},{9,8},{10,9},{11,1... | collective-permute-start | bytes 491528 | tf_op jit(solution)/shard_map/ppermute | solution.py:229
  46.1 2.3 %collective-permute-done.5.from_left = f32[40,1024]{1,0:T(8,128)S(1)} collective-permute-done((f32[40,1024]{1,0:T(8,128)S(1)}, f32[40,1024]{1,0:T(8,128)S(1)}, u32[]{:S(2)}, u32[]{:S(2)}) %collective-permute-start.5) | collective-permute-done | bytes 163872 | tf_op jit(solution)/shard_map/ppermute | solution.py:229
  48.4 4.0 %collective-permute-done.6.from_right = f32[40,1024]{1,0:T(8,128)S(1)} collective-permute-done((f32[40,1024]{1,0:T(8,128)S(1)}, f32[40,1024]{1,0:T(8,128)S(1)}, u32[]{:S(2)}, u32[]{:S(2)}) %collective-permute-start.6) | collective-permute-done | bytes 163872 | tf_op jit(solution)/shard_map/ppermute | solution.py:229
  52.4 0.0 copy-done
  52.4 1.1 %edges.1 = f32[8,24,1024]{2,1,0:T(8,128)} custom-call(f32[8,24,1024]{2,1,0:T(8,128)S(1)} %bitcast.2, f32[8,24,1024]{2,1,0:T(8,128)S(1)} %copy-done, f32[40,1024]{1,0:T(8,128)S(1)} %collective-permute-done.5.from_left, f32[40,1024]{1,0:T(8,128)S(1)} %collective-permute-done.6.from_right), custom_call_target="tpu_custom_call" | custom-call | tf_op jit(solution)/shard_map/edges/pallas_call | solution.py:276
  (6 shorter events, 0.1 us)
Async XLA Ops:
  0.0 0.7 %copy-start.4 = (s32[12,1]{0,1:T(1,128)S(1)}, s32[12,1]{0,1:T(1,128)}, u32[]{:S(2)}) copy-start(s32[12,1]{0,1:T(1,128)} %param.8) | copy-start | bytes 148
  0.7 0.7 %copy-start.1 = (f32[12,3,128]{2,1,0:T(4,128)S(1)}, f32[12,3,128]{2,1,0:T(4,128)}, u32[]{:S(2)}) copy-start(f32[12,3,128]{2,1,0:T(4,128)} %refs_1_.1) | copy-start | bytes 55300
  1.4 0.7 %copy-start.2 = (f32[12,128]{1,0:T(8,128)S(1)}, f32[12,128]{1,0:T(8,128)}, u32[]{:S(2)}) copy-start(f32[12,128]{1,0:T(8,128)} %refs_2_.1) | copy-start | bytes 18436
  2.1 0.7 %copy-start.3 = (f32[12,128]{1,0:T(8,128)S(1)}, f32[12,128]{1,0:T(8,128)}, u32[]{:S(2)}) copy-start(f32[12,128]{1,0:T(8,128)} %refs_3_.1) | copy-start | bytes 18436
  3.5 5.9 %collective-permute-start = (f32[3,3,8,128]{3,2,1,0:T(8,128)S(1)}, f32[3,3,8,128]{3,2,1,0:T(8,128)S(1)}, u32[]{:S(2)}, u32[]{:S(2)}) collective-permute-start(f32[3,3,8,128]{3,2,1,0:T(8,128)S(1)} %get-tuple-element.20), channel_id=1, source_target_pairs={{0,1},{1,2},{2,3},{3,4},{4,5},{5,6},{6,7},{7,8},{8,9},{9,10},{10,1... | collective-permute-start | bytes 110600 | tf_op jit(solution)/shard_map/ppermute | solution.py:229
  6.6 8.0 %collective-permute-start.1 = (f32[3,3,8,128]{3,2,1,0:T(8,128)S(1)}, f32[3,3,8,128]{3,2,1,0:T(8,128)S(1)}, u32[]{:S(2)}, u32[]{:S(2)}) collective-permute-start(f32[3,3,8,128]{3,2,1,0:T(8,128)S(1)} %get-tuple-element.21), channel_id=1, source_target_pairs={{1,0},{2,1},{3,2},{4,3},{5,4},{6,5},{7,6},{8,7},{9,8},{10,9},{11,1... | collective-permute-start | bytes 110600 | tf_op jit(solution)/shard_map/ppermute | solution.py:229
  14.5 12.5 %collective-permute-start.3 = (f32[2,9,8,128]{3,2,1,0:T(8,128)S(1)}, f32[2,9,8,128]{3,2,1,0:T(8,128)S(1)}, u32[]{:S(2)}, u32[]{:S(2)}) collective-permute-start(f32[2,9,8,128]{3,2,1,0:T(8,128)S(1)} %get-tuple-element.37), channel_id=1, source_target_pairs={{32,0},{48,16},{64,32},{80,48},{96,64},{112,80},{128,96},{144,112}... | collective-permute-start | bytes 221192 | tf_op jit(solution)/shard_map/ppermute | solution.py:229
  16.6 10.5 %collective-permute-start.2 = (f32[2,9,8,128]{3,2,1,0:T(8,128)S(1)}, f32[2,9,8,128]{3,2,1,0:T(8,128)S(1)}, u32[]{:S(2)}, u32[]{:S(2)}) collective-permute-start(f32[2,9,8,128]{3,2,1,0:T(8,128)S(1)} %get-tuple-element.38), channel_id=1, source_target_pairs={{0,32},{16,48},{32,64},{48,80},{64,96},{80,112},{96,128},{112,144}... | collective-permute-start | bytes 221192 | tf_op jit(solution)/shard_map/ppermute | solution.py:229
  27.1 25.3 %copy-start = (f32[8,24,1024]{2,1,0:T(8,128)S(1)}, f32[8,24,1024]{2,1,0:T(8,128)}, u32[]{:S(2)}) copy-start(f32[8,24,1024]{2,1,0:T(8,128)} %old.1) | copy-start | bytes 2359300
  27.1 3.4 %collective-permute-start.4 = (f32[4,9,8,128]{3,2,1,0:T(8,128)S(1)}, f32[4,9,8,128]{3,2,1,0:T(8,128)S(1)}, u32[]{:S(2)}, u32[]{:S(2)}) collective-permute-start(f32[4,9,8,128]{3,2,1,0:T(8,128)S(1)} %pad_maximum_fusion), channel_id=1, source_target_pairs={{0,16},{16,0},{32,48},{48,32},{64,80},{80,64},{96,112},{112,96},{1... | collective-permute-start | bytes 442376 | tf_op jit(solution)/shard_map/ppermute | solution.py:272
  40.2 8.2 %collective-permute-start.5 = (f32[40,1024]{1,0:T(8,128)S(1)}, f32[40,1024]{1,0:T(8,128)S(1)}, u32[]{:S(2)}, u32[]{:S(2)}) collective-permute-start(f32[40,1024]{1,0:T(8,128)S(1)} %get-tuple-element.31), channel_id=1, source_target_pairs={{0,1},{1,2},{2,3},{3,4},{4,5},{5,6},{6,7},{7,8},{8,9},{9,10},{10,1... | collective-permute-start | bytes 491528 | tf_op jit(solution)/shard_map/ppermute | solution.py:229
  42.1 10.3 %collective-permute-start.6 = (f32[40,1024]{1,0:T(8,128)S(1)}, f32[40,1024]{1,0:T(8,128)S(1)}, u32[]{:S(2)}, u32[]{:S(2)}) collective-permute-start(f32[40,1024]{1,0:T(8,128)S(1)} %get-tuple-element.32), channel_id=1, source_target_pairs={{1,0},{2,1},{3,2},{4,3},{5,4},{6,5},{7,6},{8,7},{9,8},{10,9},{11,1... | collective-permute-start | bytes 491528 | tf_op jit(solution)/shard_map/ppermute | solution.py:229

commit v4 on v3

--- a/solution.py
+++ b/solution.py
@@ -51,10 +51,10 @@
     count = jnp.int32(0)
     for ref, part in sources:
         bits = jnp.zeros((1, 128), f32)
-        for s in range(9):
+        for s in range(ref.shape[1]):
             bits = bits + ref[part, s, 5:6, :] * float(1 << s)
         mask = jnp.max(bits).astype(jnp.int32)
-        for s in range(9):
+        for s in range(ref.shape[1]):
             lists[group, count] = ref[part, s]
             count = count + (lax.shift_right_logical(mask, s) & 1)
     for s in range(blocks - 1):
@@ -138,30 +138,16 @@
 BLOCKS, WIDE = 4, 256
 
 
-def first_kernel(own, core, left, right, lists, ti, tj):
+def field_kernel(sources, begun, *refs):
+    core, left, right, lists, ti, tj = refs[-6:]
+    inputs = refs[:-6]
     depth = core.shape[1]
     rows, starts = prepare(ti, tj, (True, False))
-    for ref in (core, left, right):
-        ref[...] = jnp.zeros_like(ref)
-    counts = [compact(lists, g, ((own, g),), BLOCKS) for g in range(3)]
-    add_field(lists, counts, ti, tj, rows, starts, both_adds(core, left, right), depth, BLOCKS, WIDE)
-
-
-def others(above, below, beside):
-    return (
-        ((above, 1), (beside, 0)),
-        ((beside, 1), (beside, 2)),
-        ((below, 0), (beside, 3)),
-    )
-
-
-def rest_kernel(above, below, beside, core0, left0, right0, core, left, right, lists, ti, tj):
-    depth = core.shape[1]
-    rows, starts = prepare(ti, tj, (True, False))
-    core[...] = core0[...]
-    left[...] = left0[...]
-    right[...] = right0[...]
-    counts = [compact(lists, g, s, BLOCKS) for g, s in enumerate(others(above, below, beside))]
+    for n, ref in enumerate((core, left, right)):
+        ref[...] = inputs[len(inputs) - 3 + n][...] if begun else jnp.zeros_like(ref)
+    counts = [
+        compact(lists, g, [(inputs[n], part) for n, part in sources[g]], BLOCKS) for g in range(3)
+    ]
     add_field(lists, counts, ti, tj, rows, starts, both_adds(core, left, right), depth, BLOCKS, WIDE)
 
 
@@ -169,20 +155,23 @@
 HBM = pl.BlockSpec(memory_space=pltpu.HBM)
 
 
-def call(kernel, name, outs, rows, capacity, cost, *operands):
+def field(name, depth, blocks, sources, arrays, begun=()):
+    operands = (*arrays, *begun)
+    shapes = ((192, depth), (40, depth), (40, depth))
+    rows = sum(CORE_ROWS) + sum(EDGE_ROWS)
     return pl.pallas_call(
-        kernel,
-        out_shape=[jax.ShapeDtypeStruct(s, f32) for s in outs],
+        functools.partial(field_kernel, sources, bool(begun)),
+        out_shape=[jax.ShapeDtypeStruct(s, f32) for s in shapes],
         in_specs=[VM] * len(operands),
-        out_specs=[VM] * len(outs),
+        out_specs=[VM] * 3,
         scratch_shapes=[
-            pltpu.VMEM((3, capacity, 8, 128), f32),
+            pltpu.VMEM((3, 27 + 2 * BLOCKS, 8, 128), f32),
             pltpu.VMEM((rows, 128), f32),
             pltpu.VMEM((rows, 128), f32),
         ],
         compiler_params=pltpu.CompilerParams(vmem_limit_bytes=32 * 1024 * 1024),
         cost_estimate=pl.CostEstimate(
-            flops=int(cost * 2e8), bytes_accessed=4_000_000, transcendentals=int(cost * 300_000)
+            flops=blocks * 200_000_000, bytes_accessed=4_000_000, transcendentals=blocks * 300_000
         ),
         name=name,
     )(*operands)
@@ -247,30 +236,45 @@
             pltpu.SMEM((9,), jnp.int32),
             pltpu.SemaphoreType.DMA((4,)),
         ],
-        compiler_params=small,
+        compiler_params=pltpu.CompilerParams(vmem_limit_bytes=60 * 1024 * 1024),
         name="pack",
     )(heading[:, 0], offsets, widths, solvation)
-    own = jnp.concatenate(
-        [same, passed_along(plus, "gy", 1), passed_along(minus, "gy", -1)], axis=1
-    )
-    above = passed_along(own[1:3], "gx", 2)
-    below = passed_along(own[0:2], "gx", -2)
-    plane, edge = (old_map.shape[0] * old_map.shape[1], depth), (40, depth)
-    outs = [plane, edge, edge]
-    part = call(first_kernel, "first", outs, 656, 36, 12, own)
-    above, below, *part = lax.optimization_barrier((above, below, *part))
-    first = lax.rem(lax.axis_index("gx"), 2) == 0
-    handed = jnp.stack(
+    left_in, right_in = passed_along(plus, "gy", 1), passed_along(minus, "gy", -1)
+    begun = field("stored", depth, 4, [[(0, 0)], [(0, 1)], [(0, 2)]], [same])
+    left_in, right_in, *begun = lax.optimization_barrier((left_in, right_in, *begun))
+    own = jnp.concatenate([same, left_in, right_in], axis=1)
+    count = lax.axis_size("gx")
+    partner = lax.ppermute(own, "gx", [(r, r + 1 - 2 * (r % 2)) for r in range(count)])
+    even = lax.rem(lax.axis_index("gx"), 2) == 0
+    none = jnp.zeros_like(own[0])
+    far = jnp.where(
+        even,
+        jnp.stack([own[2], partner[1], partner[2]]),
+        jnp.stack([own[0], partner[1], partner[0]]),
+    )
+    near = jnp.where(even, own[0:1], own[2:3])
+    ahead = [(r, r + 2 - 4 * (r % 2)) for r in range(count)]
+    behind = [(r, r - 2 + 4 * (r % 2)) for r in range(count)]
+    far = lax.ppermute(far, "gx", [p for p in ahead if 0 <= p[1] < count])
+    near = lax.ppermute(near, "gx", [p for p in behind if 0 <= p[1] < count])
+    beside = jnp.stack(
         [
-            jnp.where(first, own[1], above[0]),
-            jnp.where(first, own[2], own[0]),
-            jnp.where(first, below[0], above[1]),
-            jnp.where(first, below[1], own[1]),
+            jnp.where(even, none, partner[1]),
+            jnp.where(even, partner[0], partner[2]),
+            jnp.where(even, partner[1], none),
         ]
     )
-    pairs = [(r, r + 1 - 2 * (r % 2)) for r in range(lax.axis_size("gx"))]
-    beside = lax.ppermute(handed, "gx", pairs)
-    core, left, right = call(rest_kernel, "rest", outs, 656, 36, 24, above, below, beside, *part)
+    begun = field(
+        "chip", depth, 16, [[(0, g), (1, g), (2, g)] for g in range(3)],
+        [left_in, right_in, beside], begun,
+    )
+    far, near, *begun = lax.optimization_barrier((far, near, *begun))
+    one = jnp.concatenate([near, jnp.zeros_like(near)])
+    above, below = jnp.where(even, far[0:2], one), jnp.where(even, one, far[0:2])
+    core, left, right = field(
+        "rest", depth, 16, [[(0, 0), (0, 1)], [(2, 2)], [(1, 0), (1, 1)]],
+        [above, below, far], begun,
+    )
     from_left = passed_along(right, "gy", 1)
     from_right = passed_along(left, "gy", -1)
     return pl.pallas_call(

time: 53.9 us -> 50.6 us (0.939)
  the two profiles are of different devices: /device:TPU:248 before, /device:TPU:122 now
where the time goes in v4:
time: 50.6 us; the launch traced here: 50.2 us
  starting transfers between devices  20.7 us (41%)
  Pallas kernels  19.1 us (38%)
  waiting for transfers between devices  9.29 us (18%)
  local copies, waits for them, and re-layouts  0.86 us (2%)
    pallas_call x3, Pallas kernels, field(): pl.pallas_call(functools.partial(field_kernel, sources, bool(begun)), out...  16.6 us
    ppermute x4, starting transfers between devices, passed_along(): lax.ppermute(value, axis, [(source, source + steps) for source in range(f...  11.7 us
    ppermute x4, waiting for transfers between devices, passed_along(): lax.ppermute(value, axis, [(source, source + steps) for source in range(f...  9.29 us
    ppermute x1, starting transfers between devices, body(): far = lax.ppermute(far, 'gx', [p for p in ahead if 0 <= p[1] < count])  5.04 us
    ppermute x1, starting transfers between devices, body(): near = lax.ppermute(near, 'gx', [p for p in behind if 0 <= p[1] < count])  2.01 us
    ppermute x1, starting transfers between devices, body(): lax.ppermute(own, 'gx', [(r, r + 1 - 2 * (r % 2)) for r in range(count)])  1.92 us
    pallas_call x1, Pallas kernels, body(): pl.pallas_call(pack_kernel, out_shape=[third] * 3, in_specs=[HBM] * 4, ou...  1.51 us
    pallas_call x1, Pallas kernels, body(): pl.pallas_call(edge_kernel, out_shape=jax.ShapeDtypeStruct(old_map.shape,...  1.06 us
  transfers between devices with their start and end apart: 7, of which 3 were waited for; matrix products, arithmetic and copies ran while one was open for 2% of the time, Pallas kernels for 20%

profile of v4, /device:TPU:122, one launch (start us, length us, event | category | flops | bytes accessed | tf_op | source)
XLA Modules:
  0.0 50.2 jit_solution(16286809800004380863)
XLA Ops:
  0.0 1.5 %pack.1 = (f32[3,3,8,128]{3,2,1,0:T(8,128)}, f32[3,3,8,128]{3,2,1,0:T(8,128)}, f32[3,3,8,128]{3,2,1,0:T(8,128)}) custom-call(s32[12]{0:T(128)} %bitcast.3, f32[12,3,128]{2,1,0:T(4,128)} %refs_1_.1, f32[12,128]{1,0:T(8,128)} %refs_2_.1, f32[12,128]{1,0:T(8,128)} %refs_3_.1), custom_call_target="tpu_custom_call" | custom-call | tf_op jit(solution)/shard_map/pack/pallas_call | solution.py:225
  1.5 3.1 %collective-permute-start = (f32[3,3,8,128]{3,2,1,0:T(8,128)}, f32[3,3,8,128]{3,2,1,0:T(8,128)S(1)}, u32[]{:S(2)}, u32[]{:S(2)}) collective-permute-start(f32[3,3,8,128]{3,2,1,0:T(8,128)} %get-tuple-element.28), channel_id=1, source_target_pairs={{0,1},{1,2},{2,3},{3,4},{4,5},{5,6},{6,7},{7,8},{8,9},{9,10},{10,1... | collective-permute-start | bytes 110600 | tf_op jit(solution)/shard_map/ppermute | solution.py:218
  4.6 2.8 %collective-permute-start.1 = (f32[3,3,8,128]{3,2,1,0:T(8,128)}, f32[3,3,8,128]{3,2,1,0:T(8,128)S(1)}, u32[]{:S(2)}, u32[]{:S(2)}) collective-permute-start(f32[3,3,8,128]{3,2,1,0:T(8,128)} %get-tuple-element.29), channel_id=1, source_target_pairs={{1,0},{2,1},{3,2},{4,3},{5,4},{6,5},{7,6},{8,7},{9,8},{10,9},{11,1... | collective-permute-start | bytes 110600 | tf_op jit(solution)/shard_map/ppermute | solution.py:218
  7.4 0.0 copy-start.1
  7.4 0.8 %constant_dynamic-update-slice_fusion.2 = f32[3,9,8,128]{3,2,1,0:T(8,128)S(1)} fusion(f32[3,3,8,128]{3,2,1,0:T(8,128)} %get-tuple-element.27.refs_0_), kind=kLoop, calls=%fused_computation.10 | loop fusion | bytes 73728
  8.2 0.0 copy-done.1
  8.2 3.0 %stored.1 = (f32[192,1024]{1,0:T(8,128)S(1)}, f32[40,1024]{1,0:T(8,128)S(1)}, f32[40,1024]{1,0:T(8,128)S(1)}) custom-call(f32[3,3,8,128]{3,2,1,0:T(8,128)S(1)} %copy-done.1), custom_call_target="tpu_custom_call" | custom-call | flops 800000000 | bytes 4000000 | tf_op jit(solution)/shard_map/stored/pallas_call | solution.py:162
  11.2 0.0 collective-permute-done.refs_0_
  11.2 1.6 %collective-permute-done.1.refs_1_ = f32[3,3,8,128]{3,2,1,0:T(8,128)S(1)} collective-permute-done((f32[3,3,8,128]{3,2,1,0:T(8,128)}, f32[3,3,8,128]{3,2,1,0:T(8,128)S(1)}, u32[]{:S(2)}, u32[]{:S(2)}) %collective-permute-start.1) | collective-permute-done | bytes 36896 | tf_op jit(solution)/shard_map/ppermute | solution.py:218
  12.8 1.9 %collective-permute-start.2 = (f32[3,9,8,128]{3,2,1,0:T(8,128)S(1)}, f32[3,9,8,128]{3,2,1,0:T(8,128)S(1)}, u32[]{:S(2)}, u32[]{:S(2)}) collective-permute-start(f32[3,9,8,128]{3,2,1,0:T(8,128)S(1)} %constant_dynamic-update-slice_fusion), channel_id=1, source_target_pairs={{0,16},{16,0},{32,48},{48,32},{64,80},{80,64},{96,112},{112,96},{1... | collective-permute-start | bytes 331784 | tf_op jit(solution)/shard_map/ppermute | solution.py:247
  14.7 2.0 %collective-permute-start.4 = (f32[1,9,8,128]{3,2,1,0:T(8,128)S(1)}, f32[1,9,8,128]{3,2,1,0:T(8,128)S(1)}, u32[]{:S(2)}, u32[]{:S(2)}) collective-permute-start(f32[1,9,8,128]{3,2,1,0:T(8,128)S(1)} %get-tuple-element.56), channel_id=1, source_target_pairs={{16,48},{32,0},{48,80},{64,32},{80,112},{96,64},{112,144},{128,96}... | collective-permute-start | bytes 110600 | tf_op jit(solution)/shard_map/ppermute | solution.py:259
  16.7 0.0 collective-permute-done.2
  16.8 5.0 %collective-permute-start.3 = (f32[3,9,8,128]{3,2,1,0:T(8,128)S(1)}, f32[3,9,8,128]{3,2,1,0:T(8,128)S(1)}, u32[]{:S(2)}, u32[]{:S(2)}) collective-permute-start(f32[3,9,8,128]{3,2,1,0:T(8,128)S(1)} %maximum_select_fusion), channel_id=1, source_target_pairs={{0,32},{32,64},{48,16},{64,96},{80,48},{96,128},{112,80},{128,160}... | collective-permute-start | bytes 331784 | tf_op jit(solution)/shard_map/ppermute | solution.py:258
  21.9 6.9 %chip.1 = (f32[192,1024]{1,0:T(8,128)S(1)}, f32[40,1024]{1,0:T(8,128)S(1)}, f32[40,1024]{1,0:T(8,128)S(1)}) custom-call(f32[3,3,8,128]{3,2,1,0:T(8,128)S(1)} %collective-permute-done.refs_0_, f32[3,3,8,128]{3,2,1,0:T(8,128)S(1)} %collective-permute-done.1.refs_1_, f32[3,9,8,128]{3,2,1,0:T(8,128)S(1)} %pad_maximum_fusion.refs_2_, ...), custom_call_target="tpu_custom_call" | custom-call | flops 3200000000 | bytes 4000000 | tf_op jit(solution)/shard_map/chip/pallas_call | solution.py:162
  28.7 0.0 collective-permute-done.4
  28.8 0.0 collective-permute-done.3.refs_2_
  28.8 0.0 copy-start
  28.8 6.8 %rest.1 = (f32[192,1024]{1,0:T(8,128)S(1)}, f32[40,1024]{1,0:T(8,128)S(1)}, f32[40,1024]{1,0:T(8,128)S(1)}) custom-call(f32[2,9,8,128]{3,2,1,0:T(8,128)S(1)} %get-tuple-element.50.refs_0_, f32[2,9,8,128]{3,2,1,0:T(8,128)S(1)} %get-tuple-element.49.refs_1_, f32[3,9,8,128]{3,2,1,0:T(8,128)S(1)} %collective-permute-done.3.refs_2_, ...), custom_call_target="tpu_custom_call" | custom-call | flops 3200000000 | bytes 4000000 | tf_op jit(solution)/shard_map/rest/pallas_call | solution.py:162
  35.6 3.6 %collective-permute-start.5 = (f32[40,1024]{1,0:T(8,128)S(1)}, f32[40,1024]{1,0:T(8,128)S(1)}, u32[]{:S(2)}, u32[]{:S(2)}) collective-permute-start(f32[40,1024]{1,0:T(8,128)S(1)} %get-tuple-element.47), channel_id=1, source_target_pairs={{0,1},{1,2},{2,3},{3,4},{4,5},{5,6},{6,7},{7,8},{8,9},{9,10},{10,1... | collective-permute-start | bytes 491528 | tf_op jit(solution)/shard_map/ppermute | solution.py:218
  39.2 2.2 %collective-permute-start.6 = (f32[40,1024]{1,0:T(8,128)S(1)}, f32[40,1024]{1,0:T(8,128)S(1)}, u32[]{:S(2)}, u32[]{:S(2)}) collective-permute-start(f32[40,1024]{1,0:T(8,128)S(1)} %get-tuple-element.48), channel_id=1, source_target_pairs={{1,0},{2,1},{3,2},{4,3},{5,4},{6,5},{7,6},{8,7},{9,8},{10,9},{11,1... | collective-permute-start | bytes 491528 | tf_op jit(solution)/shard_map/ppermute | solution.py:218
  41.4 2.2 %collective-permute-done.5.from_left = f32[40,1024]{1,0:T(8,128)S(1)} collective-permute-done((f32[40,1024]{1,0:T(8,128)S(1)}, f32[40,1024]{1,0:T(8,128)S(1)}, u32[]{:S(2)}, u32[]{:S(2)}) %collective-permute-start.5) | collective-permute-done | bytes 163872 | tf_op jit(solution)/shard_map/ppermute | solution.py:218
  43.7 5.5 %collective-permute-done.6.from_right = f32[40,1024]{1,0:T(8,128)S(1)} collective-permute-done((f32[40,1024]{1,0:T(8,128)S(1)}, f32[40,1024]{1,0:T(8,128)S(1)}, u32[]{:S(2)}, u32[]{:S(2)}) %collective-permute-start.6) | collective-permute-done | bytes 163872 | tf_op jit(solution)/shard_map/ppermute | solution.py:218
  49.2 0.0 copy-done
  49.2 1.1 %edges.1 = f32[8,24,1024]{2,1,0:T(8,128)} custom-call(f32[8,24,1024]{2,1,0:T(8,128)S(1)} %bitcast.2, f32[8,24,1024]{2,1,0:T(8,128)S(1)} %copy-done, f32[40,1024]{1,0:T(8,128)S(1)} %collective-permute-done.5.from_left, f32[40,1024]{1,0:T(8,128)S(1)} %collective-permute-done.6.from_right), custom_call_target="tpu_custom_call" | custom-call | tf_op jit(solution)/shard_map/edges/pallas_call | solution.py:280
  (8 shorter events, 0.1 us)
Async XLA Ops:
  1.5 9.7 %collective-permute-start = (f32[3,3,8,128]{3,2,1,0:T(8,128)}, f32[3,3,8,128]{3,2,1,0:T(8,128)S(1)}, u32[]{:S(2)}, u32[]{:S(2)}) collective-permute-start(f32[3,3,8,128]{3,2,1,0:T(8,128)} %get-tuple-element.28), channel_id=1, source_target_pairs={{0,1},{1,2},{2,3},{3,4},{4,5},{5,6},{6,7},{7,8},{8,9},{9,10},{10,1... | collective-permute-start | bytes 110600 | tf_op jit(solution)/shard_map/ppermute | solution.py:218
  4.6 8.2 %collective-permute-start.1 = (f32[3,3,8,128]{3,2,1,0:T(8,128)}, f32[3,3,8,128]{3,2,1,0:T(8,128)S(1)}, u32[]{:S(2)}, u32[]{:S(2)}) collective-permute-start(f32[3,3,8,128]{3,2,1,0:T(8,128)} %get-tuple-element.29), channel_id=1, source_target_pairs={{1,0},{2,1},{3,2},{4,3},{5,4},{6,5},{7,6},{8,7},{9,8},{10,9},{11,1... | collective-permute-start | bytes 110600 | tf_op jit(solution)/shard_map/ppermute | solution.py:218
  7.4 0.8 %copy-start.1 = (f32[3,3,8,128]{3,2,1,0:T(8,128)S(1)}, f32[3,3,8,128]{3,2,1,0:T(8,128)}, u32[]{:S(2)}) copy-start(f32[3,3,8,128]{3,2,1,0:T(8,128)} %get-tuple-element.27.refs_0_) | copy-start | bytes 110596
  12.8 4.0 %collective-permute-start.2 = (f32[3,9,8,128]{3,2,1,0:T(8,128)S(1)}, f32[3,9,8,128]{3,2,1,0:T(8,128)S(1)}, u32[]{:S(2)}, u32[]{:S(2)}) collective-permute-start(f32[3,9,8,128]{3,2,1,0:T(8,128)S(1)} %constant_dynamic-update-slice_fusion), channel_id=1, source_target_pairs={{0,16},{16,0},{32,48},{48,32},{64,80},{80,64},{96,112},{112,96},{1... | collective-permute-start | bytes 331784 | tf_op jit(solution)/shard_map/ppermute | solution.py:247
  14.7 14.0 %collective-permute-start.4 = (f32[1,9,8,128]{3,2,1,0:T(8,128)S(1)}, f32[1,9,8,128]{3,2,1,0:T(8,128)S(1)}, u32[]{:S(2)}, u32[]{:S(2)}) collective-permute-start(f32[1,9,8,128]{3,2,1,0:T(8,128)S(1)} %get-tuple-element.56), channel_id=1, source_target_pairs={{16,48},{32,0},{48,80},{64,32},{80,112},{96,64},{112,144},{128,96}... | collective-permute-start | bytes 110600 | tf_op jit(solution)/shard_map/ppermute | solution.py:259
  16.8 11.9 %collective-permute-start.3 = (f32[3,9,8,128]{3,2,1,0:T(8,128)S(1)}, f32[3,9,8,128]{3,2,1,0:T(8,128)S(1)}, u32[]{:S(2)}, u32[]{:S(2)}) collective-permute-start(f32[3,9,8,128]{3,2,1,0:T(8,128)S(1)} %maximum_select_fusion), channel_id=1, source_target_pairs={{0,32},{32,64},{48,16},{64,96},{80,48},{96,128},{112,80},{128,160}... | collective-permute-start | bytes 331784 | tf_op jit(solution)/shard_map/ppermute | solution.py:258
  28.8 20.4 %copy-start = (f32[8,24,1024]{2,1,0:T(8,128)S(1)}, f32[8,24,1024]{2,1,0:T(8,128)}, u32[]{:S(2)}) copy-start(f32[8,24,1024]{2,1,0:T(8,128)} %old.1) | copy-start | bytes 2359300
  35.6 8.1 %collective-permute-start.5 = (f32[40,1024]{1,0:T(8,128)S(1)}, f32[40,1024]{1,0:T(8,128)S(1)}, u32[]{:S(2)}, u32[]{:S(2)}) collective-permute-start(f32[40,1024]{1,0:T(8,128)S(1)} %get-tuple-element.47), channel_id=1, source_target_pairs={{0,1},{1,2},{2,3},{3,4},{4,5},{5,6},{6,7},{7,8},{8,9},{9,10},{10,1... | collective-permute-start | bytes 491528 | tf_op jit(solution)/shard_map/ppermute | solution.py:218
  39.2 9.9 %collective-permute-start.6 = (f32[40,1024]{1,0:T(8,128)S(1)}, f32[40,1024]{1,0:T(8,128)S(1)}, u32[]{:S(2)}, u32[]{:S(2)}) collective-permute-start(f32[40,1024]{1,0:T(8,128)S(1)} %get-tuple-element.48), channel_id=1, source_target_pairs={{1,0},{2,1},{3,2},{4,3},{5,4},{6,5},{7,6},{8,7},{9,8},{10,9},{11,1... | collective-permute-start | bytes 491528 | tf_op jit(solution)/shard_map/ppermute | solution.py:218

commit v5 on v4

--- a/solution.py
+++ b/solution.py
@@ -45,21 +45,24 @@
     return h, (v - h.astype(f32)).astype(bf16)
 
 
-def compact(lists, group, sources, blocks):
+def compact(place, sources, shift, count):
     row = lax.broadcasted_iota(jnp.int32, (8, 128), 0)
-    dead = jnp.where(row == 3, 1.0, 0.0).astype(f32)
-    count = jnp.int32(0)
     for ref, part in sources:
         bits = jnp.zeros((1, 128), f32)
         for s in range(ref.shape[1]):
             bits = bits + ref[part, s, 5:6, :] * float(1 << s)
         mask = jnp.max(bits).astype(jnp.int32)
         for s in range(ref.shape[1]):
-            lists[group, count] = ref[part, s]
+            place[count] = jnp.where(row == 6, shift, ref[part, s])
             count = count + (lax.shift_right_logical(mask, s) & 1)
+    return count
+
+
+def fill_up(place, count, blocks):
+    row = lax.broadcasted_iota(jnp.int32, (8, 128), 0)
+    dead = jnp.where(row == 3, 1.0, 0.0).astype(f32)
     for s in range(blocks - 1):
-        lists[group, count + s] = dead
-    return count
+        place[count + s] = dead
 
 
 def add_field(lists, counts, ti, tj, rows, starts, adds, depth, blocks, wide):
@@ -138,34 +141,101 @@
 BLOCKS, WIDE = 4, 256
 
 
-def field_kernel(sources, begun, *refs):
-    core, left, right, lists, ti, tj = refs[-6:]
-    inputs = refs[:-6]
-    depth = core.shape[1]
-    rows, starts = prepare(ti, tj, (True, False))
-    for n, ref in enumerate((core, left, right)):
-        ref[...] = inputs[len(inputs) - 3 + n][...] if begun else jnp.zeros_like(ref)
-    counts = [
-        compact(lists, g, [(inputs[n], part) for n, part in sources[g]], BLOCKS) for g in range(3)
-    ]
-    add_field(lists, counts, ti, tj, rows, starts, both_adds(core, left, right), depth, BLOCKS, WIDE)
+def field_kernel(sources, begun, outs, *refs):
+    lists, ti, tj = refs[-3:]
+    totals, inputs = refs[-3 - outs:-3], refs[:-3 - outs]
+    depth = totals[0].shape[1]
+    rows, starts = prepare(ti, tj, (True, False)[: max(1, outs - 1)])
+    for n, ref in enumerate(totals):
+        ref[...] = inputs[len(inputs) - outs + n][...] if begun else jnp.zeros_like(ref)
+    counts = []
+    for g in range(3):
+        segments = [(inputs[n], part) for n, part in sources[g]]
+        counts.append(compact(lists.at[g], segments, 0.0, jnp.int32(0)))
+        fill_up(lists.at[g], counts[g], BLOCKS)
+    adds = both_adds(*totals) if outs == 3 else core_adds(*totals)
+    add_field(lists, counts, ti, tj, rows, starts, adds, depth, BLOCKS, WIDE)
+
+
+def edge_field_kernel(sources, *refs):
+    left, right, lists, ti, tj = refs[-5:]
+    inputs = refs[:-5]
+    depth = left.shape[1]
+    put_rows(ti, tj, 0, OWN, False)
+    left[...] = inputs[-2][...]
+    right[...] = inputs[-1][...]
+    count = jnp.int32(0)
+    for g in range(3):
+        segments = [(inputs[n], part) for n, part in sources[g]]
+        count = compact(lists, segments, (-8.0, 0.0, 8.0)[g], count)
+    fill_up(lists, count, 8)
+    k_io = lax.broadcasted_iota(jnp.int32, (1, WIDE), 1).astype(f32)
+    dot = functools.partial(jnp.dot, preferred_element_type=f32)
+
+    def stage(at, blocks):
+        recs = [lists[at + q] for q in range(blocks)]
+        rec = jnp.concatenate(recs, axis=1)
+        x, y, weight = rec[0:1] * 8.0, rec[1:2] * 24.0, rec[4:5]
+        c = (-0.5 * LOG2E) / (rec[3:4] * rec[3:4])
+        i = jnp.concatenate([ti[...]] * blocks, axis=1) - rec[6:7]
+        dx = i - x
+        dy = jnp.concatenate([tj[...]] * blocks, axis=1) - y
+        value = jnp.exp2((dx * dx + dy * dy) * c) * weight
+        ph, plo = split(jnp.where(jnp.abs(i - 3.5) < 4.0 + W, value, 0.0))
+        cols = jnp.concatenate([jnp.transpose(r) for r in recs], axis=0)
+        z = cols[:, 2:3] * 1024.0
+        cz = (-0.5 * LOG2E) / (cols[:, 3:4] * cols[:, 3:4])
+
+        def along(b):
+            d = k_io - (z - float(b * WIDE))
+            return split(jnp.exp2(d * (d * cz)))
+
+        nxt = along(0)
+        for b in range(depth // WIDE):
+            zh, zl = nxt
+            if b + 1 < depth // WIDE:
+                nxt = along(b + 1)
+            pp = dot(jnp.concatenate([ph, plo], 0), zh)
+            r = pp[:80] + pp[80:] + dot(ph, zl)
+            left[:, b * WIDE:(b + 1) * WIDE] += r[0:40]
+            right[:, b * WIDE:(b + 1) * WIDE] += r[40:80]
+
+    def step(t, carry):
+        stage(t * 8, 8)
+        return carry
+
+    whole = lax.shift_right_logical(count + 1, 3)
+    lax.fori_loop(0, whole, step, 0)
+    after = count - whole * 8
+
+    @pl.when(after > 2)
+    def _():
+        stage(whole * 8, 4)
+
+    @pl.when(((after > 0) & (after <= 2)) | (after > 4))
+    def _():
+        stage(whole * 8 + jnp.where(after > 2, 4, 0), 2)
 
 
 VM = pl.BlockSpec(memory_space=pltpu.VMEM)
 HBM = pl.BlockSpec(memory_space=pltpu.HBM)
 
 
-def field(name, depth, blocks, sources, arrays, begun=()):
+def field(name, depth, blocks, sources, arrays, begun=(), outs=3):
     operands = (*arrays, *begun)
-    shapes = ((192, depth), (40, depth), (40, depth))
-    rows = sum(CORE_ROWS) + sum(EDGE_ROWS)
+    shapes = ((192, depth), (40, depth), (40, depth))[:outs]
+    rows, place = sum(CORE_ROWS) + sum(EDGE_ROWS), (3, 27 + 2 * BLOCKS, 8, 128)
+    kernel = functools.partial(field_kernel, sources, bool(begun), outs)
+    if outs == 2:
+        shapes, rows, place = ((40, depth),) * 2, EDGE_ROWS[OWN], (81 + 8, 8, 128)
+        kernel = functools.partial(edge_field_kernel, sources)
     return pl.pallas_call(
-        functools.partial(field_kernel, sources, bool(begun)),
+        kernel,
         out_shape=[jax.ShapeDtypeStruct(s, f32) for s in shapes],
         in_specs=[VM] * len(operands),
-        out_specs=[VM] * 3,
+        out_specs=[VM] * len(shapes),
         scratch_shapes=[
-            pltpu.VMEM((3, 27 + 2 * BLOCKS, 8, 128), f32),
+            pltpu.VMEM(place, f32),
             pltpu.VMEM((rows, 128), f32),
             pltpu.VMEM((rows, 128), f32),
         ],
@@ -271,12 +341,11 @@
     far, near, *begun = lax.optimization_barrier((far, near, *begun))
     one = jnp.concatenate([near, jnp.zeros_like(near)])
     above, below = jnp.where(even, far[0:2], one), jnp.where(even, one, far[0:2])
-    core, left, right = field(
-        "rest", depth, 16, [[(0, 0), (0, 1)], [(2, 2)], [(1, 0), (1, 1)]],
-        [above, below, far], begun,
-    )
-    from_left = passed_along(right, "gy", 1)
-    from_right = passed_along(left, "gy", -1)
+    sources, arrays = [[(0, 0), (0, 1)], [(2, 2)], [(1, 0), (1, 1)]], [above, below, far]
+    left, right = field("rest_edges", depth, 16, sources, arrays, begun[1:], 2)
+    from_left, from_right = passed_along(right, "gy", 1), passed_along(left, "gy", -1)
+    (core,) = field("rest_core", depth, 16, sources, arrays, begun[:1], 1)
+    core, from_left, from_right = lax.optimization_barrier((core, from_left, from_right))
     return pl.pallas_call(
         edge_kernel,
         out_shape=jax.ShapeDtypeStruct(old_map.shape, f32),

time: 50.6 us -> 49.6 us (0.980)
  the two profiles are of different devices: /device:TPU:122 before, /device:TPU:101 now
where the time goes in v5:
time: 49.6 us; the launch traced here: 49.2 us
  starting transfers between devices  24.7 us (50%)
  Pallas kernels  23.3 us (47%)
  local copies, waits for them, and re-layouts  0.86 us (2%)
    pallas_call x4, Pallas kernels, field(): pl.pallas_call(kernel, out_shape=[jax.ShapeDtypeStruct(s, f32) for s in s...  20.7 us
    ppermute x4, starting transfers between devices, passed_along(): lax.ppermute(value, axis, [(source, source + steps) for source in range(f...  14.9 us
    ppermute x1, starting transfers between devices, body(): near = lax.ppermute(near, 'gx', [p for p in behind if 0 <= p[1] < count])  4.76 us
    ppermute x1, starting transfers between devices, body(): lax.ppermute(own, 'gx', [(r, r + 1 - 2 * (r % 2)) for r in range(count)])  3.14 us
    ppermute x1, starting transfers between devices, body(): far = lax.ppermute(far, 'gx', [p for p in ahead if 0 <= p[1] < count])  1.92 us
    pallas_call x1, Pallas kernels, body(): pl.pallas_call(pack_kernel, out_shape=[third] * 3, in_specs=[HBM] * 4, ou...  1.51 us
    pallas_call x1, Pallas kernels, body(): pl.pallas_call(edge_kernel, out_shape=jax.ShapeDtypeStruct(old_map.shape,...  1.06 us
  transfers between devices with their start and end apart: 7, of which 0 were waited for; matrix products, arithmetic and copies ran while one was open for 2% of the time, Pallas kernels for 33%

profile of v5, /device:TPU:101, one launch (start us, length us, event | category | flops | bytes accessed | tf_op | source)
XLA Modules:
  0.0 49.2 jit_solution(2742208998633700118)
XLA Ops:
  0.0 1.5 %pack.1 = (f32[3,3,8,128]{3,2,1,0:T(8,128)}, f32[3,3,8,128]{3,2,1,0:T(8,128)}, f32[3,3,8,128]{3,2,1,0:T(8,128)}) custom-call(s32[12]{0:T(128)} %bitcast.3, f32[12,3,128]{2,1,0:T(4,128)} %refs_1_.1, f32[12,128]{1,0:T(8,128)} %refs_2_.1, f32[12,128]{1,0:T(8,128)} %refs_3_.1), custom_call_target="tpu_custom_call" | custom-call | tf_op jit(solution)/shard_map/pack/pallas_call | solution.py:295
  1.5 3.2 %collective-permute-start = (f32[3,3,8,128]{3,2,1,0:T(8,128)}, f32[3,3,8,128]{3,2,1,0:T(8,128)S(1)}, u32[]{:S(2)}, u32[]{:S(2)}) collective-permute-start(f32[3,3,8,128]{3,2,1,0:T(8,128)} %get-tuple-element.30), channel_id=1, source_target_pairs={{0,1},{1,2},{2,3},{3,4},{4,5},{5,6},{6,7},{7,8},{8,9},{9,10},{10,1... | collective-permute-start | bytes 110600 | tf_op jit(solution)/shard_map/ppermute | solution.py:288
  4.7 4.2 %collective-permute-start.1 = (f32[3,3,8,128]{3,2,1,0:T(8,128)}, f32[3,3,8,128]{3,2,1,0:T(8,128)S(1)}, u32[]{:S(2)}, u32[]{:S(2)}) collective-permute-start(f32[3,3,8,128]{3,2,1,0:T(8,128)} %get-tuple-element.31), channel_id=1, source_target_pairs={{1,0},{2,1},{3,2},{4,3},{5,4},{6,5},{7,6},{8,7},{9,8},{10,9},{11,1... | collective-permute-start | bytes 110600 | tf_op jit(solution)/shard_map/ppermute | solution.py:288
  8.9 0.0 copy-start.1
  8.9 0.8 %constant_dynamic-update-slice_fusion.2 = f32[3,9,8,128]{3,2,1,0:T(8,128)S(1)} fusion(f32[3,3,8,128]{3,2,1,0:T(8,128)} %get-tuple-element.29.refs_0_), kind=kLoop, calls=%fused_computation.10 | loop fusion | bytes 73728
  9.8 0.0 copy-done.1
  9.8 3.0 %stored.1 = (f32[192,1024]{1,0:T(8,128)S(1)}, f32[40,1024]{1,0:T(8,128)S(1)}, f32[40,1024]{1,0:T(8,128)S(1)}) custom-call(f32[3,3,8,128]{3,2,1,0:T(8,128)S(1)} %copy-done.1), custom_call_target="tpu_custom_call" | custom-call | flops 800000000 | bytes 4000000 | tf_op jit(solution)/shard_map/stored/pallas_call | solution.py:232
  12.8 0.0 collective-permute-done.refs_0_
  12.8 0.0 collective-permute-done.1.refs_1_
  12.8 3.1 %collective-permute-start.2 = (f32[3,9,8,128]{3,2,1,0:T(8,128)S(1)}, f32[3,9,8,128]{3,2,1,0:T(8,128)S(1)}, u32[]{:S(2)}, u32[]{:S(2)}) collective-permute-start(f32[3,9,8,128]{3,2,1,0:T(8,128)S(1)} %constant_dynamic-update-slice_fusion), channel_id=1, source_target_pairs={{0,16},{16,0},{32,48},{48,32},{64,80},{80,64},{96,112},{112,96},{1... | collective-permute-start | bytes 331784 | tf_op jit(solution)/shard_map/ppermute | solution.py:317
  16.0 4.8 %collective-permute-start.4 = (f32[1,9,8,128]{3,2,1,0:T(8,128)S(1)}, f32[1,9,8,128]{3,2,1,0:T(8,128)S(1)}, u32[]{:S(2)}, u32[]{:S(2)}) collective-permute-start(f32[1,9,8,128]{3,2,1,0:T(8,128)S(1)} %get-tuple-element.60), channel_id=1, source_target_pairs={{16,48},{32,0},{48,80},{64,32},{80,112},{96,64},{112,144},{128,96}... | collective-permute-start | bytes 110600 | tf_op jit(solution)/shard_map/ppermute | solution.py:329
  20.7 0.0 collective-permute-done.2
  20.8 1.9 %collective-permute-start.3 = (f32[3,9,8,128]{3,2,1,0:T(8,128)S(1)}, f32[3,9,8,128]{3,2,1,0:T(8,128)S(1)}, u32[]{:S(2)}, u32[]{:S(2)}) collective-permute-start(f32[3,9,8,128]{3,2,1,0:T(8,128)S(1)} %maximum_select_fusion), channel_id=1, source_target_pairs={{0,32},{32,64},{48,16},{64,96},{80,48},{96,128},{112,80},{128,160}... | collective-permute-start | bytes 331784 | tf_op jit(solution)/shard_map/ppermute | solution.py:328
  22.8 6.5 %chip.1 = (f32[192,1024]{1,0:T(8,128)S(1)}, f32[40,1024]{1,0:T(8,128)S(1)}, f32[40,1024]{1,0:T(8,128)S(1)}) custom-call(f32[3,3,8,128]{3,2,1,0:T(8,128)S(1)} %collective-permute-done.refs_0_, f32[3,3,8,128]{3,2,1,0:T(8,128)S(1)} %collective-permute-done.1.refs_1_, f32[3,9,8,128]{3,2,1,0:T(8,128)S(1)} %pad_maximum_fusion.refs_2_, ...), custom_call_target="tpu_custom_call" | custom-call | flops 3200000000 | bytes 4000000 | tf_op jit(solution)/shard_map/chip/pallas_call | solution.py:232
  29.2 0.0 collective-permute-done.4
  29.2 0.0 collective-permute-done.3.refs_2_
  29.3 4.6 %rest_edges.1 = (f32[40,1024]{1,0:T(8,128)S(1)}, f32[40,1024]{1,0:T(8,128)S(1)}) custom-call(f32[2,9,8,128]{3,2,1,0:T(8,128)S(1)} %get-tuple-element.54.refs_0_, f32[2,9,8,128]{3,2,1,0:T(8,128)S(1)} %get-tuple-element.53.refs_1_, f32[3,9,8,128]{3,2,1,0:T(8,128)S(1)} %collective-permute-done.3.refs_2_, f32[40,1024]{1,0:T(8,128)S(1)} %get-tuple-element.46.refs_3_, ...), custom_call_target="tpu_custom_call" | custom-call | flops 3200000000 | bytes 4000000 | tf_op jit(solution)/shard_map/rest_edges/pallas_call | solution.py:232
  33.9 1.9 %collective-permute-start.5 = (f32[40,1024]{1,0:T(8,128)S(1)}, f32[40,1024]{1,0:T(8,128)S(1)}, u32[]{:S(2)}, u32[]{:S(2)}) collective-permute-start(f32[40,1024]{1,0:T(8,128)S(1)} %get-tuple-element.48), channel_id=1, source_target_pairs={{0,1},{1,2},{2,3},{3,4},{4,5},{5,6},{6,7},{7,8},{8,9},{9,10},{10,1... | collective-permute-start | bytes 491528 | tf_op jit(solution)/shard_map/ppermute | solution.py:288
  35.8 0.0 copy-start
  35.8 5.6 %collective-permute-start.6 = (f32[40,1024]{1,0:T(8,128)S(1)}, f32[40,1024]{1,0:T(8,128)S(1)}, u32[]{:S(2)}, u32[]{:S(2)}) collective-permute-start(f32[40,1024]{1,0:T(8,128)S(1)} %get-tuple-element.49), channel_id=1, source_target_pairs={{1,0},{2,1},{3,2},{4,3},{5,4},{6,5},{7,6},{8,7},{9,8},{10,9},{11,1... | collective-permute-start | bytes 491528 | tf_op jit(solution)/shard_map/ppermute | solution.py:288
  41.4 6.7 %rest_core.1 = f32[192,1024]{1,0:T(8,128)S(1)} custom-call(f32[2,9,8,128]{3,2,1,0:T(8,128)S(1)} %get-tuple-element.54.refs_0_, f32[2,9,8,128]{3,2,1,0:T(8,128)S(1)} %get-tuple-element.53.refs_1_, f32[3,9,8,128]{3,2,1,0:T(8,128)S(1)} %collective-permute-done.3.refs_2_, f32[192,1024]{1,0:T(8,128)S(1)} %get-tuple-element.45.refs_3_), custom_call_target="tpu_custom_call" | custom-call | flops 3200000000 | bytes 4000000 | tf_op jit(solution)/shard_map/rest_core/pallas_call | solution.py:232
  48.1 0.0 collective-permute-done.5.from_left
  48.1 0.0 collective-permute-done.6.from_right
  48.1 0.0 copy-done
  48.1 1.1 %edges.1 = f32[8,24,1024]{2,1,0:T(8,128)} custom-call(f32[8,24,1024]{2,1,0:T(8,128)S(1)} %bitcast.2, f32[8,24,1024]{2,1,0:T(8,128)S(1)} %copy-done, f32[40,1024]{1,0:T(8,128)S(1)} %collective-permute-done.5.from_left, f32[40,1024]{1,0:T(8,128)S(1)} %collective-permute-done.6.from_right), custom_call_target="tpu_custom_call" | custom-call | tf_op jit(solution)/shard_map/edges/pallas_call | solution.py:349
  (8 shorter events, 0.1 us)
Async XLA Ops:
  1.5 11.2 %collective-permute-start = (f32[3,3,8,128]{3,2,1,0:T(8,128)}, f32[3,3,8,128]{3,2,1,0:T(8,128)S(1)}, u32[]{:S(2)}, u32[]{:S(2)}) collective-permute-start(f32[3,3,8,128]{3,2,1,0:T(8,128)} %get-tuple-element.30), channel_id=1, source_target_pairs={{0,1},{1,2},{2,3},{3,4},{4,5},{5,6},{6,7},{7,8},{8,9},{9,10},{10,1... | collective-permute-start | bytes 110600 | tf_op jit(solution)/shard_map/ppermute | solution.py:288
  4.7 8.0 %collective-permute-start.1 = (f32[3,3,8,128]{3,2,1,0:T(8,128)}, f32[3,3,8,128]{3,2,1,0:T(8,128)S(1)}, u32[]{:S(2)}, u32[]{:S(2)}) collective-permute-start(f32[3,3,8,128]{3,2,1,0:T(8,128)} %get-tuple-element.31), channel_id=1, source_target_pairs={{1,0},{2,1},{3,2},{4,3},{5,4},{6,5},{7,6},{8,7},{9,8},{10,9},{11,1... | collective-permute-start | bytes 110600 | tf_op jit(solution)/shard_map/ppermute | solution.py:288
  8.9 0.8 %copy-start.1 = (f32[3,3,8,128]{3,2,1,0:T(8,128)S(1)}, f32[3,3,8,128]{3,2,1,0:T(8,128)}, u32[]{:S(2)}) copy-start(f32[3,3,8,128]{3,2,1,0:T(8,128)} %get-tuple-element.29.refs_0_) | copy-start | bytes 110596
  12.8 7.9 %collective-permute-start.2 = (f32[3,9,8,128]{3,2,1,0:T(8,128)S(1)}, f32[3,9,8,128]{3,2,1,0:T(8,128)S(1)}, u32[]{:S(2)}, u32[]{:S(2)}) collective-permute-start(f32[3,9,8,128]{3,2,1,0:T(8,128)S(1)} %constant_dynamic-update-slice_fusion), channel_id=1, source_target_pairs={{0,16},{16,0},{32,48},{48,32},{64,80},{80,64},{96,112},{112,96},{1... | collective-permute-start | bytes 331784 | tf_op jit(solution)/shard_map/ppermute | solution.py:317
  16.0 13.3 %collective-permute-start.4 = (f32[1,9,8,128]{3,2,1,0:T(8,128)S(1)}, f32[1,9,8,128]{3,2,1,0:T(8,128)S(1)}, u32[]{:S(2)}, u32[]{:S(2)}) collective-permute-start(f32[1,9,8,128]{3,2,1,0:T(8,128)S(1)} %get-tuple-element.60), channel_id=1, source_target_pairs={{16,48},{32,0},{48,80},{64,32},{80,112},{96,64},{112,144},{128,96}... | collective-permute-start | bytes 110600 | tf_op jit(solution)/shard_map/ppermute | solution.py:329
  20.8 8.4 %collective-permute-start.3 = (f32[3,9,8,128]{3,2,1,0:T(8,128)S(1)}, f32[3,9,8,128]{3,2,1,0:T(8,128)S(1)}, u32[]{:S(2)}, u32[]{:S(2)}) collective-permute-start(f32[3,9,8,128]{3,2,1,0:T(8,128)S(1)} %maximum_select_fusion), channel_id=1, source_target_pairs={{0,32},{32,64},{48,16},{64,96},{80,48},{96,128},{112,80},{128,160}... | collective-permute-start | bytes 331784 | tf_op jit(solution)/shard_map/ppermute | solution.py:328
  33.9 14.2 %collective-permute-start.5 = (f32[40,1024]{1,0:T(8,128)S(1)}, f32[40,1024]{1,0:T(8,128)S(1)}, u32[]{:S(2)}, u32[]{:S(2)}) collective-permute-start(f32[40,1024]{1,0:T(8,128)S(1)} %get-tuple-element.48), channel_id=1, source_target_pairs={{0,1},{1,2},{2,3},{3,4},{4,5},{5,6},{6,7},{7,8},{8,9},{9,10},{10,1... | collective-permute-start | bytes 491528 | tf_op jit(solution)/shard_map/ppermute | solution.py:288
  35.8 12.3 %copy-start = (f32[8,24,1024]{2,1,0:T(8,128)S(1)}, f32[8,24,1024]{2,1,0:T(8,128)}, u32[]{:S(2)}) copy-start(f32[8,24,1024]{2,1,0:T(8,128)} %old.1) | copy-start | bytes 2359300
  35.8 12.3 %collective-permute-start.6 = (f32[40,1024]{1,0:T(8,128)S(1)}, f32[40,1024]{1,0:T(8,128)S(1)}, u32[]{:S(2)}, u32[]{:S(2)}) collective-permute-start(f32[40,1024]{1,0:T(8,128)S(1)} %get-tuple-element.49), channel_id=1, source_target_pairs={{1,0},{2,1},{3,2},{4,3},{5,4},{6,5},{7,6},{8,7},{9,8},{10,9},{11,1... | collective-permute-start | bytes 491528 | tf_op jit(solution)/shard_map/ppermute | solution.py:288

commit v6 on v5

--- a/solution.py
+++ b/solution.py
@@ -30,7 +30,8 @@
         side = m >= n // 2
         e = jnp.where(side, m - n // 2, m) + (8 if group == BELOW else 0)
         i = quotient(e, 5)
-        j = e - i * 5 + jnp.where(side, 24, -W)
+        right = jnp.logical_xor(side, lax.rem(lax.axis_index("gy"), 2) == 0)
+        j = e - i * 5 + jnp.where(right, 24, -W)
     place = (i + (8, 0, -8)[group]).astype(f32)
     if group == ABOVE:
         place = jnp.where(i >= W, FAR, place)
@@ -112,18 +113,18 @@
     return [[(ref, 0, 128, 0)], [(ref, 0, 192, 0)], [(ref, 64, 128, 0)]]
 
 
-def edge_adds(left, right):
+def edge_adds(first, second):
     return [
-        [(left, 0, 32, 0), (right, 0, 32, 32)],
-        [(left, 0, 40, 0), (right, 0, 40, 40)],
-        [(left, 8, 32, 0), (right, 8, 32, 32)],
+        [(first, 0, 32, 0), (second, 0, 32, 32)],
+        [(first, 0, 40, 0), (second, 0, 40, 40)],
+        [(first, 8, 32, 0), (second, 8, 32, 32)],
     ]
 
 
-def both_adds(core, left, right):
+def both_adds(core, first, second):
     return [
         a + [(ref, to, n, source + CORE_ROWS[g]) for ref, to, n, source in b]
-        for g, (a, b) in enumerate(zip(core_adds(core), edge_adds(left, right)))
+        for g, (a, b) in enumerate(zip(core_adds(core), edge_adds(first, second)))
     ]
 
 
@@ -158,12 +159,12 @@
 
 
 def edge_field_kernel(sources, *refs):
-    left, right, lists, ti, tj = refs[-5:]
+    first, second, lists, ti, tj = refs[-5:]
     inputs = refs[:-5]
-    depth = left.shape[1]
+    depth = first.shape[1]
     put_rows(ti, tj, 0, OWN, False)
-    left[...] = inputs[-2][...]
-    right[...] = inputs[-1][...]
+    first[...] = inputs[-2][...]
+    second[...] = inputs[-1][...]
     count = jnp.int32(0)
     for g in range(3):
         segments = [(inputs[n], part) for n, part in sources[g]]
@@ -197,8 +198,8 @@
                 nxt = along(b + 1)
             pp = dot(jnp.concatenate([ph, plo], 0), zh)
             r = pp[:80] + pp[80:] + dot(ph, zl)
-            left[:, b * WIDE:(b + 1) * WIDE] += r[0:40]
-            right[:, b * WIDE:(b + 1) * WIDE] += r[40:80]
+            first[:, b * WIDE:(b + 1) * WIDE] += r[0:40]
+            second[:, b * WIDE:(b + 1) * WIDE] += r[40:80]
 
     def step(t, carry):
         stage(t * 8, 8)
@@ -248,7 +249,7 @@
 
 
 def pack_kernel(*refs):
-    hbm, (minus, same, plus), local, (slots, taken, sems) = refs[:4], refs[4:7], refs[7:11], refs[11:]
+    hbm, (pair_out, same, other_out), local, (slots, taken, sems) = refs[:4], refs[4:7], refs[7:11], refs[11:]
     fetches = [pltpu.make_async_copy(a, b, sems.at[n]) for n, (a, b) in enumerate(zip(hbm, local))]
     for fetch in fetches:
         fetch.start()
@@ -271,28 +272,39 @@
         home = tile_row + row - 1
         inside = (home >= 0) & (home < tile_rows)
         slots[place, 5:6, :] = jnp.full((1, 128), jnp.where(inside, 1.0, 0.0), f32)
-    for k, out in enumerate((minus, same, plus)):
-        out[...] = slots[9 * k:9 * k + 9].reshape(out.shape)
-
-
-def edge_kernel(core, old, from_left, from_right, out):
+    even = lax.rem(lax.axis_index("gy"), 2) == 0
+    for k, out in ((jnp.where(even, 2, 0), pair_out), (1, same), (jnp.where(even, 0, 2), other_out)):
+        out[...] = slots[pl.ds(9 * k, 9)].reshape(out.shape)
+
+
+def edge_kernel(core, old, first, second, out):
     out[...] = core[...] + old[...]
-    for i in range(core.shape[0]):
-        out[i, 0:5, :] += from_left[i * 5:i * 5 + 5, :]
-        out[i, 19:24, :] += from_right[i * 5:i * 5 + 5, :]
-
-
-def passed_along(value, axis, steps):
-    count = lax.axis_size(axis)
-    first, last = (max(0, -steps), min(count, count - steps))
-    return lax.ppermute(value, axis, [(source, source + steps) for source in range(first, last)])
+    even = lax.rem(lax.axis_index("gy"), 2) == 0
+
+    def add(from_left, from_right):
+        for i in range(core.shape[0]):
+            out[i, 0:5, :] += from_left[i * 5:i * 5 + 5, :]
+            out[i, 19:24, :] += from_right[i * 5:i * 5 + 5, :]
+
+    @pl.when(even)
+    def _():
+        add(second, first)
+
+    @pl.when(jnp.logical_not(even))
+    def _():
+        add(first, second)
+
+
+def swapped(value, start):
+    pairs = [(k, k + 1) for k in range(start, lax.axis_size("gy") - 1, 2)]
+    return lax.ppermute(value, "gy", pairs + [(b, a) for a, b in pairs])
 
 
 def body(offsets, widths, solvation, heading, old_map):
     depth = old_map.shape[2]
     third = jax.ShapeDtypeStruct((3, 3, 8, 128), f32)
     small = pltpu.CompilerParams(vmem_limit_bytes=8 * 1024 * 1024)
-    minus, same, plus = pl.pallas_call(
+    first, same, second = pl.pallas_call(
         pack_kernel,
         out_shape=[third] * 3,
         in_specs=[HBM] * 4,
@@ -309,10 +321,10 @@
         compiler_params=pltpu.CompilerParams(vmem_limit_bytes=60 * 1024 * 1024),
         name="pack",
     )(heading[:, 0], offsets, widths, solvation)
-    left_in, right_in = passed_along(plus, "gy", 1), passed_along(minus, "gy", -1)
+    first, second = swapped(first, 0), swapped(second, 1)
     begun = field("stored", depth, 4, [[(0, 0)], [(0, 1)], [(0, 2)]], [same])
-    left_in, right_in, *begun = lax.optimization_barrier((left_in, right_in, *begun))
-    own = jnp.concatenate([same, left_in, right_in], axis=1)
+    first, second, *begun = lax.optimization_barrier((first, second, *begun))
+    own = jnp.concatenate([same, first, second], axis=1)
     count = lax.axis_size("gx")
     partner = lax.ppermute(own, "gx", [(r, r + 1 - 2 * (r % 2)) for r in range(count)])
     even = lax.rem(lax.axis_index("gx"), 2) == 0
@@ -336,16 +348,16 @@
     )
     begun = field(
         "chip", depth, 16, [[(0, g), (1, g), (2, g)] for g in range(3)],
-        [left_in, right_in, beside], begun,
+        [first, second, beside], begun,
     )
     far, near, *begun = lax.optimization_barrier((far, near, *begun))
     one = jnp.concatenate([near, jnp.zeros_like(near)])
     above, below = jnp.where(even, far[0:2], one), jnp.where(even, one, far[0:2])
     sources, arrays = [[(0, 0), (0, 1)], [(2, 2)], [(1, 0), (1, 1)]], [above, below, far]
-    left, right = field("rest_edges", depth, 16, sources, arrays, begun[1:], 2)
-    from_left, from_right = passed_along(right, "gy", 1), passed_along(left, "gy", -1)
+    edges = field("rest_edges", depth, 16, sources, arrays, begun[1:], 2)
+    first, second = swapped(edges[0], 0), swapped(edges[1], 1)
     (core,) = field("rest_core", depth, 16, sources, arrays, begun[:1], 1)
-    core, from_left, from_right = lax.optimization_barrier((core, from_left, from_right))
+    core, first, second = lax.optimization_barrier((core, first, second))
     return pl.pallas_call(
         edge_kernel,
         out_shape=jax.ShapeDtypeStruct(old_map.shape, f32),
@@ -353,7 +365,7 @@
         out_specs=VM,
         compiler_params=small,
         name="edges",
-    )(core.reshape(old_map.shape), old_map, from_left, from_right)
+    )(core.reshape(old_map.shape), old_map, first, second)
 
 
 def solution(mesh):

time: 49.6 us -> 47.2 us (0.952)
  the two profiles are of different devices: /device:TPU:101 before, /device:TPU:102 now
where the time goes in v6:
time: 47.2 us; the launch traced here: 46.9 us
  starting transfers between devices  23.2 us (49%)
  Pallas kernels  21.5 us (46%)
  waiting for transfers between devices  0.97 us (2%)
  local copies, waits for them, and re-layouts  0.86 us (2%)
    pallas_call x4, Pallas kernels, field(): pl.pallas_call(kernel, out_shape=[jax.ShapeDtypeStruct(s, f32) for s in s...  19 us
    ppermute x4, starting transfers between devices, swapped(): return lax.ppermute(value, 'gy', pairs + [(b, a) for a, b in pairs])  14.2 us
    ppermute x1, starting transfers between devices, body(): far = lax.ppermute(far, 'gx', [p for p in ahead if 0 <= p[1] < count])  5.03 us
    ppermute x1, starting transfers between devices, body(): near = lax.ppermute(near, 'gx', [p for p in behind if 0 <= p[1] < count])  2.02 us
    ppermute x1, starting transfers between devices, body(): lax.ppermute(own, 'gx', [(r, r + 1 - 2 * (r % 2)) for r in range(count)])  1.92 us
    pallas_call x1, Pallas kernels, body(): pl.pallas_call(pack_kernel, out_shape=[third] * 3, in_specs=[HBM] * 4, ou...  1.51 us
    pallas_call x1, Pallas kernels, body(): pl.pallas_call(edge_kernel, out_shape=jax.ShapeDtypeStruct(old_map.shape,...  1.07 us
    ppermute x4, waiting for transfers between devices, swapped(): return lax.ppermute(value, 'gy', pairs + [(b, a) for a, b in pairs])  0.97 us
  transfers between devices with their start and end apart: 7, of which 1 were waited for; matrix products, arithmetic and copies ran while one was open for 2% of the time, Pallas kernels for 32%

profile of v6, /device:TPU:102, one launch (start us, length us, event | category | flops | bytes accessed | tf_op | source)
XLA Modules:
  0.0 46.9 jit_solution(9286307194414696698)
XLA Ops:
  0.0 1.5 %pack.1 = (f32[3,3,8,128]{3,2,1,0:T(8,128)}, f32[3,3,8,128]{3,2,1,0:T(8,128)}, f32[3,3,8,128]{3,2,1,0:T(8,128)}) custom-call(s32[12]{0:T(128)} %bitcast.3, f32[12,3,128]{2,1,0:T(4,128)} %refs_1_.1, f32[12,128]{1,0:T(8,128)} %refs_2_.1, f32[12,128]{1,0:T(8,128)} %refs_3_.1), custom_call_target="tpu_custom_call" | custom-call | tf_op jit(solution)/shard_map/pack/pallas_call | solution.py:307
  1.5 3.5 %collective-permute-start = (f32[3,3,8,128]{3,2,1,0:T(8,128)}, f32[3,3,8,128]{3,2,1,0:T(8,128)S(1)}, u32[]{:S(2)}, u32[]{:S(2)}) collective-permute-start(f32[3,3,8,128]{3,2,1,0:T(8,128)} %get-tuple-element.30), channel_id=1, source_target_pairs={{0,1},{2,3},{4,5},{6,7},{8,9},{10,11},{12,13},{14,15},{1,0},{3,2},... | collective-permute-start | bytes 110600 | tf_op jit(solution)/shard_map/ppermute | solution.py:300
  5.0 4.4 %collective-permute-start.1 = (f32[3,3,8,128]{3,2,1,0:T(8,128)}, f32[3,3,8,128]{3,2,1,0:T(8,128)S(1)}, u32[]{:S(2)}, u32[]{:S(2)}) collective-permute-start(f32[3,3,8,128]{3,2,1,0:T(8,128)} %get-tuple-element.31), channel_id=1, source_target_pairs={{1,2},{3,4},{5,6},{7,8},{9,10},{11,12},{13,14},{2,1},{4,3},{6,5},{... | collective-permute-start | bytes 110600 | tf_op jit(solution)/shard_map/ppermute | solution.py:300
  9.4 0.0 copy-start.1
  9.4 0.8 %constant_dynamic-update-slice_fusion.2 = f32[3,9,8,128]{3,2,1,0:T(8,128)S(1)} fusion(f32[3,3,8,128]{3,2,1,0:T(8,128)} %get-tuple-element.29.refs_0_), kind=kLoop, calls=%fused_computation.10 | loop fusion | bytes 73728
  10.2 0.0 copy-done.1
  10.2 2.9 %stored.1 = (f32[192,1024]{1,0:T(8,128)S(1)}, f32[40,1024]{1,0:T(8,128)S(1)}, f32[40,1024]{1,0:T(8,128)S(1)}) custom-call(f32[3,3,8,128]{3,2,1,0:T(8,128)S(1)} %copy-done.1), custom_call_target="tpu_custom_call" | custom-call | flops 800000000 | bytes 4000000 | tf_op jit(solution)/shard_map/stored/pallas_call | solution.py:233
  13.2 0.0 collective-permute-done.refs_0_
  13.2 0.0 collective-permute-done.1.refs_1_
  13.2 1.9 %collective-permute-start.2 = (f32[3,9,8,128]{3,2,1,0:T(8,128)S(1)}, f32[3,9,8,128]{3,2,1,0:T(8,128)S(1)}, u32[]{:S(2)}, u32[]{:S(2)}) collective-permute-start(f32[3,9,8,128]{3,2,1,0:T(8,128)S(1)} %constant_dynamic-update-slice_fusion), channel_id=1, source_target_pairs={{0,16},{16,0},{32,48},{48,32},{64,80},{80,64},{96,112},{112,96},{1... | collective-permute-start | bytes 331784 | tf_op jit(solution)/shard_map/ppermute | solution.py:329
  15.2 2.0 %collective-permute-start.4 = (f32[1,9,8,128]{3,2,1,0:T(8,128)S(1)}, f32[1,9,8,128]{3,2,1,0:T(8,128)S(1)}, u32[]{:S(2)}, u32[]{:S(2)}) collective-permute-start(f32[1,9,8,128]{3,2,1,0:T(8,128)S(1)} %get-tuple-element.60), channel_id=1, source_target_pairs={{16,48},{32,0},{48,80},{64,32},{80,112},{96,64},{112,144},{128,96}... | collective-permute-start | bytes 110600 | tf_op jit(solution)/shard_map/ppermute | solution.py:341
  17.2 0.0 collective-permute-done.2
  17.3 5.0 %collective-permute-start.3 = (f32[3,9,8,128]{3,2,1,0:T(8,128)S(1)}, f32[3,9,8,128]{3,2,1,0:T(8,128)S(1)}, u32[]{:S(2)}, u32[]{:S(2)}) collective-permute-start(f32[3,9,8,128]{3,2,1,0:T(8,128)S(1)} %maximum_select_fusion), channel_id=1, source_target_pairs={{0,32},{32,64},{48,16},{64,96},{80,48},{96,128},{112,80},{128,160}... | collective-permute-start | bytes 331784 | tf_op jit(solution)/shard_map/ppermute | solution.py:340
  22.3 7.0 %chip.1 = (f32[192,1024]{1,0:T(8,128)S(1)}, f32[40,1024]{1,0:T(8,128)S(1)}, f32[40,1024]{1,0:T(8,128)S(1)}) custom-call(f32[3,3,8,128]{3,2,1,0:T(8,128)S(1)} %collective-permute-done.refs_0_, f32[3,3,8,128]{3,2,1,0:T(8,128)S(1)} %collective-permute-done.1.refs_1_, f32[3,9,8,128]{3,2,1,0:T(8,128)S(1)} %pad_maximum_fusion.refs_2_, ...), custom_call_target="tpu_custom_call" | custom-call | flops 3200000000 | bytes 4000000 | tf_op jit(solution)/shard_map/chip/pallas_call | solution.py:233
  29.4 0.0 collective-permute-done.4
  29.4 0.0 collective-permute-done.3.refs_2_
  29.4 3.9 %rest_edges.1 = (f32[40,1024]{1,0:T(8,128)S(1)}, f32[40,1024]{1,0:T(8,128)S(1)}) custom-call(f32[2,9,8,128]{3,2,1,0:T(8,128)S(1)} %get-tuple-element.54.refs_0_, f32[2,9,8,128]{3,2,1,0:T(8,128)S(1)} %get-tuple-element.53.refs_1_, f32[3,9,8,128]{3,2,1,0:T(8,128)S(1)} %collective-permute-done.3.refs_2_, f32[40,1024]{1,0:T(8,128)S(1)} %get-tuple-element.46.refs_3_, ...), custom_call_target="tpu_custom_call" | custom-call | flops 3200000000 | bytes 4000000 | tf_op jit(solution)/shard_map/rest_edges/pallas_call | solution.py:233
  33.3 2.3 %collective-permute-start.5 = (f32[40,1024]{1,0:T(8,128)S(1)}, f32[40,1024]{1,0:T(8,128)S(1)}, u32[]{:S(2)}, u32[]{:S(2)}) collective-permute-start(f32[40,1024]{1,0:T(8,128)S(1)} %get-tuple-element.48), channel_id=1, source_target_pairs={{0,1},{2,3},{4,5},{6,7},{8,9},{10,11},{12,13},{14,15},{1,0},{3,2},... | collective-permute-start | bytes 491528 | tf_op jit(solution)/shard_map/ppermute | solution.py:300
  35.7 0.0 copy-start
  35.7 4.0 %collective-permute-start.6 = (f32[40,1024]{1,0:T(8,128)S(1)}, f32[40,1024]{1,0:T(8,128)S(1)}, u32[]{:S(2)}, u32[]{:S(2)}) collective-permute-start(f32[40,1024]{1,0:T(8,128)S(1)} %get-tuple-element.49), channel_id=1, source_target_pairs={{1,2},{3,4},{5,6},{7,8},{9,10},{11,12},{13,14},{2,1},{4,3},{6,5},{... | collective-permute-start | bytes 491528 | tf_op jit(solution)/shard_map/ppermute | solution.py:300
  39.7 5.1 %rest_core.1 = f32[192,1024]{1,0:T(8,128)S(1)} custom-call(f32[2,9,8,128]{3,2,1,0:T(8,128)S(1)} %get-tuple-element.54.refs_0_, f32[2,9,8,128]{3,2,1,0:T(8,128)S(1)} %get-tuple-element.53.refs_1_, f32[3,9,8,128]{3,2,1,0:T(8,128)S(1)} %collective-permute-done.3.refs_2_, f32[192,1024]{1,0:T(8,128)S(1)} %get-tuple-element.45.refs_3_), custom_call_target="tpu_custom_call" | custom-call | flops 3200000000 | bytes 4000000 | tf_op jit(solution)/shard_map/rest_core/pallas_call | solution.py:233
  44.8 0.0 collective-permute-done.5.first
  44.8 1.0 %collective-permute-done.6.second = f32[40,1024]{1,0:T(8,128)S(1)} collective-permute-done((f32[40,1024]{1,0:T(8,128)S(1)}, f32[40,1024]{1,0:T(8,128)S(1)}, u32[]{:S(2)}, u32[]{:S(2)}) %collective-permute-start.6) | collective-permute-done | bytes 163872 | tf_op jit(solution)/shard_map/ppermute | solution.py:300
  45.8 0.0 copy-done
  45.8 1.1 %edges.1 = f32[8,24,1024]{2,1,0:T(8,128)} custom-call(f32[8,24,1024]{2,1,0:T(8,128)S(1)} %bitcast.2, f32[8,24,1024]{2,1,0:T(8,128)S(1)} %copy-done, f32[40,1024]{1,0:T(8,128)S(1)} %collective-permute-done.5.first, f32[40,1024]{1,0:T(8,128)S(1)} %collective-permute-done.6.second), custom_call_target="tpu_custom_call" | custom-call | tf_op jit(solution)/shard_map/edges/pallas_call | solution.py:361
  (8 shorter events, 0.1 us)
Async XLA Ops:
  1.5 11.7 %collective-permute-start = (f32[3,3,8,128]{3,2,1,0:T(8,128)}, f32[3,3,8,128]{3,2,1,0:T(8,128)S(1)}, u32[]{:S(2)}, u32[]{:S(2)}) collective-permute-start(f32[3,3,8,128]{3,2,1,0:T(8,128)} %get-tuple-element.30), channel_id=1, source_target_pairs={{0,1},{2,3},{4,5},{6,7},{8,9},{10,11},{12,13},{14,15},{1,0},{3,2},... | collective-permute-start | bytes 110600 | tf_op jit(solution)/shard_map/ppermute | solution.py:300
  5.0 8.2 %collective-permute-start.1 = (f32[3,3,8,128]{3,2,1,0:T(8,128)}, f32[3,3,8,128]{3,2,1,0:T(8,128)S(1)}, u32[]{:S(2)}, u32[]{:S(2)}) collective-permute-start(f32[3,3,8,128]{3,2,1,0:T(8,128)} %get-tuple-element.31), channel_id=1, source_target_pairs={{1,2},{3,4},{5,6},{7,8},{9,10},{11,12},{13,14},{2,1},{4,3},{6,5},{... | collective-permute-start | bytes 110600 | tf_op jit(solution)/shard_map/ppermute | solution.py:300
  9.4 0.8 %copy-start.1 = (f32[3,3,8,128]{3,2,1,0:T(8,128)S(1)}, f32[3,3,8,128]{3,2,1,0:T(8,128)}, u32[]{:S(2)}) copy-start(f32[3,3,8,128]{3,2,1,0:T(8,128)} %get-tuple-element.29.refs_0_) | copy-start | bytes 110596
  13.2 4.0 %collective-permute-start.2 = (f32[3,9,8,128]{3,2,1,0:T(8,128)S(1)}, f32[3,9,8,128]{3,2,1,0:T(8,128)S(1)}, u32[]{:S(2)}, u32[]{:S(2)}) collective-permute-start(f32[3,9,8,128]{3,2,1,0:T(8,128)S(1)} %constant_dynamic-update-slice_fusion), channel_id=1, source_target_pairs={{0,16},{16,0},{32,48},{48,32},{64,80},{80,64},{96,112},{112,96},{1... | collective-permute-start | bytes 331784 | tf_op jit(solution)/shard_map/ppermute | solution.py:329
  15.2 14.2 %collective-permute-start.4 = (f32[1,9,8,128]{3,2,1,0:T(8,128)S(1)}, f32[1,9,8,128]{3,2,1,0:T(8,128)S(1)}, u32[]{:S(2)}, u32[]{:S(2)}) collective-permute-start(f32[1,9,8,128]{3,2,1,0:T(8,128)S(1)} %get-tuple-element.60), channel_id=1, source_target_pairs={{16,48},{32,0},{48,80},{64,32},{80,112},{96,64},{112,144},{128,96}... | collective-permute-start | bytes 110600 | tf_op jit(solution)/shard_map/ppermute | solution.py:341
  17.3 12.1 %collective-permute-start.3 = (f32[3,9,8,128]{3,2,1,0:T(8,128)S(1)}, f32[3,9,8,128]{3,2,1,0:T(8,128)S(1)}, u32[]{:S(2)}, u32[]{:S(2)}) collective-permute-start(f32[3,9,8,128]{3,2,1,0:T(8,128)S(1)} %maximum_select_fusion), channel_id=1, source_target_pairs={{0,32},{32,64},{48,16},{64,96},{80,48},{96,128},{112,80},{128,160}... | collective-permute-start | bytes 331784 | tf_op jit(solution)/shard_map/ppermute | solution.py:340
  33.3 11.5 %collective-permute-start.5 = (f32[40,1024]{1,0:T(8,128)S(1)}, f32[40,1024]{1,0:T(8,128)S(1)}, u32[]{:S(2)}, u32[]{:S(2)}) collective-permute-start(f32[40,1024]{1,0:T(8,128)S(1)} %get-tuple-element.48), channel_id=1, source_target_pairs={{0,1},{2,3},{4,5},{6,7},{8,9},{10,11},{12,13},{14,15},{1,0},{3,2},... | collective-permute-start | bytes 491528 | tf_op jit(solution)/shard_map/ppermute | solution.py:300
  35.7 10.1 %copy-start = (f32[8,24,1024]{2,1,0:T(8,128)S(1)}, f32[8,24,1024]{2,1,0:T(8,128)}, u32[]{:S(2)}) copy-start(f32[8,24,1024]{2,1,0:T(8,128)} %old.1) | copy-start | bytes 2359300
  35.7 10.1 %collective-permute-start.6 = (f32[40,1024]{1,0:T(8,128)S(1)}, f32[40,1024]{1,0:T(8,128)S(1)}, u32[]{:S(2)}, u32[]{:S(2)}) collective-permute-start(f32[40,1024]{1,0:T(8,128)S(1)} %get-tuple-element.49), channel_id=1, source_target_pairs={{1,2},{3,4},{5,6},{7,8},{9,10},{11,12},{13,14},{2,1},{4,3},{6,5},{... | collective-permute-start | bytes 491528 | tf_op jit(solution)/shard_map/ppermute | solution.py:300

commit v7 on v6

--- a/solution.py
+++ b/solution.py
@@ -21,17 +21,21 @@
 
 def put_rows(ti, tj, start, group, core):
     n = (CORE_ROWS if core else EDGE_ROWS)[group]
+    if core:
+        inner = lax.broadcasted_iota(jnp.int32, (8, 128), 0).astype(f32)
+        for v in range(n // 8):
+            i, part = divmod(v + (8 if group == BELOW else 0), 3)
+            dead = (group == ABOVE and i >= W) or (group == BELOW and i < 8 - W)
+            place = FAR if dead else float(i + (8, 0, -8)[group])
+            ti[start + v * 8:start + v * 8 + 8, :] = jnp.full((8, 128), place, f32)
+            tj[start + v * 8:start + v * 8 + 8, :] = inner + 8.0 * part
+        return
     m = lax.broadcasted_iota(jnp.int32, (n, 128), 0)
-    if core:
-        row = m + (64 if group == BELOW else 0)
-        i = quotient(row, 24)
-        j = row - i * 24
-    else:
-        side = m >= n // 2
-        e = jnp.where(side, m - n // 2, m) + (8 if group == BELOW else 0)
-        i = quotient(e, 5)
-        right = jnp.logical_xor(side, lax.rem(lax.axis_index("gy"), 2) == 0)
-        j = e - i * 5 + jnp.where(right, 24, -W)
+    side = m >= n // 2
+    e = jnp.where(side, m - n // 2, m) + (8 if group == BELOW else 0)
+    i = quotient(e, 5)
+    right = jnp.logical_xor(side, lax.rem(lax.axis_index("gy"), 2) == 0)
+    j = e - i * 5 + jnp.where(right, 24, -W)
     place = (i + (8, 0, -8)[group]).astype(f32)
     if group == ABOVE:
         place = jnp.where(i >= W, FAR, place)
@@ -46,15 +50,21 @@
     return h, (v - h.astype(f32)).astype(bf16)
 
 
-def compact(place, sources, shift, count):
-    row = lax.broadcasted_iota(jnp.int32, (8, 128), 0)
+def masks(sources):
+    found = []
     for ref, part in sources:
         bits = jnp.zeros((1, 128), f32)
         for s in range(ref.shape[1]):
             bits = bits + ref[part, s, 5:6, :] * float(1 << s)
-        mask = jnp.max(bits).astype(jnp.int32)
+        found.append(jnp.max(bits).astype(jnp.int32))
+    return found
+
+
+def compact(place, sources, present, shift, count):
+    row = lax.broadcasted_iota(jnp.int32, (8, 128), 0)
+    for (ref, part), mask in zip(sources, present):
         for s in range(ref.shape[1]):
-            place[count] = jnp.where(row == 6, shift, ref[part, s])
+            place[count] = jnp.where(row == 6, shift, ref[part, s]) if shift else ref[part, s]
             count = count + (lax.shift_right_logical(mask, s) & 1)
     return count
 
@@ -97,16 +107,28 @@
             for ref, to, count, source in adds[g]:
                 ref[to:to + count, b * wide:(b + 1) * wide] += r[source:source + count]
 
+    def together(t, carry):
+        for g in range(3):
+            stage(g, t * blocks, blocks)
+        return carry
+
+    parts = [lax.div(c + blocks // 2, jnp.int32(blocks)) for c in counts]
+    joint = jnp.minimum(jnp.minimum(parts[0], parts[1]), parts[2])
+    lax.fori_loop(0, joint, together, 0)
     for g in range(3):
-        def step(t, carry, g=g):
-            stage(g, t * blocks, blocks)
+        begin = joint * blocks
+        left = jnp.maximum(counts[g] - begin, 0)
+        whole = lax.div(left + (blocks // 2 - 1), jnp.int32(blocks))
+
+        def step(t, carry, g=g, begin=begin):
+            stage(g, begin + t * blocks, blocks)
             return carry
-        whole = lax.div(counts[g] + (blocks // 2 - 1), jnp.int32(blocks))
+
         lax.fori_loop(0, whole, step, 0)
 
-        @pl.when(whole * blocks < counts[g])
-        def _(g=g, whole=whole):
-            stage(g, whole * blocks, blocks // 2)
+        @pl.when(whole * blocks < left)
+        def _(g=g, at=begin + whole * blocks):
+            stage(g, at, blocks // 2)
 
 
 def core_adds(ref):
@@ -139,20 +161,23 @@
     return rows, starts
 
 
-BLOCKS, WIDE = 4, 256
-
-
-def field_kernel(sources, begun, outs, *refs):
+BLOCKS, WIDE, EDGE_WIDE = 4, 512, 256
+
+
+def field_kernel(sources, begun, outs, keep, *refs):
     lists, ti, tj = refs[-3:]
     totals, inputs = refs[-3 - outs:-3], refs[:-3 - outs]
+    if keep:
+        inputs[-1][...] = inputs[0][...]
     depth = totals[0].shape[1]
     rows, starts = prepare(ti, tj, (True, False)[: max(1, outs - 1)])
     for n, ref in enumerate(totals):
         ref[...] = inputs[len(inputs) - outs + n][...] if begun else jnp.zeros_like(ref)
+    segments = [[(inputs[n], part) for n, part in sources[g]] for g in range(3)]
+    present = [masks(segments[g]) for g in range(3)]
     counts = []
     for g in range(3):
-        segments = [(inputs[n], part) for n, part in sources[g]]
-        counts.append(compact(lists.at[g], segments, 0.0, jnp.int32(0)))
+        counts.append(compact(lists.at[g], segments[g], present[g], 0.0, jnp.int32(0)))
         fill_up(lists.at[g], counts[g], BLOCKS)
     adds = both_adds(*totals) if outs == 3 else core_adds(*totals)
     add_field(lists, counts, ti, tj, rows, starts, adds, depth, BLOCKS, WIDE)
@@ -165,12 +190,13 @@
     put_rows(ti, tj, 0, OWN, False)
     first[...] = inputs[-2][...]
     second[...] = inputs[-1][...]
+    segments = [[(inputs[n], part) for n, part in sources[g]] for g in range(3)]
+    present = [masks(segments[g]) for g in range(3)]
     count = jnp.int32(0)
     for g in range(3):
-        segments = [(inputs[n], part) for n, part in sources[g]]
-        count = compact(lists, segments, (-8.0, 0.0, 8.0)[g], count)
+        count = compact(lists, segments[g], present[g], (-8.0, 0.0, 8.0)[g], count)
     fill_up(lists, count, 8)
-    k_io = lax.broadcasted_iota(jnp.int32, (1, WIDE), 1).astype(f32)
+    k_io = lax.broadcasted_iota(jnp.int32, (1, EDGE_WIDE), 1).astype(f32)
     dot = functools.partial(jnp.dot, preferred_element_type=f32)
 
     def stage(at, blocks):
@@ -188,18 +214,18 @@
         cz = (-0.5 * LOG2E) / (cols[:, 3:4] * cols[:, 3:4])
 
         def along(b):
-            d = k_io - (z - float(b * WIDE))
+            d = k_io - (z - float(b * EDGE_WIDE))
             return split(jnp.exp2(d * (d * cz)))
 
         nxt = along(0)
-        for b in range(depth // WIDE):
+        for b in range(depth // EDGE_WIDE):
             zh, zl = nxt
-            if b + 1 < depth // WIDE:
+            if b + 1 < depth // EDGE_WIDE:
                 nxt = along(b + 1)
             pp = dot(jnp.concatenate([ph, plo], 0), zh)
             r = pp[:80] + pp[80:] + dot(ph, zl)
-            first[:, b * WIDE:(b + 1) * WIDE] += r[0:40]
-            second[:, b * WIDE:(b + 1) * WIDE] += r[40:80]
+            first[:, b * EDGE_WIDE:(b + 1) * EDGE_WIDE] += r[0:40]
+            second[:, b * EDGE_WIDE:(b + 1) * EDGE_WIDE] += r[40:80]
 
     def step(t, carry):
         stage(t * 8, 8)
@@ -222,14 +248,16 @@
 HBM = pl.BlockSpec(memory_space=pltpu.HBM)
 
 
-def field(name, depth, blocks, sources, arrays, begun=(), outs=3):
+def field(name, depth, blocks, sources, arrays, begun=(), outs=3, keep=False):
     operands = (*arrays, *begun)
     shapes = ((192, depth), (40, depth), (40, depth))[:outs]
     rows, place = sum(CORE_ROWS) + sum(EDGE_ROWS), (3, 27 + 2 * BLOCKS, 8, 128)
-    kernel = functools.partial(field_kernel, sources, bool(begun), outs)
+    kernel = functools.partial(field_kernel, sources, bool(begun), outs, keep)
     if outs == 2:
         shapes, rows, place = ((40, depth),) * 2, EDGE_ROWS[OWN], (81 + 8, 8, 128)
         kernel = functools.partial(edge_field_kernel, sources)
+    if keep:
+        shapes = (arrays[0].shape, *shapes)
     return pl.pallas_call(
         kernel,
         out_shape=[jax.ShapeDtypeStruct(s, f32) for s in shapes],
@@ -322,7 +350,7 @@
         name="pack",
     )(heading[:, 0], offsets, widths, solvation)
     first, second = swapped(first, 0), swapped(second, 1)
-    begun = field("stored", depth, 4, [[(0, 0)], [(0, 1)], [(0, 2)]], [same])
+    same, *begun = field("stored", depth, 4, [[(0, 0)], [(0, 1)], [(0, 2)]], [same], keep=True)
     first, second, *begun = lax.optimization_barrier((first, second, *begun))
     own = jnp.concatenate([same, first, second], axis=1)
     count = lax.axis_size("gx")

time: 47.2 us -> 46.6 us (0.987)
  the two profiles are of different devices: /device:TPU:102 before, /device:TPU:261 now
where the time goes in v7:
time: 46.6 us; the launch traced here: 46.2 us
  starting transfers between devices  22.3 us (48%)
  Pallas kernels  20.3 us (44%)
  waiting for transfers between devices  2.56 us (5%)
  local copies, waits for them, and re-layouts  0.79 us (2%)
    pallas_call x4, Pallas kernels, field(): pl.pallas_call(kernel, out_shape=[jax.ShapeDtypeStruct(s, f32) for s in s...  17.7 us
    ppermute x4, starting transfers between devices, swapped(): return lax.ppermute(value, 'gy', pairs + [(b, a) for a, b in pairs])  12.7 us
    ppermute x1, starting transfers between devices, body(): far = lax.ppermute(far, 'gx', [p for p in ahead if 0 <= p[1] < count])  3.84 us
    ppermute x1, starting transfers between devices, body(): lax.ppermute(own, 'gx', [(r, r + 1 - 2 * (r % 2)) for r in range(count)])  3.14 us
    ppermute x1, starting transfers between devices, body(): near = lax.ppermute(near, 'gx', [p for p in behind if 0 <= p[1] < count])  2.65 us
    ppermute x4, waiting for transfers between devices, swapped(): return lax.ppermute(value, 'gy', pairs + [(b, a) for a, b in pairs])  2.55 us
    pallas_call x1, Pallas kernels, body(): pl.pallas_call(pack_kernel, out_shape=[third] * 3, in_specs=[HBM] * 4, ou...  1.52 us
    pallas_call x1, Pallas kernels, body(): pl.pallas_call(edge_kernel, out_shape=jax.ShapeDtypeStruct(old_map.shape,...  1.07 us
  transfers between devices with their start and end apart: 7, of which 1 were waited for; matrix products, arithmetic and copies ran while one was open for 0% of the time, Pallas kernels for 30%

profile of v7, /device:TPU:261, one launch (start us, length us, event | category | flops | bytes accessed | tf_op | source)
XLA Modules:
  0.0 46.2 jit_solution(5554144721828407453)
XLA Ops:
  0.0 1.5 %pack.1 = (f32[3,3,8,128]{3,2,1,0:T(8,128)}, f32[3,3,8,128]{3,2,1,0:T(8,128)}, f32[3,3,8,128]{3,2,1,0:T(8,128)}) custom-call(s32[12]{0:T(128)} %bitcast.3, f32[12,3,128]{2,1,0:T(4,128)} %refs_1_.1, f32[12,128]{1,0:T(8,128)} %refs_2_.1, f32[12,128]{1,0:T(8,128)} %refs_3_.1), custom_call_target="tpu_custom_call" | custom-call | tf_op jit(solution)/shard_map/pack/pallas_call | solution.py:335
  1.5 3.2 %collective-permute-start = (f32[3,3,8,128]{3,2,1,0:T(8,128)}, f32[3,3,8,128]{3,2,1,0:T(8,128)S(1)}, u32[]{:S(2)}, u32[]{:S(2)}) collective-permute-start(f32[3,3,8,128]{3,2,1,0:T(8,128)} %get-tuple-element.32), channel_id=1, source_target_pairs={{0,1},{2,3},{4,5},{6,7},{8,9},{10,11},{12,13},{14,15},{1,0},{3,2},... | collective-permute-start | bytes 110600 | tf_op jit(solution)/shard_map/ppermute | solution.py:328
  4.7 3.8 %collective-permute-start.1 = (f32[3,3,8,128]{3,2,1,0:T(8,128)}, f32[3,3,8,128]{3,2,1,0:T(8,128)S(1)}, u32[]{:S(2)}, u32[]{:S(2)}) collective-permute-start(f32[3,3,8,128]{3,2,1,0:T(8,128)} %get-tuple-element.33), channel_id=1, source_target_pairs={{1,2},{3,4},{5,6},{7,8},{9,10},{11,12},{13,14},{2,1},{4,3},{6,5},{... | collective-permute-start | bytes 110600 | tf_op jit(solution)/shard_map/ppermute | solution.py:328
  8.5 0.0 copy-start.1
  8.5 0.8 %copy-done.1 = f32[3,3,8,128]{3,2,1,0:T(8,128)S(1)} copy-done((f32[3,3,8,128]{3,2,1,0:T(8,128)S(1)}, f32[3,3,8,128]{3,2,1,0:T(8,128)}, u32[]{:S(2)}) %copy-start.1) | copy-done | bytes 36888
  9.3 3.5 %stored.1 = (f32[3,3,8,128]{3,2,1,0:T(8,128)S(1)}, f32[192,1024]{1,0:T(8,128)S(1)}, f32[40,1024]{1,0:T(8,128)S(1)}, f32[40,1024]{1,0:T(8,128)S(1)}) custom-call(f32[3,3,8,128]{3,2,1,0:T(8,128)S(1)} %copy-done.1), custom_call_target="tpu_custom_call" | custom-call | flops 800000000 | bytes 4000000 | tf_op jit(solution)/shard_map/stored/pallas_call | solution.py:261
  12.8 0.0 collective-permute-done.refs_0_
  12.8 0.0 collective-permute-done.1.refs_1_
  12.9 3.1 %collective-permute-start.2 = (f32[3,9,8,128]{3,2,1,0:T(8,128)S(1)}, f32[3,9,8,128]{3,2,1,0:T(8,128)S(1)}, u32[]{:S(2)}, u32[]{:S(2)}) collective-permute-start(f32[3,9,8,128]{3,2,1,0:T(8,128)S(1)} %constant_dynamic-update-slice_fusion), channel_id=1, source_target_pairs={{0,16},{16,0},{32,48},{48,32},{64,80},{80,64},{96,112},{112,96},{1... | collective-permute-start | bytes 331784 | tf_op jit(solution)/shard_map/ppermute | solution.py:357
  16.0 2.7 %collective-permute-start.4 = (f32[1,9,8,128]{3,2,1,0:T(8,128)S(1)}, f32[1,9,8,128]{3,2,1,0:T(8,128)S(1)}, u32[]{:S(2)}, u32[]{:S(2)}) collective-permute-start(f32[1,9,8,128]{3,2,1,0:T(8,128)S(1)} %get-tuple-element.62), channel_id=1, source_target_pairs={{16,48},{32,0},{48,80},{64,32},{80,112},{96,64},{112,144},{128,96}... | collective-permute-start | bytes 110600 | tf_op jit(solution)/shard_map/ppermute | solution.py:369
  18.7 0.0 collective-permute-done.2
  18.8 3.8 %collective-permute-start.3 = (f32[3,9,8,128]{3,2,1,0:T(8,128)S(1)}, f32[3,9,8,128]{3,2,1,0:T(8,128)S(1)}, u32[]{:S(2)}, u32[]{:S(2)}) collective-permute-start(f32[3,9,8,128]{3,2,1,0:T(8,128)S(1)} %maximum_select_fusion), channel_id=1, source_target_pairs={{0,32},{32,64},{48,16},{64,96},{80,48},{96,128},{112,80},{128,160}... | collective-permute-start | bytes 331784 | tf_op jit(solution)/shard_map/ppermute | solution.py:368
  22.6 5.9 %chip.1 = (f32[192,1024]{1,0:T(8,128)S(1)}, f32[40,1024]{1,0:T(8,128)S(1)}, f32[40,1024]{1,0:T(8,128)S(1)}) custom-call(f32[3,3,8,128]{3,2,1,0:T(8,128)S(1)} %collective-permute-done.refs_0_, f32[3,3,8,128]{3,2,1,0:T(8,128)S(1)} %collective-permute-done.1.refs_1_, f32[3,9,8,128]{3,2,1,0:T(8,128)S(1)} %pad_maximum_fusion.refs_2_, ...), custom_call_target="tpu_custom_call" | custom-call | flops 3200000000 | bytes 4000000 | tf_op jit(solution)/shard_map/chip/pallas_call | solution.py:261
  28.6 0.0 collective-permute-done.4
  28.6 0.0 collective-permute-done.3.refs_2_
  28.6 3.9 %rest_edges.1 = (f32[40,1024]{1,0:T(8,128)S(1)}, f32[40,1024]{1,0:T(8,128)S(1)}) custom-call(f32[2,9,8,128]{3,2,1,0:T(8,128)S(1)} %get-tuple-element.56.refs_0_, f32[2,9,8,128]{3,2,1,0:T(8,128)S(1)} %get-tuple-element.55.refs_1_, f32[3,9,8,128]{3,2,1,0:T(8,128)S(1)} %collective-permute-done.3.refs_2_, f32[40,1024]{1,0:T(8,128)S(1)} %get-tuple-element.48.refs_3_, ...), custom_call_target="tpu_custom_call" | custom-call | flops 3200000000 | bytes 4000000 | tf_op jit(solution)/shard_map/rest_edges/pallas_call | solution.py:261
  32.5 2.3 %collective-permute-start.5 = (f32[40,1024]{1,0:T(8,128)S(1)}, f32[40,1024]{1,0:T(8,128)S(1)}, u32[]{:S(2)}, u32[]{:S(2)}) collective-permute-start(f32[40,1024]{1,0:T(8,128)S(1)} %get-tuple-element.50), channel_id=1, source_target_pairs={{0,1},{2,3},{4,5},{6,7},{8,9},{10,11},{12,13},{14,15},{1,0},{3,2},... | collective-permute-start | bytes 491528 | tf_op jit(solution)/shard_map/ppermute | solution.py:328
  34.9 0.0 copy-start
  34.9 3.3 %collective-permute-start.6 = (f32[40,1024]{1,0:T(8,128)S(1)}, f32[40,1024]{1,0:T(8,128)S(1)}, u32[]{:S(2)}, u32[]{:S(2)}) collective-permute-start(f32[40,1024]{1,0:T(8,128)S(1)} %get-tuple-element.51), channel_id=1, source_target_pairs={{1,2},{3,4},{5,6},{7,8},{9,10},{11,12},{13,14},{2,1},{4,3},{6,5},{... | collective-permute-start | bytes 491528 | tf_op jit(solution)/shard_map/ppermute | solution.py:328
  38.2 4.4 %rest_core.1 = f32[192,1024]{1,0:T(8,128)S(1)} custom-call(f32[2,9,8,128]{3,2,1,0:T(8,128)S(1)} %get-tuple-element.56.refs_0_, f32[2,9,8,128]{3,2,1,0:T(8,128)S(1)} %get-tuple-element.55.refs_1_, f32[3,9,8,128]{3,2,1,0:T(8,128)S(1)} %collective-permute-done.3.refs_2_, f32[192,1024]{1,0:T(8,128)S(1)} %get-tuple-element.47.refs_3_), custom_call_target="tpu_custom_call" | custom-call | flops 3200000000 | bytes 4000000 | tf_op jit(solution)/shard_map/rest_core/pallas_call | solution.py:261
  42.6 0.0 collective-permute-done.5.first
  42.6 2.5 %collective-permute-done.6.second = f32[40,1024]{1,0:T(8,128)S(1)} collective-permute-done((f32[40,1024]{1,0:T(8,128)S(1)}, f32[40,1024]{1,0:T(8,128)S(1)}, u32[]{:S(2)}, u32[]{:S(2)}) %collective-permute-start.6) | collective-permute-done | bytes 163872 | tf_op jit(solution)/shard_map/ppermute | solution.py:328
  45.2 0.0 copy-done
  45.2 1.1 %edges.1 = f32[8,24,1024]{2,1,0:T(8,128)} custom-call(f32[8,24,1024]{2,1,0:T(8,128)S(1)} %bitcast.2, f32[8,24,1024]{2,1,0:T(8,128)S(1)} %copy-done, f32[40,1024]{1,0:T(8,128)S(1)} %collective-permute-done.5.first, f32[40,1024]{1,0:T(8,128)S(1)} %collective-permute-done.6.second), custom_call_target="tpu_custom_call" | custom-call | tf_op jit(solution)/shard_map/edges/pallas_call | solution.py:389
  (9 shorter events, 0.1 us)
Async XLA Ops:
  1.5 11.3 %collective-permute-start = (f32[3,3,8,128]{3,2,1,0:T(8,128)}, f32[3,3,8,128]{3,2,1,0:T(8,128)S(1)}, u32[]{:S(2)}, u32[]{:S(2)}) collective-permute-start(f32[3,3,8,128]{3,2,1,0:T(8,128)} %get-tuple-element.32), channel_id=1, source_target_pairs={{0,1},{2,3},{4,5},{6,7},{8,9},{10,11},{12,13},{14,15},{1,0},{3,2},... | collective-permute-start | bytes 110600 | tf_op jit(solution)/shard_map/ppermute | solution.py:328
  4.7 8.1 %collective-permute-start.1 = (f32[3,3,8,128]{3,2,1,0:T(8,128)}, f32[3,3,8,128]{3,2,1,0:T(8,128)S(1)}, u32[]{:S(2)}, u32[]{:S(2)}) collective-permute-start(f32[3,3,8,128]{3,2,1,0:T(8,128)} %get-tuple-element.33), channel_id=1, source_target_pairs={{1,2},{3,4},{5,6},{7,8},{9,10},{11,12},{13,14},{2,1},{4,3},{6,5},{... | collective-permute-start | bytes 110600 | tf_op jit(solution)/shard_map/ppermute | solution.py:328
  8.5 0.8 %copy-start.1 = (f32[3,3,8,128]{3,2,1,0:T(8,128)S(1)}, f32[3,3,8,128]{3,2,1,0:T(8,128)}, u32[]{:S(2)}) copy-start(f32[3,3,8,128]{3,2,1,0:T(8,128)} %get-tuple-element.30.refs_0_) | copy-start | bytes 110596
  12.9 5.8 %collective-permute-start.2 = (f32[3,9,8,128]{3,2,1,0:T(8,128)S(1)}, f32[3,9,8,128]{3,2,1,0:T(8,128)S(1)}, u32[]{:S(2)}, u32[]{:S(2)}) collective-permute-start(f32[3,9,8,128]{3,2,1,0:T(8,128)S(1)} %constant_dynamic-update-slice_fusion), channel_id=1, source_target_pairs={{0,16},{16,0},{32,48},{48,32},{64,80},{80,64},{96,112},{112,96},{1... | collective-permute-start | bytes 331784 | tf_op jit(solution)/shard_map/ppermute | solution.py:357
  16.0 12.5 %collective-permute-start.4 = (f32[1,9,8,128]{3,2,1,0:T(8,128)S(1)}, f32[1,9,8,128]{3,2,1,0:T(8,128)S(1)}, u32[]{:S(2)}, u32[]{:S(2)}) collective-permute-start(f32[1,9,8,128]{3,2,1,0:T(8,128)S(1)} %get-tuple-element.62), channel_id=1, source_target_pairs={{16,48},{32,0},{48,80},{64,32},{80,112},{96,64},{112,144},{128,96}... | collective-permute-start | bytes 110600 | tf_op jit(solution)/shard_map/ppermute | solution.py:369
  18.8 9.8 %collective-permute-start.3 = (f32[3,9,8,128]{3,2,1,0:T(8,128)S(1)}, f32[3,9,8,128]{3,2,1,0:T(8,128)S(1)}, u32[]{:S(2)}, u32[]{:S(2)}) collective-permute-start(f32[3,9,8,128]{3,2,1,0:T(8,128)S(1)} %maximum_select_fusion), channel_id=1, source_target_pairs={{0,32},{32,64},{48,16},{64,96},{80,48},{96,128},{112,80},{128,160}... | collective-permute-start | bytes 331784 | tf_op jit(solution)/shard_map/ppermute | solution.py:368
  32.5 10.1 %collective-permute-start.5 = (f32[40,1024]{1,0:T(8,128)S(1)}, f32[40,1024]{1,0:T(8,128)S(1)}, u32[]{:S(2)}, u32[]{:S(2)}) collective-permute-start(f32[40,1024]{1,0:T(8,128)S(1)} %get-tuple-element.50), channel_id=1, source_target_pairs={{0,1},{2,3},{4,5},{6,7},{8,9},{10,11},{12,13},{14,15},{1,0},{3,2},... | collective-permute-start | bytes 491528 | tf_op jit(solution)/shard_map/ppermute | solution.py:328
  34.9 10.3 %copy-start = (f32[8,24,1024]{2,1,0:T(8,128)S(1)}, f32[8,24,1024]{2,1,0:T(8,128)}, u32[]{:S(2)}) copy-start(f32[8,24,1024]{2,1,0:T(8,128)} %old.1) | copy-start | bytes 2359300
  34.9 10.3 %collective-permute-start.6 = (f32[40,1024]{1,0:T(8,128)S(1)}, f32[40,1024]{1,0:T(8,128)S(1)}, u32[]{:S(2)}, u32[]{:S(2)}) collective-permute-start(f32[40,1024]{1,0:T(8,128)S(1)} %get-tuple-element.51), channel_id=1, source_target_pairs={{1,2},{3,4},{5,6},{7,8},{9,10},{11,12},{13,14},{2,1},{4,3},{6,5},{... | collective-permute-start | bytes 491528 | tf_op jit(solution)/shard_map/ppermute | solution.py:328

commit v8 on v7

--- a/solution.py
+++ b/solution.py
@@ -227,12 +227,19 @@
             first[:, b * EDGE_WIDE:(b + 1) * EDGE_WIDE] += r[0:40]
             second[:, b * EDGE_WIDE:(b + 1) * EDGE_WIDE] += r[40:80]
 
-    def step(t, carry):
-        stage(t * 8, 8)
+    def two(t, carry):
+        stage(t * 16, 8)
+        stage(t * 16 + 8, 8)
         return carry
 
+    twos = lax.shift_right_logical(count + 1, 4)
+    lax.fori_loop(0, twos, two, 0)
     whole = lax.shift_right_logical(count + 1, 3)
-    lax.fori_loop(0, whole, step, 0)
+
+    @pl.when(whole > twos * 2)
+    def _():
+        stage(twos * 16, 8)
+
     after = count - whole * 8
 
     @pl.when(after > 2)

time: 46.6 us -> 46.5 us (level)
  the two profiles are of different devices: /device:TPU:261 before, /device:TPU:135 now
where the time goes in v8:
time: 46.5 us; the launch traced here: 46.1 us
  starting transfers between devices  23.2 us (50%)
  Pallas kernels  20.7 us (45%)
  waiting for transfers between devices  1.16 us (2%)
  local copies, waits for them, and re-layouts  0.79 us (2%)
    pallas_call x4, Pallas kernels, field(): pl.pallas_call(kernel, out_shape=[jax.ShapeDtypeStruct(s, f32) for s in s...  18.1 us
    ppermute x4, starting transfers between devices, swapped(): return lax.ppermute(value, 'gy', pairs + [(b, a) for a, b in pairs])  13.4 us
    ppermute x1, starting transfers between devices, body(): near = lax.ppermute(near, 'gx', [p for p in behind if 0 <= p[1] < count])  3.55 us
    ppermute x1, starting transfers between devices, body(): lax.ppermute(own, 'gx', [(r, r + 1 - 2 * (r % 2)) for r in range(count)])  3.27 us
    ppermute x1, starting transfers between devices, body(): far = lax.ppermute(far, 'gx', [p for p in ahead if 0 <= p[1] < count])  2.95 us
    pallas_call x1, Pallas kernels, body(): pl.pallas_call(pack_kernel, out_shape=[third] * 3, in_specs=[HBM] * 4, ou...  1.51 us
    ppermute x4, waiting for transfers between devices, swapped(): return lax.ppermute(value, 'gy', pairs + [(b, a) for a, b in pairs])  1.15 us
    pallas_call x1, Pallas kernels, body(): pl.pallas_call(edge_kernel, out_shape=jax.ShapeDtypeStruct(old_map.shape,...  1.07 us
  transfers between devices with their start and end apart: 7, of which 1 were waited for; matrix products, arithmetic and copies ran while one was open for 0% of the time, Pallas kernels for 31%

profile of v8, /device:TPU:135, one launch (start us, length us, event | category | flops | bytes accessed | tf_op | source)
XLA Modules:
  0.0 46.1 jit_solution(1679366994489450334)
XLA Ops:
  0.0 1.5 %pack.1 = (f32[3,3,8,128]{3,2,1,0:T(8,128)}, f32[3,3,8,128]{3,2,1,0:T(8,128)}, f32[3,3,8,128]{3,2,1,0:T(8,128)}) custom-call(s32[12]{0:T(128)} %bitcast.3, f32[12,3,128]{2,1,0:T(4,128)} %refs_1_.1, f32[12,128]{1,0:T(8,128)} %refs_2_.1, f32[12,128]{1,0:T(8,128)} %refs_3_.1), custom_call_target="tpu_custom_call" | custom-call | tf_op jit(solution)/shard_map/pack/pallas_call | solution.py:342
  1.5 3.2 %collective-permute-start = (f32[3,3,8,128]{3,2,1,0:T(8,128)}, f32[3,3,8,128]{3,2,1,0:T(8,128)S(1)}, u32[]{:S(2)}, u32[]{:S(2)}) collective-permute-start(f32[3,3,8,128]{3,2,1,0:T(8,128)} %get-tuple-element.32), channel_id=1, source_target_pairs={{0,1},{2,3},{4,5},{6,7},{8,9},{10,11},{12,13},{14,15},{1,0},{3,2},... | collective-permute-start | bytes 110600 | tf_op jit(solution)/shard_map/ppermute | solution.py:335
  4.7 4.1 %collective-permute-start.1 = (f32[3,3,8,128]{3,2,1,0:T(8,128)}, f32[3,3,8,128]{3,2,1,0:T(8,128)S(1)}, u32[]{:S(2)}, u32[]{:S(2)}) collective-permute-start(f32[3,3,8,128]{3,2,1,0:T(8,128)} %get-tuple-element.33), channel_id=1, source_target_pairs={{1,2},{3,4},{5,6},{7,8},{9,10},{11,12},{13,14},{2,1},{4,3},{6,5},{... | collective-permute-start | bytes 110600 | tf_op jit(solution)/shard_map/ppermute | solution.py:335
  8.8 0.0 copy-start.1
  8.8 0.8 %copy-done.1 = f32[3,3,8,128]{3,2,1,0:T(8,128)S(1)} copy-done((f32[3,3,8,128]{3,2,1,0:T(8,128)S(1)}, f32[3,3,8,128]{3,2,1,0:T(8,128)}, u32[]{:S(2)}) %copy-start.1) | copy-done | bytes 36888
  9.6 2.9 %stored.1 = (f32[3,3,8,128]{3,2,1,0:T(8,128)S(1)}, f32[192,1024]{1,0:T(8,128)S(1)}, f32[40,1024]{1,0:T(8,128)S(1)}, f32[40,1024]{1,0:T(8,128)S(1)}) custom-call(f32[3,3,8,128]{3,2,1,0:T(8,128)S(1)} %copy-done.1), custom_call_target="tpu_custom_call" | custom-call | flops 800000000 | bytes 4000000 | tf_op jit(solution)/shard_map/stored/pallas_call | solution.py:268
  12.5 0.0 collective-permute-done.refs_0_
  12.5 0.0 collective-permute-done.1.refs_1_
  12.5 3.3 %collective-permute-start.2 = (f32[3,9,8,128]{3,2,1,0:T(8,128)S(1)}, f32[3,9,8,128]{3,2,1,0:T(8,128)S(1)}, u32[]{:S(2)}, u32[]{:S(2)}) collective-permute-start(f32[3,9,8,128]{3,2,1,0:T(8,128)S(1)} %constant_dynamic-update-slice_fusion), channel_id=1, source_target_pairs={{0,16},{16,0},{32,48},{48,32},{64,80},{80,64},{96,112},{112,96},{1... | collective-permute-start | bytes 331784 | tf_op jit(solution)/shard_map/ppermute | solution.py:364
  15.8 3.5 %collective-permute-start.4 = (f32[1,9,8,128]{3,2,1,0:T(8,128)S(1)}, f32[1,9,8,128]{3,2,1,0:T(8,128)S(1)}, u32[]{:S(2)}, u32[]{:S(2)}) collective-permute-start(f32[1,9,8,128]{3,2,1,0:T(8,128)S(1)} %get-tuple-element.62), channel_id=1, source_target_pairs={{16,48},{32,0},{48,80},{64,32},{80,112},{96,64},{112,144},{128,96}... | collective-permute-start | bytes 110600 | tf_op jit(solution)/shard_map/ppermute | solution.py:376
  19.4 0.0 collective-permute-done.2
  19.4 2.9 %collective-permute-start.3 = (f32[3,9,8,128]{3,2,1,0:T(8,128)S(1)}, f32[3,9,8,128]{3,2,1,0:T(8,128)S(1)}, u32[]{:S(2)}, u32[]{:S(2)}) collective-permute-start(f32[3,9,8,128]{3,2,1,0:T(8,128)S(1)} %maximum_select_fusion), channel_id=1, source_target_pairs={{0,32},{32,64},{48,16},{64,96},{80,48},{96,128},{112,80},{128,160}... | collective-permute-start | bytes 331784 | tf_op jit(solution)/shard_map/ppermute | solution.py:375
  22.4 6.6 %chip.1 = (f32[192,1024]{1,0:T(8,128)S(1)}, f32[40,1024]{1,0:T(8,128)S(1)}, f32[40,1024]{1,0:T(8,128)S(1)}) custom-call(f32[3,3,8,128]{3,2,1,0:T(8,128)S(1)} %collective-permute-done.refs_0_, f32[3,3,8,128]{3,2,1,0:T(8,128)S(1)} %collective-permute-done.1.refs_1_, f32[3,9,8,128]{3,2,1,0:T(8,128)S(1)} %pad_maximum_fusion.refs_2_, ...), custom_call_target="tpu_custom_call" | custom-call | flops 3200000000 | bytes 4000000 | tf_op jit(solution)/shard_map/chip/pallas_call | solution.py:268
  29.0 0.0 collective-permute-done.4
  29.0 0.0 collective-permute-done.3.refs_2_
  29.0 3.8 %rest_edges.1 = (f32[40,1024]{1,0:T(8,128)S(1)}, f32[40,1024]{1,0:T(8,128)S(1)}) custom-call(f32[2,9,8,128]{3,2,1,0:T(8,128)S(1)} %get-tuple-element.56.refs_0_, f32[2,9,8,128]{3,2,1,0:T(8,128)S(1)} %get-tuple-element.55.refs_1_, f32[3,9,8,128]{3,2,1,0:T(8,128)S(1)} %collective-permute-done.3.refs_2_, f32[40,1024]{1,0:T(8,128)S(1)} %get-tuple-element.48.refs_3_, ...), custom_call_target="tpu_custom_call" | custom-call | flops 3200000000 | bytes 4000000 | tf_op jit(solution)/shard_map/rest_edges/pallas_call | solution.py:268
  32.8 1.9 %collective-permute-start.5 = (f32[40,1024]{1,0:T(8,128)S(1)}, f32[40,1024]{1,0:T(8,128)S(1)}, u32[]{:S(2)}, u32[]{:S(2)}) collective-permute-start(f32[40,1024]{1,0:T(8,128)S(1)} %get-tuple-element.50), channel_id=1, source_target_pairs={{0,1},{2,3},{4,5},{6,7},{8,9},{10,11},{12,13},{14,15},{1,0},{3,2},... | collective-permute-start | bytes 491528 | tf_op jit(solution)/shard_map/ppermute | solution.py:335
  34.8 0.0 copy-start
  34.8 4.2 %collective-permute-start.6 = (f32[40,1024]{1,0:T(8,128)S(1)}, f32[40,1024]{1,0:T(8,128)S(1)}, u32[]{:S(2)}, u32[]{:S(2)}) collective-permute-start(f32[40,1024]{1,0:T(8,128)S(1)} %get-tuple-element.51), channel_id=1, source_target_pairs={{1,2},{3,4},{5,6},{7,8},{9,10},{11,12},{13,14},{2,1},{4,3},{6,5},{... | collective-permute-start | bytes 491528 | tf_op jit(solution)/shard_map/ppermute | solution.py:335
  39.0 4.9 %rest_core.1 = f32[192,1024]{1,0:T(8,128)S(1)} custom-call(f32[2,9,8,128]{3,2,1,0:T(8,128)S(1)} %get-tuple-element.56.refs_0_, f32[2,9,8,128]{3,2,1,0:T(8,128)S(1)} %get-tuple-element.55.refs_1_, f32[3,9,8,128]{3,2,1,0:T(8,128)S(1)} %collective-permute-done.3.refs_2_, f32[192,1024]{1,0:T(8,128)S(1)} %get-tuple-element.47.refs_3_), custom_call_target="tpu_custom_call" | custom-call | flops 3200000000 | bytes 4000000 | tf_op jit(solution)/shard_map/rest_core/pallas_call | solution.py:268
  43.9 0.0 collective-permute-done.5.first
  43.9 1.1 %collective-permute-done.6.second = f32[40,1024]{1,0:T(8,128)S(1)} collective-permute-done((f32[40,1024]{1,0:T(8,128)S(1)}, f32[40,1024]{1,0:T(8,128)S(1)}, u32[]{:S(2)}, u32[]{:S(2)}) %collective-permute-start.6) | collective-permute-done | bytes 163872 | tf_op jit(solution)/shard_map/ppermute | solution.py:335
  45.0 0.0 copy-done
  45.0 1.1 %edges.1 = f32[8,24,1024]{2,1,0:T(8,128)} custom-call(f32[8,24,1024]{2,1,0:T(8,128)S(1)} %bitcast.2, f32[8,24,1024]{2,1,0:T(8,128)S(1)} %copy-done, f32[40,1024]{1,0:T(8,128)S(1)} %collective-permute-done.5.first, f32[40,1024]{1,0:T(8,128)S(1)} %collective-permute-done.6.second), custom_call_target="tpu_custom_call" | custom-call | tf_op jit(solution)/shard_map/edges/pallas_call | solution.py:396
  (9 shorter events, 0.1 us)
Async XLA Ops:
  1.5 10.9 %collective-permute-start = (f32[3,3,8,128]{3,2,1,0:T(8,128)}, f32[3,3,8,128]{3,2,1,0:T(8,128)S(1)}, u32[]{:S(2)}, u32[]{:S(2)}) collective-permute-start(f32[3,3,8,128]{3,2,1,0:T(8,128)} %get-tuple-element.32), channel_id=1, source_target_pairs={{0,1},{2,3},{4,5},{6,7},{8,9},{10,11},{12,13},{14,15},{1,0},{3,2},... | collective-permute-start | bytes 110600 | tf_op jit(solution)/shard_map/ppermute | solution.py:335
  4.7 7.7 %collective-permute-start.1 = (f32[3,3,8,128]{3,2,1,0:T(8,128)}, f32[3,3,8,128]{3,2,1,0:T(8,128)S(1)}, u32[]{:S(2)}, u32[]{:S(2)}) collective-permute-start(f32[3,3,8,128]{3,2,1,0:T(8,128)} %get-tuple-element.33), channel_id=1, source_target_pairs={{1,2},{3,4},{5,6},{7,8},{9,10},{11,12},{13,14},{2,1},{4,3},{6,5},{... | collective-permute-start | bytes 110600 | tf_op jit(solution)/shard_map/ppermute | solution.py:335
  8.8 0.8 %copy-start.1 = (f32[3,3,8,128]{3,2,1,0:T(8,128)S(1)}, f32[3,3,8,128]{3,2,1,0:T(8,128)}, u32[]{:S(2)}) copy-start(f32[3,3,8,128]{3,2,1,0:T(8,128)} %get-tuple-element.30.refs_0_) | copy-start | bytes 110596
  12.5 6.9 %collective-permute-start.2 = (f32[3,9,8,128]{3,2,1,0:T(8,128)S(1)}, f32[3,9,8,128]{3,2,1,0:T(8,128)S(1)}, u32[]{:S(2)}, u32[]{:S(2)}) collective-permute-start(f32[3,9,8,128]{3,2,1,0:T(8,128)S(1)} %constant_dynamic-update-slice_fusion), channel_id=1, source_target_pairs={{0,16},{16,0},{32,48},{48,32},{64,80},{80,64},{96,112},{112,96},{1... | collective-permute-start | bytes 331784 | tf_op jit(solution)/shard_map/ppermute | solution.py:364
  15.8 13.2 %collective-permute-start.4 = (f32[1,9,8,128]{3,2,1,0:T(8,128)S(1)}, f32[1,9,8,128]{3,2,1,0:T(8,128)S(1)}, u32[]{:S(2)}, u32[]{:S(2)}) collective-permute-start(f32[1,9,8,128]{3,2,1,0:T(8,128)S(1)} %get-tuple-element.62), channel_id=1, source_target_pairs={{16,48},{32,0},{48,80},{64,32},{80,112},{96,64},{112,144},{128,96}... | collective-permute-start | bytes 110600 | tf_op jit(solution)/shard_map/ppermute | solution.py:376
  19.4 9.6 %collective-permute-start.3 = (f32[3,9,8,128]{3,2,1,0:T(8,128)S(1)}, f32[3,9,8,128]{3,2,1,0:T(8,128)S(1)}, u32[]{:S(2)}, u32[]{:S(2)}) collective-permute-start(f32[3,9,8,128]{3,2,1,0:T(8,128)S(1)} %maximum_select_fusion), channel_id=1, source_target_pairs={{0,32},{32,64},{48,16},{64,96},{80,48},{96,128},{112,80},{128,160}... | collective-permute-start | bytes 331784 | tf_op jit(solution)/shard_map/ppermute | solution.py:375
  32.8 11.1 %collective-permute-start.5 = (f32[40,1024]{1,0:T(8,128)S(1)}, f32[40,1024]{1,0:T(8,128)S(1)}, u32[]{:S(2)}, u32[]{:S(2)}) collective-permute-start(f32[40,1024]{1,0:T(8,128)S(1)} %get-tuple-element.50), channel_id=1, source_target_pairs={{0,1},{2,3},{4,5},{6,7},{8,9},{10,11},{12,13},{14,15},{1,0},{3,2},... | collective-permute-start | bytes 491528 | tf_op jit(solution)/shard_map/ppermute | solution.py:335
  34.8 10.3 %copy-start = (f32[8,24,1024]{2,1,0:T(8,128)S(1)}, f32[8,24,1024]{2,1,0:T(8,128)}, u32[]{:S(2)}) copy-start(f32[8,24,1024]{2,1,0:T(8,128)} %old.1) | copy-start | bytes 2359300
  34.8 10.2 %collective-permute-start.6 = (f32[40,1024]{1,0:T(8,128)S(1)}, f32[40,1024]{1,0:T(8,128)S(1)}, u32[]{:S(2)}, u32[]{:S(2)}) collective-permute-start(f32[40,1024]{1,0:T(8,128)S(1)} %get-tuple-element.51), channel_id=1, source_target_pairs={{1,2},{3,4},{5,6},{7,8},{9,10},{11,12},{13,14},{2,1},{4,3},{6,5},{... | collective-permute-start | bytes 491528 | tf_op jit(solution)/shard_map/ppermute | solution.py:335

commit v9 on v8

--- a/solution.py
+++ b/solution.py
@@ -34,7 +34,7 @@
     side = m >= n // 2
     e = jnp.where(side, m - n // 2, m) + (8 if group == BELOW else 0)
     i = quotient(e, 5)
-    right = jnp.logical_xor(side, lax.rem(lax.axis_index("gy"), 2) == 0)
+    right = jnp.logical_xor(side, lax.rem(lax.axis_index("gy"), 2) == 1)
     j = e - i * 5 + jnp.where(right, 24, -W)
     place = (i + (8, 0, -8)[group]).astype(f32)
     if group == ABOVE:
@@ -323,11 +323,11 @@
 
     @pl.when(even)
     def _():
-        add(second, first)
+        add(first, second)
 
     @pl.when(jnp.logical_not(even))
     def _():
-        add(first, second)
+        add(second, first)
 
 
 def swapped(value, start):
@@ -390,7 +390,7 @@
     above, below = jnp.where(even, far[0:2], one), jnp.where(even, one, far[0:2])
     sources, arrays = [[(0, 0), (0, 1)], [(2, 2)], [(1, 0), (1, 1)]], [above, below, far]
     edges = field("rest_edges", depth, 16, sources, arrays, begun[1:], 2)
-    first, second = swapped(edges[0], 0), swapped(edges[1], 1)
+    first, second = swapped(edges[0], 1), swapped(edges[1], 0)
     (core,) = field("rest_core", depth, 16, sources, arrays, begun[:1], 1)
     core, first, second = lax.optimization_barrier((core, first, second))
     return pl.pallas_call(

time: 46.5 us -> 46.3 us (level)
  starting transfers between devices: 23.2 us -> 22.7 us
  transfers between devices with their start and end apart: 7 -> 7, of which waited for: 1 -> 1; matrix products, arithmetic and copies ran while one was open for 0% -> 0% of each run, Pallas kernels for 31% -> 30%
where the time goes in v9:
time: 46.3 us; the launch traced here: 45.7 us
  starting transfers between devices  22.7 us (49%)
  Pallas kernels  20.3 us (44%)
  waiting for transfers between devices  1.58 us (3%)
  local copies, waits for them, and re-layouts  0.79 us (2%)
    pallas_call x4, Pallas kernels, field(): pl.pallas_call(kernel, out_shape=[jax.ShapeDtypeStruct(s, f32) for s in s...  17.7 us
    ppermute x4, starting transfers between devices, swapped(): return lax.ppermute(value, 'gy', pairs + [(b, a) for a, b in pairs])  13.1 us
    ppermute x1, starting transfers between devices, body(): near = lax.ppermute(near, 'gx', [p for p in behind if 0 <= p[1] < count])  3.54 us
    ppermute x1, starting transfers between devices, body(): lax.ppermute(own, 'gx', [(r, r + 1 - 2 * (r % 2)) for r in range(count)])  3.14 us
    ppermute x1, starting transfers between devices, body(): far = lax.ppermute(far, 'gx', [p for p in ahead if 0 <= p[1] < count])  2.95 us
    ppermute x4, waiting for transfers between devices, swapped(): return lax.ppermute(value, 'gy', pairs + [(b, a) for a, b in pairs])  1.57 us
    pallas_call x1, Pallas kernels, body(): pl.pallas_call(pack_kernel, out_shape=[third] * 3, in_specs=[HBM] * 4, ou...  1.51 us
    pallas_call x1, Pallas kernels, body(): pl.pallas_call(edge_kernel, out_shape=jax.ShapeDtypeStruct(old_map.shape,...  1.07 us
  transfers between devices with their start and end apart: 7, of which 1 were waited for; matrix products, arithmetic and copies ran while one was open for 0% of the time, Pallas kernels for 30%

profile of v9, /device:TPU:135, one launch (start us, length us, event | category | flops | bytes accessed | tf_op | source)
XLA Modules:
  0.0 45.7 jit_solution(17631617743730942626)
XLA Ops:
  0.0 1.5 %pack.1 = (f32[3,3,8,128]{3,2,1,0:T(8,128)}, f32[3,3,8,128]{3,2,1,0:T(8,128)}, f32[3,3,8,128]{3,2,1,0:T(8,128)}) custom-call(s32[12]{0:T(128)} %bitcast.3, f32[12,3,128]{2,1,0:T(4,128)} %refs_1_.1, f32[12,128]{1,0:T(8,128)} %refs_2_.1, f32[12,128]{1,0:T(8,128)} %refs_3_.1), custom_call_target="tpu_custom_call" | custom-call | tf_op jit(solution)/shard_map/pack/pallas_call | solution.py:342
  1.5 3.2 %collective-permute-start = (f32[3,3,8,128]{3,2,1,0:T(8,128)}, f32[3,3,8,128]{3,2,1,0:T(8,128)S(1)}, u32[]{:S(2)}, u32[]{:S(2)}) collective-permute-start(f32[3,3,8,128]{3,2,1,0:T(8,128)} %get-tuple-element.32), channel_id=1, source_target_pairs={{0,1},{2,3},{4,5},{6,7},{8,9},{10,11},{12,13},{14,15},{1,0},{3,2},... | collective-permute-start | bytes 110600 | tf_op jit(solution)/shard_map/ppermute | solution.py:335
  4.7 4.1 %collective-permute-start.1 = (f32[3,3,8,128]{3,2,1,0:T(8,128)}, f32[3,3,8,128]{3,2,1,0:T(8,128)S(1)}, u32[]{:S(2)}, u32[]{:S(2)}) collective-permute-start(f32[3,3,8,128]{3,2,1,0:T(8,128)} %get-tuple-element.33), channel_id=1, source_target_pairs={{1,2},{3,4},{5,6},{7,8},{9,10},{11,12},{13,14},{2,1},{4,3},{6,5},{... | collective-permute-start | bytes 110600 | tf_op jit(solution)/shard_map/ppermute | solution.py:335
  8.8 0.0 copy-start.1
  8.8 0.8 %copy-done.1 = f32[3,3,8,128]{3,2,1,0:T(8,128)S(1)} copy-done((f32[3,3,8,128]{3,2,1,0:T(8,128)S(1)}, f32[3,3,8,128]{3,2,1,0:T(8,128)}, u32[]{:S(2)}) %copy-start.1) | copy-done | bytes 36888
  9.6 3.3 %stored.1 = (f32[3,3,8,128]{3,2,1,0:T(8,128)S(1)}, f32[192,1024]{1,0:T(8,128)S(1)}, f32[40,1024]{1,0:T(8,128)S(1)}, f32[40,1024]{1,0:T(8,128)S(1)}) custom-call(f32[3,3,8,128]{3,2,1,0:T(8,128)S(1)} %copy-done.1), custom_call_target="tpu_custom_call" | custom-call | flops 800000000 | bytes 4000000 | tf_op jit(solution)/shard_map/stored/pallas_call | solution.py:268
  12.9 0.0 collective-permute-done.refs_0_
  12.9 0.0 collective-permute-done.1.refs_1_
  13.0 3.1 %collective-permute-start.2 = (f32[3,9,8,128]{3,2,1,0:T(8,128)S(1)}, f32[3,9,8,128]{3,2,1,0:T(8,128)S(1)}, u32[]{:S(2)}, u32[]{:S(2)}) collective-permute-start(f32[3,9,8,128]{3,2,1,0:T(8,128)S(1)} %constant_dynamic-update-slice_fusion), channel_id=1, source_target_pairs={{0,16},{16,0},{32,48},{48,32},{64,80},{80,64},{96,112},{112,96},{1... | collective-permute-start | bytes 331784 | tf_op jit(solution)/shard_map/ppermute | solution.py:364
  16.1 3.5 %collective-permute-start.4 = (f32[1,9,8,128]{3,2,1,0:T(8,128)S(1)}, f32[1,9,8,128]{3,2,1,0:T(8,128)S(1)}, u32[]{:S(2)}, u32[]{:S(2)}) collective-permute-start(f32[1,9,8,128]{3,2,1,0:T(8,128)S(1)} %get-tuple-element.62), channel_id=1, source_target_pairs={{16,48},{32,0},{48,80},{64,32},{80,112},{96,64},{112,144},{128,96}... | collective-permute-start | bytes 110600 | tf_op jit(solution)/shard_map/ppermute | solution.py:376
  19.7 0.0 collective-permute-done.2
  19.8 3.0 %collective-permute-start.3 = (f32[3,9,8,128]{3,2,1,0:T(8,128)S(1)}, f32[3,9,8,128]{3,2,1,0:T(8,128)S(1)}, u32[]{:S(2)}, u32[]{:S(2)}) collective-permute-start(f32[3,9,8,128]{3,2,1,0:T(8,128)S(1)} %maximum_select_fusion), channel_id=1, source_target_pairs={{0,32},{32,64},{48,16},{64,96},{80,48},{96,128},{112,80},{128,160}... | collective-permute-start | bytes 331784 | tf_op jit(solution)/shard_map/ppermute | solution.py:375
  22.7 6.1 %chip.1 = (f32[192,1024]{1,0:T(8,128)S(1)}, f32[40,1024]{1,0:T(8,128)S(1)}, f32[40,1024]{1,0:T(8,128)S(1)}) custom-call(f32[3,3,8,128]{3,2,1,0:T(8,128)S(1)} %collective-permute-done.refs_0_, f32[3,3,8,128]{3,2,1,0:T(8,128)S(1)} %collective-permute-done.1.refs_1_, f32[3,9,8,128]{3,2,1,0:T(8,128)S(1)} %pad_maximum_fusion.refs_2_, ...), custom_call_target="tpu_custom_call" | custom-call | flops 3200000000 | bytes 4000000 | tf_op jit(solution)/shard_map/chip/pallas_call | solution.py:268
  28.9 0.0 collective-permute-done.4
  28.9 0.0 collective-permute-done.3.refs_2_
  28.9 3.8 %rest_edges.1 = (f32[40,1024]{1,0:T(8,128)S(1)}, f32[40,1024]{1,0:T(8,128)S(1)}) custom-call(f32[2,9,8,128]{3,2,1,0:T(8,128)S(1)} %get-tuple-element.56.refs_0_, f32[2,9,8,128]{3,2,1,0:T(8,128)S(1)} %get-tuple-element.55.refs_1_, f32[3,9,8,128]{3,2,1,0:T(8,128)S(1)} %collective-permute-done.3.refs_2_, f32[40,1024]{1,0:T(8,128)S(1)} %get-tuple-element.48.refs_3_, ...), custom_call_target="tpu_custom_call" | custom-call | flops 3200000000 | bytes 4000000 | tf_op jit(solution)/shard_map/rest_edges/pallas_call | solution.py:268
  32.7 3.8 %collective-permute-start.5 = (f32[40,1024]{1,0:T(8,128)S(1)}, f32[40,1024]{1,0:T(8,128)S(1)}, u32[]{:S(2)}, u32[]{:S(2)}) collective-permute-start(f32[40,1024]{1,0:T(8,128)S(1)} %get-tuple-element.50), channel_id=1, source_target_pairs={{1,2},{3,4},{5,6},{7,8},{9,10},{11,12},{13,14},{2,1},{4,3},{6,5},{... | collective-permute-start | bytes 491528 | tf_op jit(solution)/shard_map/ppermute | solution.py:335
  36.5 0.0 copy-start
  36.5 2.1 %collective-permute-start.6 = (f32[40,1024]{1,0:T(8,128)S(1)}, f32[40,1024]{1,0:T(8,128)S(1)}, u32[]{:S(2)}, u32[]{:S(2)}) collective-permute-start(f32[40,1024]{1,0:T(8,128)S(1)} %get-tuple-element.51), channel_id=1, source_target_pairs={{0,1},{2,3},{4,5},{6,7},{8,9},{10,11},{12,13},{14,15},{1,0},{3,2},... | collective-permute-start | bytes 491528 | tf_op jit(solution)/shard_map/ppermute | solution.py:335
  38.6 4.5 %rest_core.1 = f32[192,1024]{1,0:T(8,128)S(1)} custom-call(f32[2,9,8,128]{3,2,1,0:T(8,128)S(1)} %get-tuple-element.56.refs_0_, f32[2,9,8,128]{3,2,1,0:T(8,128)S(1)} %get-tuple-element.55.refs_1_, f32[3,9,8,128]{3,2,1,0:T(8,128)S(1)} %collective-permute-done.3.refs_2_, f32[192,1024]{1,0:T(8,128)S(1)} %get-tuple-element.47.refs_3_), custom_call_target="tpu_custom_call" | custom-call | flops 3200000000 | bytes 4000000 | tf_op jit(solution)/shard_map/rest_core/pallas_call | solution.py:268
  43.0 0.0 collective-permute-done.5.first
  43.1 1.6 %collective-permute-done.6.second = f32[40,1024]{1,0:T(8,128)S(1)} collective-permute-done((f32[40,1024]{1,0:T(8,128)S(1)}, f32[40,1024]{1,0:T(8,128)S(1)}, u32[]{:S(2)}, u32[]{:S(2)}) %collective-permute-start.6) | collective-permute-done | bytes 163872 | tf_op jit(solution)/shard_map/ppermute | solution.py:335
  44.6 0.0 copy-done
  44.6 1.1 %edges.1 = f32[8,24,1024]{2,1,0:T(8,128)} custom-call(f32[8,24,1024]{2,1,0:T(8,128)S(1)} %bitcast.2, f32[8,24,1024]{2,1,0:T(8,128)S(1)} %copy-done, f32[40,1024]{1,0:T(8,128)S(1)} %collective-permute-done.5.first, f32[40,1024]{1,0:T(8,128)S(1)} %collective-permute-done.6.second), custom_call_target="tpu_custom_call" | custom-call | tf_op jit(solution)/shard_map/edges/pallas_call | solution.py:396
  (9 shorter events, 0.1 us)
Async XLA Ops:
  1.5 11.4 %collective-permute-start = (f32[3,3,8,128]{3,2,1,0:T(8,128)}, f32[3,3,8,128]{3,2,1,0:T(8,128)S(1)}, u32[]{:S(2)}, u32[]{:S(2)}) collective-permute-start(f32[3,3,8,128]{3,2,1,0:T(8,128)} %get-tuple-element.32), channel_id=1, source_target_pairs={{0,1},{2,3},{4,5},{6,7},{8,9},{10,11},{12,13},{14,15},{1,0},{3,2},... | collective-permute-start | bytes 110600 | tf_op jit(solution)/shard_map/ppermute | solution.py:335
  4.7 8.2 %collective-permute-start.1 = (f32[3,3,8,128]{3,2,1,0:T(8,128)}, f32[3,3,8,128]{3,2,1,0:T(8,128)S(1)}, u32[]{:S(2)}, u32[]{:S(2)}) collective-permute-start(f32[3,3,8,128]{3,2,1,0:T(8,128)} %get-tuple-element.33), channel_id=1, source_target_pairs={{1,2},{3,4},{5,6},{7,8},{9,10},{11,12},{13,14},{2,1},{4,3},{6,5},{... | collective-permute-start | bytes 110600 | tf_op jit(solution)/shard_map/ppermute | solution.py:335
  8.8 0.8 %copy-start.1 = (f32[3,3,8,128]{3,2,1,0:T(8,128)S(1)}, f32[3,3,8,128]{3,2,1,0:T(8,128)}, u32[]{:S(2)}) copy-start(f32[3,3,8,128]{3,2,1,0:T(8,128)} %get-tuple-element.30.refs_0_) | copy-start | bytes 110596
  13.0 6.7 %collective-permute-start.2 = (f32[3,9,8,128]{3,2,1,0:T(8,128)S(1)}, f32[3,9,8,128]{3,2,1,0:T(8,128)S(1)}, u32[]{:S(2)}, u32[]{:S(2)}) collective-permute-start(f32[3,9,8,128]{3,2,1,0:T(8,128)S(1)} %constant_dynamic-update-slice_fusion), channel_id=1, source_target_pairs={{0,16},{16,0},{32,48},{48,32},{64,80},{80,64},{96,112},{112,96},{1... | collective-permute-start | bytes 331784 | tf_op jit(solution)/shard_map/ppermute | solution.py:364
  16.1 12.8 %collective-permute-start.4 = (f32[1,9,8,128]{3,2,1,0:T(8,128)S(1)}, f32[1,9,8,128]{3,2,1,0:T(8,128)S(1)}, u32[]{:S(2)}, u32[]{:S(2)}) collective-permute-start(f32[1,9,8,128]{3,2,1,0:T(8,128)S(1)} %get-tuple-element.62), channel_id=1, source_target_pairs={{16,48},{32,0},{48,80},{64,32},{80,112},{96,64},{112,144},{128,96}... | collective-permute-start | bytes 110600 | tf_op jit(solution)/shard_map/ppermute | solution.py:376
  19.8 9.1 %collective-permute-start.3 = (f32[3,9,8,128]{3,2,1,0:T(8,128)S(1)}, f32[3,9,8,128]{3,2,1,0:T(8,128)S(1)}, u32[]{:S(2)}, u32[]{:S(2)}) collective-permute-start(f32[3,9,8,128]{3,2,1,0:T(8,128)S(1)} %maximum_select_fusion), channel_id=1, source_target_pairs={{0,32},{32,64},{48,16},{64,96},{80,48},{96,128},{112,80},{128,160}... | collective-permute-start | bytes 331784 | tf_op jit(solution)/shard_map/ppermute | solution.py:375
  32.7 10.3 %collective-permute-start.5 = (f32[40,1024]{1,0:T(8,128)S(1)}, f32[40,1024]{1,0:T(8,128)S(1)}, u32[]{:S(2)}, u32[]{:S(2)}) collective-permute-start(f32[40,1024]{1,0:T(8,128)S(1)} %get-tuple-element.50), channel_id=1, source_target_pairs={{1,2},{3,4},{5,6},{7,8},{9,10},{11,12},{13,14},{2,1},{4,3},{6,5},{... | collective-permute-start | bytes 491528 | tf_op jit(solution)/shard_map/ppermute | solution.py:335
  36.5 8.1 %copy-start = (f32[8,24,1024]{2,1,0:T(8,128)S(1)}, f32[8,24,1024]{2,1,0:T(8,128)}, u32[]{:S(2)}) copy-start(f32[8,24,1024]{2,1,0:T(8,128)} %old.1) | copy-start | bytes 2359300
  36.5 8.1 %collective-permute-start.6 = (f32[40,1024]{1,0:T(8,128)S(1)}, f32[40,1024]{1,0:T(8,128)S(1)}, u32[]{:S(2)}, u32[]{:S(2)}) collective-permute-start(f32[40,1024]{1,0:T(8,128)S(1)} %get-tuple-element.51), channel_id=1, source_target_pairs={{0,1},{2,3},{4,5},{6,7},{8,9},{10,11},{12,13},{14,15},{1,0},{3,2},... | collective-permute-start | bytes 491528 | tf_op jit(solution)/shard_map/ppermute | solution.py:335
